TPU v7x, 128 devices: a whole 4x4x4 slice. The times are simulated.
128 devices in a mesh: gx: 4 (over x), gy: 8 (over y, core), gz: 4 (over z).
Axes of the slice: x: 4, y: 4, z: 4, core: 2. Of those that a mesh axis runs over, the one named last changes fastest.
Arguments:
- star_residual: bfloat16 [512, 64, 1152], P(('gx', 'gy', 'gz')), may hold values from -6 to 6
- patch_inverse: bfloat16 [512, 1152, 1152], P(('gx', 'gy', 'gz')), may hold values from -0.1875 to 0.1875
- block_owner: int32 [512, 9], P(('gx', 'gy', 'gz')), may hold values from 0 to 127, as said below
- block_slot: int32 [512, 9], P(('gx', 'gy', 'gz')), may hold values from 0 to 1, as said below
- recv_target: int32 [128, 27, 2], P(('gx', 'gy', 'gz')), may hold values from -1 to 7, as said below
Outputs:
- owned_sum: float32 [1024, 64, 128], P(('gx', 'gy', 'gz'))
- combined: float32 [512, 9, 64, 128], P(('gx', 'gy', 'gz'))
Inputs may be any that keep to these rules, and one draw needn't show every extreme that they name: `block_owner`: each block's owner is the block's own partition or one whose coordinate differs by at most one step along each of the three mesh axes, counted with wrap-around. `block_slot`: blocks of one partition that have the same owner have distinct slots; in every partition some owner receives exactly 2 of its blocks. `recv_target`: every slot that a block uses maps to an owned block of its owner; slots that no block uses hold -1.
All inputs are finite; a program needn't handle non-finite values.
Results may differ from a plain program's by a relative error of at most 0.0003.
Values sent between devices are 32-bit elements; how exact they have to be, the bound alone decides.
No kernel may reach another device: no remote copies, remote signals or barrier semaphores. Data moves between devices by JAX's collectives and lax.ppermute only.
A program may use at most 64 MiB of HBM per device.

v0:
```python
import jax
import jax.numpy as jnp
from jax import lax
from jax.sharding import PartitionSpec as P

OWNB = 8


def from_behind(array, axis, by):
    length = lax.axis_size(axis)
    return lax.ppermute(array, axis, [(i, (i + by) % length) for i in range(length)])


def axis_code(far_index, near_index, extent):
    distance = (far_index - near_index) % extent
    return jnp.where(distance == 0, 1, jnp.where(distance == 1, 2, 0)).astype(jnp.int32)


def offset_code(far_ids, near_ids, extents):
    size_x, size_y, size_z = extents
    code_x = axis_code(far_ids // (size_y * size_z), near_ids // (size_y * size_z), size_x)
    code_y = axis_code(far_ids // size_z % size_y, near_ids // size_z % size_y, size_y)
    code_z = axis_code(far_ids % size_z, near_ids % size_z, size_z)
    return 9 * code_x + 3 * code_y + code_z


def one_hot(indices, count):
    return (indices[:, None] == jnp.arange(count, dtype=jnp.int32)[None, :]).astype(jnp.float32)


def spread(placing, values):
    return jnp.einsum("nk,nf->kf", placing, values, precision=lax.Precision.HIGHEST)


def collect(placing, values):
    return jnp.einsum("nk,kf->nf", placing, values, precision=lax.Precision.HIGHEST)


def move_layers(buffer, dim, upper_move, lower_move):
    lower = lax.index_in_dim(buffer, 0, dim, keepdims=True)
    middle = lax.index_in_dim(buffer, 1, dim, keepdims=True)
    upper = lax.index_in_dim(buffer, 2, dim, keepdims=True)
    return jnp.concatenate([lower_move(lower), middle, upper_move(upper)], axis=dim)


def on_device(star_residual, patch_inverse, block_owner, block_slot, recv_target):
    extents = (lax.axis_size("gx"), lax.axis_size("gy"), lax.axis_size("gz"))
    my_index = lax.axis_index(("gx", "gy", "gz"))
    patch_count, rhs_count, patch_order = star_residual.shape
    block_count = block_owner.shape[1]
    block_width = patch_order // block_count
    capacity = recv_target.shape[2]
    feature = rhs_count * block_width
    inverse_blocks = patch_inverse.reshape(patch_count, block_count, block_width, patch_order)
    contribution = jnp.einsum(
        "prj,pbwj->pbrw", star_residual, inverse_blocks, preferred_element_type=jnp.float32
    )
    blocks = contribution.reshape(patch_count * block_count, feature)
    owner_ids = block_owner.reshape(-1)
    slot_ids = block_slot.reshape(-1)
    target_table = recv_target[0]
    send_code = offset_code(owner_ids, my_index, extents)
    placing = one_hot(send_code * capacity + slot_ids, 27 * capacity)
    outgoing = spread(placing, blocks).reshape(3, 3, 3, capacity, feature)
    arrived = move_layers(
        outgoing, 0, lambda v: from_behind(v, "gx", 1), lambda v: from_behind(v, "gx", -1)
    )
    arrived = move_layers(
        arrived, 1, lambda v: from_behind(v, "gy", 1), lambda v: from_behind(v, "gy", -1)
    )
    arrived = move_layers(
        arrived, 2, lambda v: from_behind(v, "gz", 1), lambda v: from_behind(v, "gz", -1)
    )
    arrived = arrived.reshape(27 * capacity, feature)
    picking = one_hot(target_table.reshape(-1), OWNB)
    owned_total = spread(picking, arrived)
    answer = collect(picking, owned_total).reshape(3, 3, 3, capacity, feature)
    returned = move_layers(
        answer, 0, lambda v: from_behind(v, "gx", -1), lambda v: from_behind(v, "gx", 1)
    )
    returned = move_layers(
        returned, 1, lambda v: from_behind(v, "gy", -1), lambda v: from_behind(v, "gy", 1)
    )
    returned = move_layers(
        returned, 2, lambda v: from_behind(v, "gz", -1), lambda v: from_behind(v, "gz", 1)
    )
    combined_blocks = collect(placing, returned.reshape(27 * capacity, feature))
    owned_sum = owned_total.reshape(OWNB, rhs_count, block_width)
    combined = combined_blocks.reshape(patch_count, block_count, rhs_count, block_width)
    return (owned_sum, combined)


def solution(mesh):
    placed = (
        P(("gx", "gy", "gz"), None, None),
        P(("gx", "gy", "gz"), None, None),
        P(("gx", "gy", "gz"), None),
        P(("gx", "gy", "gz"), None),
        P(("gx", "gy", "gz"), None, None),
    )
    return jax.shard_map(
        on_device,
        mesh=mesh,
        in_specs=placed,
        out_specs=(P(("gx", "gy", "gz"), None, None), P(("gx", "gy", "gz"), None, None, None)),
        check_vma=False,
    )
```

profile of v0, /device:TPU:1, one launch (start us, length us, event | category | flops | bytes accessed | tf_op | source)
XLA Modules:
  0.0 124.6 jit_solution(13433063272320304511)
XLA Ops:
  0.7 0.8 reshape.186
  2.3 6.0 %fusion.3 = f32[4,9,128,64]{2,3,1,0:T(8,128)S(1)} fusion(bf16[4,9,128,1152]{3,2,1,0:T(8,128)(2,1)} %bitcast.32, bf16[4,64,1152]{2,1,0:T(8,128)(2,1)S(1)} %copy-done), kind=kOutput, calls=%fused_computation.8 | convolution fusion | flops 679477248 | bytes 12386304 | tf_op jit(solution)/shard_map/prj,pbwj->pbrw/dot_general | solution.py:55
  9.3 1.0 fusion.9
  10.5 1.2 slice.73
  11.6 3.3 %collective-permute-start = (f32[1,3,3,2,8192]{4,3,2,1,0:T(2,128)}, f32[1,3,3,2,8192]{4,3,2,1,0:T(2,128)S(1)}, u32[]{:S(2)}, u32[]{:S(2)}) collective-permute-start(f32[1,3,3,2,8192]{4,3,2,1,0:T(2,128)} %slice.73), channel_id=1, source_target_pairs={{0,96},{32,0},{64,32},{96,64},{1,97},{33,1},{65,33},{97,65},{2,98}... | collective-permute-start | bytes 1769480 | tf_op jit(solution)/shard_map/ppermute | solution.py:11
  14.9 1.2 slice.77
  16.5 10.8 %collective-permute-done = f32[1,3,3,2,8192]{4,3,2,1,0:T(2,128)S(1)} collective-permute-done((f32[1,3,3,2,8192]{4,3,2,1,0:T(2,128)}, f32[1,3,3,2,8192]{4,3,2,1,0:T(2,128)S(1)}, u32[]{:S(2)}, u32[]{:S(2)}) %collective-permute-start) | collective-permute-done | bytes 589856 | tf_op jit(solution)/shard_map/ppermute | solution.py:11
  27.4 4.0 %collective-permute-done.1 = f32[1,3,3,2,8192]{4,3,2,1,0:T(2,128)S(1)} collective-permute-done((f32[1,3,3,2,8192]{4,3,2,1,0:T(2,128)}, f32[1,3,3,2,8192]{4,3,2,1,0:T(2,128)S(1)}, u32[]{:S(2)}, u32[]{:S(2)}) %collective-permute-start.1) | collective-permute-done | bytes 589856 | tf_op jit(solution)/shard_map/ppermute | solution.py:11
  31.6 1.9 %collective-permute-start.2 = (f32[3,1,3,2,8192]{4,3,2,1,0:T(2,128)S(1)}, f32[3,1,3,2,8192]{4,3,2,1,0:T(2,128)S(1)}, u32[]{:S(2)}, u32[]{:S(2)}) collective-permute-start(f32[3,1,3,2,8192]{4,3,2,1,0:T(2,128)S(1)} %get-tuple-element.21), channel_id=1, source_target_pairs={{0,28},{4,0},{8,4},{12,8},{16,12},{20,16},{24,20},{28,24},{1,29},{... | collective-permute-start | bytes 1769480 | tf_op jit(solution)/shard_map/ppermute | solution.py:11
  33.5 1.2 collective-permute-start.3
  34.7 7.8 %collective-permute-done.2 = f32[3,1,3,2,8192]{4,3,2,1,0:T(2,128)S(1)} collective-permute-done((f32[3,1,3,2,8192]{4,3,2,1,0:T(2,128)S(1)}, f32[3,1,3,2,8192]{4,3,2,1,0:T(2,128)S(1)}, u32[]{:S(2)}, u32[]{:S(2)}) %collective-permute-start.2) | collective-permute-done | bytes 589856 | tf_op jit(solution)/shard_map/ppermute | solution.py:11
  42.6 1.3 %pad_maximum_fusion = f32[3,3,3,2,8192]{4,3,2,1,0:T(2,128)S(1)} fusion(f32[3,1,3,2,8192]{4,3,2,1,0:T(2,128)S(1)} %collective-permute-done.3, f32[3,1,3,2,8192]{4,3,2,1,0:T(2,128)S(1)} %get-tuple-element.23, f32[3,1,3,2,8192]{4,3,2,1,0:T(2,128)S(1)} %collective-permute-done.2), kind=kLoop, calls=%fused_computation.4 | loop fusion | flops 884736 | bytes 3538944 | tf_op jit(solution)/shard_map/concatenate | solution.py:43
  44.0 3.8 %collective-permute-start.4 = (f32[3,3,1,2,8192]{4,3,2,1,0:T(2,128)S(1)}, f32[3,3,1,2,8192]{4,3,2,1,0:T(2,128)S(1)}, u32[]{:S(2)}, u32[]{:S(2)}) collective-permute-start(f32[3,3,1,2,8192]{4,3,2,1,0:T(2,128)S(1)} %get-tuple-element.18), channel_id=1, source_target_pairs={{0,3},{1,0},{2,1},{3,2},{4,7},{5,4},{6,5},{7,6},{8,11},{9,8},{10,9... | collective-permute-start | bytes 1769480 | tf_op jit(solution)/shard_map/ppermute | solution.py:11
  49.2 8.5 %collective-permute-done.4 = f32[3,3,1,2,8192]{4,3,2,1,0:T(2,128)S(1)} collective-permute-done((f32[3,3,1,2,8192]{4,3,2,1,0:T(2,128)S(1)}, f32[3,3,1,2,8192]{4,3,2,1,0:T(2,128)S(1)}, u32[]{:S(2)}, u32[]{:S(2)}) %collective-permute-start.4) | collective-permute-done | bytes 589856 | tf_op jit(solution)/shard_map/ppermute | solution.py:11
  57.7 3.1 %collective-permute-done.5 = f32[3,3,1,2,8192]{4,3,2,1,0:T(2,128)S(1)} collective-permute-done((f32[3,3,1,2,8192]{4,3,2,1,0:T(2,128)S(1)}, f32[3,3,1,2,8192]{4,3,2,1,0:T(2,128)S(1)}, u32[]{:S(2)}, u32[]{:S(2)}) %collective-permute-start.5) | collective-permute-done | bytes 589856 | tf_op jit(solution)/shard_map/ppermute | solution.py:11
  60.9 2.2 %pad_maximum_fusion.1 = f32[3,3,3,2,8192]{4,3,2,1,0:T(2,128)} fusion(f32[3,3,1,2,8192]{4,3,2,1,0:T(2,128)S(1)} %collective-permute-done.5, f32[3,3,1,2,8192]{4,3,2,1,0:T(2,128)S(1)} %get-tuple-element.20, f32[3,3,1,2,8192]{4,3,2,1,0:T(2,128)S(1)} %collective-permute-done.4), kind=kLoop, calls=%fused_computation.5 | loop fusion | flops 884736 | bytes 3538944 | tf_op jit(solution)/shard_map/concatenate | solution.py:43
  63.0 2.5 %reshape.190 = f32[54,8192]{1,0:T(8,128)S(1)} reshape(f32[3,3,3,2,8192]{4,3,2,1,0:T(2,128)} %pad_maximum_fusion.1) | data formatting | bytes 3538944 | tf_op jit(solution)/shard_map/reshape | solution.py:74
  66.3 0.9 fusion.7
  67.4 1.2 slice.85
  68.6 1.2 slice.89
  70.1 2.7 %collective-permute-start.7 = (f32[1,3,3,2,8192]{4,3,2,1,0:T(2,128)}, f32[1,3,3,2,8192]{4,3,2,1,0:T(2,128)S(1)}, u32[]{:S(2)}, u32[]{:S(2)}) collective-permute-start(f32[1,3,3,2,8192]{4,3,2,1,0:T(2,128)} %slice.89), channel_id=1, source_target_pairs={{0,96},{32,0},{64,32},{96,64},{1,97},{33,1},{65,33},{97,65},{2,98}... | collective-permute-start | bytes 1769480 | tf_op jit(solution)/shard_map/ppermute | solution.py:11
  72.9 8.0 %collective-permute-done.6 = f32[1,3,3,2,8192]{4,3,2,1,0:T(2,128)S(1)} collective-permute-done((f32[1,3,3,2,8192]{4,3,2,1,0:T(2,128)}, f32[1,3,3,2,8192]{4,3,2,1,0:T(2,128)S(1)}, u32[]{:S(2)}, u32[]{:S(2)}) %collective-permute-start.6) | collective-permute-done | bytes 589856 | tf_op jit(solution)/shard_map/ppermute | solution.py:11
  81.8 8.6 %collective-permute-start.8 = (f32[3,1,3,2,8192]{4,3,2,1,0:T(2,128)S(1)}, f32[3,1,3,2,8192]{4,3,2,1,0:T(2,128)S(1)}, u32[]{:S(2)}, u32[]{:S(2)}) collective-permute-start(f32[3,1,3,2,8192]{4,3,2,1,0:T(2,128)S(1)} %get-tuple-element.15), channel_id=1, source_target_pairs={{0,4},{4,8},{8,12},{12,16},{16,20},{20,24},{24,28},{28,0},{1,5},{5... | collective-permute-start | bytes 1769480 | tf_op jit(solution)/shard_map/ppermute | solution.py:11
  90.5 6.8 %collective-permute-done.8 = f32[3,1,3,2,8192]{4,3,2,1,0:T(2,128)S(1)} collective-permute-done((f32[3,1,3,2,8192]{4,3,2,1,0:T(2,128)S(1)}, f32[3,1,3,2,8192]{4,3,2,1,0:T(2,128)S(1)}, u32[]{:S(2)}, u32[]{:S(2)}) %collective-permute-start.8) | collective-permute-done | bytes 589856 | tf_op jit(solution)/shard_map/ppermute | solution.py:11
  97.3 2.5 %collective-permute-done.9 = f32[3,1,3,2,8192]{4,3,2,1,0:T(2,128)S(1)} collective-permute-done((f32[3,1,3,2,8192]{4,3,2,1,0:T(2,128)S(1)}, f32[3,1,3,2,8192]{4,3,2,1,0:T(2,128)S(1)}, u32[]{:S(2)}, u32[]{:S(2)}) %collective-permute-start.9) | collective-permute-done | bytes 589856 | tf_op jit(solution)/shard_map/ppermute | solution.py:11
  99.8 1.3 %pad_maximum_fusion.2 = f32[3,3,3,2,8192]{4,3,2,1,0:T(2,128)S(1)} fusion(f32[3,1,3,2,8192]{4,3,2,1,0:T(2,128)S(1)} %collective-permute-done.9, f32[3,1,3,2,8192]{4,3,2,1,0:T(2,128)S(1)} %get-tuple-element.17, f32[3,1,3,2,8192]{4,3,2,1,0:T(2,128)S(1)} %collective-permute-done.8), kind=kLoop, calls=%fused_computation.6 | loop fusion | flops 884736 | bytes 3538944 | tf_op jit(solution)/shard_map/concatenate | solution.py:43
  101.3 2.7 %collective-permute-start.11 = (f32[3,3,1,2,8192]{4,3,2,1,0:T(2,128)S(1)}, f32[3,3,1,2,8192]{4,3,2,1,0:T(2,128)S(1)}, u32[]{:S(2)}, u32[]{:S(2)}) collective-permute-start(f32[3,3,1,2,8192]{4,3,2,1,0:T(2,128)S(1)} %get-tuple-element.13), channel_id=1, source_target_pairs={{0,3},{1,0},{2,1},{3,2},{4,7},{5,4},{6,5},{7,6},{8,11},{9,8},{10,9... | collective-permute-start | bytes 1769480 | tf_op jit(solution)/shard_map/ppermute | solution.py:11
  104.7 11.0 %collective-permute-done.10 = f32[3,3,1,2,8192]{4,3,2,1,0:T(2,128)S(1)} collective-permute-done((f32[3,3,1,2,8192]{4,3,2,1,0:T(2,128)S(1)}, f32[3,3,1,2,8192]{4,3,2,1,0:T(2,128)S(1)}, u32[]{:S(2)}, u32[]{:S(2)}) %collective-permute-start.10) | collective-permute-done | bytes 589856 | tf_op jit(solution)/shard_map/ppermute | solution.py:11
  115.7 2.2 %pad_maximum_fusion.3 = f32[3,3,3,2,8192]{4,3,2,1,0:T(2,128)} fusion(f32[3,3,1,2,8192]{4,3,2,1,0:T(2,128)S(1)} %collective-permute-done.11, f32[3,3,1,2,8192]{4,3,2,1,0:T(2,128)S(1)} %get-tuple-element.14, f32[3,3,1,2,8192]{4,3,2,1,0:T(2,128)S(1)} %collective-permute-done.10), kind=kLoop, calls=%fused_computation.7 | loop fusion | flops 884736 | bytes 3538944 | tf_op jit(solution)/shard_map/concatenate | solution.py:43
  117.9 2.5 %reshape.192 = f32[54,8192]{1,0:T(8,128)S(1)} reshape(f32[3,3,3,2,8192]{4,3,2,1,0:T(2,128)} %pad_maximum_fusion.3) | data formatting | bytes 3538944 | tf_op jit(solution)/shard_map/reshape | solution.py:87
  121.0 2.2 %fusion = f32[4,9,64,128]{3,1,2,0:T(8,128)S(1)} fusion(f32[64,128,54]{1,0,2:T(8,128)S(1)} %slice_bitcast_fusion, s32[4,9]{1,0:T(4,128)S(1)} %multiply_add_fusion), kind=kOutput, calls=%fused_computation | convolution fusion | flops 191104928 | bytes 2949264 | tf_op jit(solution)/shard_map/nk,kf->nf/dot_general | solution.py:36
  123.2 1.4 %copy.13 = f32[4,9,64,128]{3,2,1,0:T(8,128)} copy(f32[4,9,64,128]{3,1,2,0:T(8,128)S(1)} %fusion) | data formatting | bytes 2359296
  (41 shorter events, 7.8 us)
Async XLA Ops:
  0.6 1.6 %copy-start = (bf16[4,64,1152]{2,1,0:T(8,128)(2,1)S(1)}, bf16[4,64,1152]{2,1,0:T(8,128)(2,1)}, u32[]{:S(2)}) copy-start(bf16[4,64,1152]{2,1,0:T(8,128)(2,1)} %param.5) | copy-start | bytes 1769476
  11.6 15.6 %collective-permute-start = (f32[1,3,3,2,8192]{4,3,2,1,0:T(2,128)}, f32[1,3,3,2,8192]{4,3,2,1,0:T(2,128)S(1)}, u32[]{:S(2)}, u32[]{:S(2)}) collective-permute-start(f32[1,3,3,2,8192]{4,3,2,1,0:T(2,128)} %slice.73), channel_id=1, source_target_pairs={{0,96},{32,0},{64,32},{96,64},{1,97},{33,1},{65,33},{97,65},{2,98}... | collective-permute-start | bytes 1769480 | tf_op jit(solution)/shard_map/ppermute | solution.py:11
  16.1 15.3 %collective-permute-start.1 = (f32[1,3,3,2,8192]{4,3,2,1,0:T(2,128)}, f32[1,3,3,2,8192]{4,3,2,1,0:T(2,128)S(1)}, u32[]{:S(2)}, u32[]{:S(2)}) collective-permute-start(f32[1,3,3,2,8192]{4,3,2,1,0:T(2,128)} %slice.77), channel_id=1, source_target_pairs={{0,32},{32,64},{64,96},{96,0},{1,33},{33,65},{65,97},{97,1},{2,34}... | collective-permute-start | bytes 1769480 | tf_op jit(solution)/shard_map/ppermute | solution.py:11
  31.6 10.9 %collective-permute-start.2 = (f32[3,1,3,2,8192]{4,3,2,1,0:T(2,128)S(1)}, f32[3,1,3,2,8192]{4,3,2,1,0:T(2,128)S(1)}, u32[]{:S(2)}, u32[]{:S(2)}) collective-permute-start(f32[3,1,3,2,8192]{4,3,2,1,0:T(2,128)S(1)} %get-tuple-element.21), channel_id=1, source_target_pairs={{0,28},{4,0},{8,4},{12,8},{16,12},{20,16},{24,20},{28,24},{1,29},{... | collective-permute-start | bytes 1769480 | tf_op jit(solution)/shard_map/ppermute | solution.py:11
  33.5 9.0 %collective-permute-start.3 = (f32[3,1,3,2,8192]{4,3,2,1,0:T(2,128)S(1)}, f32[3,1,3,2,8192]{4,3,2,1,0:T(2,128)S(1)}, u32[]{:S(2)}, u32[]{:S(2)}) collective-permute-start(f32[3,1,3,2,8192]{4,3,2,1,0:T(2,128)S(1)} %get-tuple-element.22), channel_id=1, source_target_pairs={{0,4},{4,8},{8,12},{12,16},{16,20},{20,24},{24,28},{28,0},{1,5},{5... | collective-permute-start | bytes 1769480 | tf_op jit(solution)/shard_map/ppermute | solution.py:11
  44.0 13.7 %collective-permute-start.4 = (f32[3,3,1,2,8192]{4,3,2,1,0:T(2,128)S(1)}, f32[3,3,1,2,8192]{4,3,2,1,0:T(2,128)S(1)}, u32[]{:S(2)}, u32[]{:S(2)}) collective-permute-start(f32[3,3,1,2,8192]{4,3,2,1,0:T(2,128)S(1)} %get-tuple-element.18), channel_id=1, source_target_pairs={{0,3},{1,0},{2,1},{3,2},{4,7},{5,4},{6,5},{7,6},{8,11},{9,8},{10,9... | collective-permute-start | bytes 1769480 | tf_op jit(solution)/shard_map/ppermute | solution.py:11
  47.8 13.0 %collective-permute-start.5 = (f32[3,3,1,2,8192]{4,3,2,1,0:T(2,128)S(1)}, f32[3,3,1,2,8192]{4,3,2,1,0:T(2,128)S(1)}, u32[]{:S(2)}, u32[]{:S(2)}) collective-permute-start(f32[3,3,1,2,8192]{4,3,2,1,0:T(2,128)S(1)} %get-tuple-element.19), channel_id=1, source_target_pairs={{0,1},{1,2},{2,3},{3,0},{4,5},{5,6},{6,7},{7,4},{8,9},{9,10},{10,1... | collective-permute-start | bytes 1769480 | tf_op jit(solution)/shard_map/ppermute | solution.py:11
  63.0 2.5 %copy-start.3 = (s32[54]{0:T(128)S(1)}, s32[54]{0:T(128)}, u32[]{:S(2)}) copy-start(s32[54]{0:T(128)} %eq.119) | copy-start | bytes 652
  68.6 12.3 %collective-permute-start.6 = (f32[1,3,3,2,8192]{4,3,2,1,0:T(2,128)}, f32[1,3,3,2,8192]{4,3,2,1,0:T(2,128)S(1)}, u32[]{:S(2)}, u32[]{:S(2)}) collective-permute-start(f32[1,3,3,2,8192]{4,3,2,1,0:T(2,128)} %slice.85), channel_id=1, source_target_pairs={{0,32},{32,64},{64,96},{96,0},{1,33},{33,65},{65,97},{97,1},{2,34}... | collective-permute-start | bytes 1769480 | tf_op jit(solution)/shard_map/ppermute | solution.py:11
  70.1 11.5 %collective-permute-start.7 = (f32[1,3,3,2,8192]{4,3,2,1,0:T(2,128)}, f32[1,3,3,2,8192]{4,3,2,1,0:T(2,128)S(1)}, u32[]{:S(2)}, u32[]{:S(2)}) collective-permute-start(f32[1,3,3,2,8192]{4,3,2,1,0:T(2,128)} %slice.89), channel_id=1, source_target_pairs={{0,96},{32,0},{64,32},{96,64},{1,97},{33,1},{65,33},{97,65},{2,98}... | collective-permute-start | bytes 1769480 | tf_op jit(solution)/shard_map/ppermute | solution.py:11
  81.8 15.5 %collective-permute-start.8 = (f32[3,1,3,2,8192]{4,3,2,1,0:T(2,128)S(1)}, f32[3,1,3,2,8192]{4,3,2,1,0:T(2,128)S(1)}, u32[]{:S(2)}, u32[]{:S(2)}) collective-permute-start(f32[3,1,3,2,8192]{4,3,2,1,0:T(2,128)S(1)} %get-tuple-element.15), channel_id=1, source_target_pairs={{0,4},{4,8},{8,12},{12,16},{16,20},{20,24},{24,28},{28,0},{1,5},{5... | collective-permute-start | bytes 1769480 | tf_op jit(solution)/shard_map/ppermute | solution.py:11
  90.5 9.3 %collective-permute-start.9 = (f32[3,1,3,2,8192]{4,3,2,1,0:T(2,128)S(1)}, f32[3,1,3,2,8192]{4,3,2,1,0:T(2,128)S(1)}, u32[]{:S(2)}, u32[]{:S(2)}) collective-permute-start(f32[3,1,3,2,8192]{4,3,2,1,0:T(2,128)S(1)} %get-tuple-element.16), channel_id=1, source_target_pairs={{0,28},{4,0},{8,4},{12,8},{16,12},{20,16},{24,20},{28,24},{1,29},{... | collective-permute-start | bytes 1769480 | tf_op jit(solution)/shard_map/ppermute | solution.py:11
  101.0 2.9 %copy-start.1 = (s32[4,9]{1,0:T(4,128)S(1)}, s32[4,9]{1,0:T(4,128)}, u32[]{:S(2)}) copy-start(s32[4,9]{1,0:T(4,128)} %param.8) | copy-start | bytes 436
  101.0 2.9 %copy-start.2 = (s32[4,9]{1,0:T(4,128)S(1)}, s32[4,9]{1,0:T(4,128)}, u32[]{:S(2)}) copy-start(s32[4,9]{1,0:T(4,128)} %param.7) | copy-start | bytes 436
  101.2 14.5 %collective-permute-start.10 = (f32[3,3,1,2,8192]{4,3,2,1,0:T(2,128)S(1)}, f32[3,3,1,2,8192]{4,3,2,1,0:T(2,128)S(1)}, u32[]{:S(2)}, u32[]{:S(2)}) collective-permute-start(f32[3,3,1,2,8192]{4,3,2,1,0:T(2,128)S(1)} %get-tuple-element.12), channel_id=1, source_target_pairs={{0,1},{1,2},{2,3},{3,0},{4,5},{5,6},{6,7},{7,4},{8,9},{9,10},{10,1... | collective-permute-start | bytes 1769480 | tf_op jit(solution)/shard_map/ppermute | solution.py:11
  101.3 14.5 %collective-permute-start.11 = (f32[3,3,1,2,8192]{4,3,2,1,0:T(2,128)S(1)}, f32[3,3,1,2,8192]{4,3,2,1,0:T(2,128)S(1)}, u32[]{:S(2)}, u32[]{:S(2)}) collective-permute-start(f32[3,3,1,2,8192]{4,3,2,1,0:T(2,128)S(1)} %get-tuple-element.13), channel_id=1, source_target_pairs={{0,3},{1,0},{2,1},{3,2},{4,7},{5,4},{6,5},{7,6},{8,11},{9,8},{10,9... | collective-permute-start | bytes 1769480 | tf_op jit(solution)/shard_map/ppermute | solution.py:11
where the time goes:
time: 126 us; the launch traced here: 125 us
  waiting for transfers between devices  63.2 us (50%)
  starting transfers between devices  24.3 us (19%)
  local copies, waits for them, and re-layouts  18.3 us (15%)
  matrix products  10.9 us (9%)
  other arithmetic  6.95 us (6%)
    ppermute x12, waiting for transfers between devices, from_behind(): lax.ppermute(array, axis, [(i, (i + by) % length) for i in range(length)])  63.2 us
    ppermute x12, starting transfers between devices, from_behind(): lax.ppermute(array, axis, [(i, (i + by) % length) for i in range(length)])  24.3 us
    concatenate x4, other arithmetic, move_layers(): jnp.concatenate([lower_move(lower), middle, upper_move(upper)], axis=dim)  6.89 us
    dot_general x1, matrix products, on_device(): jnp.einsum('prj,pbwj->pbrw', star_residual, inverse_blocks, preferred_ele...  5.98 us
    unnamed x18, local copies, waits for them, and re-layouts  4.42 us
    dot_general x2, matrix products, collect(): jnp.einsum('nk,kf->nf', placing, values, precision=lax.Precision.HIGHEST)  3.15 us
    slice x6, local copies, waits for them, and re-layouts, move_layers(): lower = lax.index_in_dim(buffer, 0, dim, keepdims=True)  2.91 us
    slice x4, local copies, waits for them, and re-layouts, move_layers(): upper = lax.index_in_dim(buffer, 2, dim, keepdims=True)  2.67 us
  transfers between devices with their start and end apart: 12, of which 10 were waited for; matrix products, arithmetic and copies ran while one was open for 4% of the time, Pallas kernels for 0%

commit v1 on v0

v1 whole, which is shorter than its diff:
```python
import functools

import jax
import jax.numpy as jnp
from jax import lax
from jax.experimental import pallas as pl
from jax.experimental.pallas import tpu as pltpu
from jax.sharding import PartitionSpec as P

OWNB = 8
AXES = ("gx", "gy", "gz")
PLANE = [(dy, dz) for dy in (-1, 0, 1) for dz in (-1, 0, 1)]
HOME = PLANE.index((0, 0))
ABROAD = [i for i in range(len(PLANE)) if i != HOME]
VMEM = pltpu.VMEM
SMEM = pltpu.SMEM


def axis_code(far, near, extent):
    ahead = jnp.where(near == extent - 1, 0, near + 1)
    return jnp.where(far == near, 1, jnp.where(far == ahead, 2, 0))


def slot_index(owner, slot, extents, capacity):
    size_x, size_y, size_z = extents
    near = [lax.axis_index(a) for a in AXES]
    far_x = lax.div(owner, size_y * size_z)
    far_y = lax.rem(lax.div(owner, size_z), size_y)
    far_z = lax.rem(owner, size_z)
    code_x = axis_code(far_x, near[0], size_x)
    code_y = axis_code(far_y, near[1], size_y)
    code_z = axis_code(far_z, near[2], size_z)
    return ((code_y * 3 + code_z) * 3 + code_x) * capacity + slot


def contribute_kernel(extents, capacity, owner_ref, slot_ref, residual_ref, inverse_ref, *rest):
    outs, placed = rest[:-1], rest[-1]
    patch = pl.program_id(0)
    blocks = owner_ref.shape[1]
    width = inverse_ref.shape[1] // blocks
    product = lax.dot_general(
        residual_ref[0],
        inverse_ref[0],
        (((1,), (1,)), ((), ())),
        preferred_element_type=jnp.float32,
    )
    for b in range(blocks):
        at = slot_index(owner_ref[patch, b], slot_ref[patch, b], extents, capacity)
        placed[at] = product[:, b * width : (b + 1) * width]

    @pl.when(patch == pl.num_programs(0) - 1)
    def _():
        per = 3 * capacity
        for i, out in enumerate(outs):
            out[...] = placed[i * per : (i + 1) * per]


def contribute(owner, slot, residual, inverse, extents, capacity):
    patches, rhs, order = residual.shape
    width = order // owner.shape[1]
    per = 3 * capacity
    whole = pl.BlockSpec((per, rhs, width), lambda p: (0, 0, 0))
    return pl.pallas_call(
        functools.partial(contribute_kernel, extents, capacity),
        grid=(patches,),
        in_specs=[
            pl.BlockSpec(memory_space=SMEM),
            pl.BlockSpec(memory_space=SMEM),
            pl.BlockSpec((1, rhs, order), lambda p: (p, 0, 0)),
            pl.BlockSpec((1, order, order), lambda p: (p, 0, 0)),
        ],
        out_specs=[whole] * 9,
        out_shape=[jax.ShapeDtypeStruct((per, rhs, width), jnp.float32)] * 9,
        scratch_shapes=[VMEM((9 * per, rhs, width), jnp.float32)],
        compiler_params=pltpu.CompilerParams(vmem_limit_bytes=32 * 2**20),
    )(owner, slot, residual, inverse)


def table_entry(tables, cx, plane, c):
    dy, dz = PLANE[plane]
    return tables[cx][c, 9 * cx + 3 * (dy + 1) + (dz + 1)]


def gather_kernel(capacity, *refs):
    tables, arrived = refs[0:3], refs[3:12]
    outs, total = refs[12:15], refs[15]
    total[...] = jnp.zeros_like(total)
    for i in range(9):
        for cx in range(3):
            for c in range(capacity):
                t = table_entry(tables, cx, i, c)
                t = jnp.where(t < 0, OWNB, t)
                total[cx, t] += arrived[i][cx * capacity + c]
    for cx in range(3):
        outs[cx][...] = total[cx, :OWNB]


def gather(tables, arrived, capacity):
    _, rhs, width = arrived[0].shape
    return pl.pallas_call(
        functools.partial(gather_kernel, capacity),
        in_specs=[pl.BlockSpec(memory_space=SMEM)] * 3 + [pl.BlockSpec(memory_space=VMEM)] * 9,
        out_specs=[pl.BlockSpec(memory_space=VMEM)] * 3,
        out_shape=[jax.ShapeDtypeStruct((OWNB, rhs, width), jnp.float32)] * 3,
        scratch_shapes=[VMEM((3, OWNB + 1, rhs, width), jnp.float32)],
        compiler_params=pltpu.CompilerParams(vmem_limit_bytes=32 * 2**20),
    )(*tables, *arrived)


def answer_kernel(capacity, *refs):
    tables, totals, outs = refs[0:3], refs[3:6], refs[6:15]
    for i in range(9):
        for cx in range(3):
            for c in range(capacity):
                t = table_entry(tables, cx, i, c)
                outs[i][cx * capacity + c] = totals[cx][jnp.maximum(t, 0)]


def answer(tables, totals, capacity):
    _, rhs, width = totals[0].shape
    per = 3 * capacity
    return pl.pallas_call(
        functools.partial(answer_kernel, capacity),
        in_specs=[pl.BlockSpec(memory_space=SMEM)] * 3 + [pl.BlockSpec(memory_space=VMEM)] * 3,
        out_specs=[pl.BlockSpec(memory_space=VMEM)] * 9,
        out_shape=[jax.ShapeDtypeStruct((per, rhs, width), jnp.float32)] * 9,
        compiler_params=pltpu.CompilerParams(vmem_limit_bytes=32 * 2**20),
    )(*tables, *totals)


def collect_kernel(extents, capacity, owner_ref, slot_ref, *refs):
    returned, out, wide, back = refs[0:9], refs[9], refs[10], refs[11]
    patches, blocks = owner_ref.shape
    per = 3 * capacity
    for k in range(9 * per):
        back[k] = patches * blocks
    for p in range(patches):
        for b in range(blocks):
            at = slot_index(owner_ref[p, b], slot_ref[p, b], extents, capacity)
            back[at] = p * blocks + b
    for i in range(9):
        for k in range(per):
            wide[back[i * per + k]] = returned[i][k]
    for p in range(patches):
        out[p] = wide[p * blocks : (p + 1) * blocks]


def collect(owner, slot, returned, extents, capacity):
    patches, blocks = owner.shape
    _, rhs, width = returned[0].shape
    return pl.pallas_call(
        functools.partial(collect_kernel, extents, capacity),
        in_specs=[pl.BlockSpec(memory_space=SMEM)] * 2 + [pl.BlockSpec(memory_space=VMEM)] * 9,
        out_specs=pl.BlockSpec(memory_space=VMEM),
        out_shape=jax.ShapeDtypeStruct((patches, blocks, rhs, width), jnp.float32),
        scratch_shapes=[
            VMEM((patches * blocks + 1, rhs, width), jnp.float32),
            SMEM((27 * capacity,), jnp.int32),
        ],
        compiler_params=pltpu.CompilerParams(vmem_limit_bytes=32 * 2**20),
    )(owner, slot, *returned)


def shift(array, extents, by):
    size_x, size_y, size_z = extents
    pairs = []
    for x in range(size_x):
        for y in range(size_y):
            for z in range(size_z):
                to = ((x + by[0]) % size_x * size_y + (y + by[1]) % size_y) * size_z + (z + by[2]) % size_z
                pairs.append(((x * size_y + y) * size_z + z, to))
    return lax.ppermute(array, AXES, pairs)


def on_device(star_residual, patch_inverse, block_owner, block_slot, recv_target):
    extents = tuple(lax.axis_size(a) for a in AXES)
    capacity = recv_target.shape[2]
    table = jnp.swapaxes(recv_target, 1, 2)[0]
    tables = [shift(table, extents, (1, 0, 0)), table, shift(table, extents, (-1, 0, 0))]

    outgoing = contribute(block_owner, block_slot, star_residual, patch_inverse, extents, capacity)
    arrived = [
        outgoing[i] if i == HOME else shift(outgoing[i], extents, (0,) + PLANE[i]) for i in range(9)
    ]
    below, own, above = gather(tables, arrived, capacity)
    owned = own + shift(above, extents, (1, 0, 0)) + shift(below, extents, (-1, 0, 0))
    totals = [shift(owned, extents, (1, 0, 0)), owned, shift(owned, extents, (-1, 0, 0))]
    answers = answer(tables, totals, capacity)
    returned = [
        answers[i]
        if i == HOME
        else shift(answers[i], extents, (0, -PLANE[i][0], -PLANE[i][1]))
        for i in range(9)
    ]
    combined = collect(block_owner, block_slot, returned, extents, capacity)
    return owned, combined


def solution(mesh):
    return jax.shard_map(
        on_device,
        mesh=mesh,
        in_specs=(
            P(AXES, None, None),
            P(AXES, None, None),
            P(AXES, None),
            P(AXES, None),
            P(AXES, None, None),
        ),
        out_specs=(P(AXES, None, None), P(AXES, None, None, None)),
        check_vma=False,
    )
```

time: 126 us -> 83 us (0.66)
  waiting for transfers between devices: 63.2 us -> 21.1 us
  starting transfers between devices: 24.3 us -> 46 us
  local copies, waits for them, and re-layouts: 18.3 us -> 6.45 us
  matrix products: 10.9 us -> 0 us
  Pallas kernels: 0 us -> 8.4 us
  other arithmetic: 6.95 us -> 0.05 us
    ppermute x12 -> x22, waiting for transfers between devices: 63.2 us -> 21.1 us  [shift(): return lax.ppermute(array, AXES, pairs)]
    ppermute x12 -> x22, starting transfers between devices: 24.3 us -> 46 us  [shift(): return lax.ppermute(array, AXES, pairs)]
    dot_general x5 -> x0, matrix products: 10.9 us -> none  [the longest x1 5.98 us: on_device(): jnp.einsum('prj,pbwj->pbrw', star_residual, inverse_blocks, preferred_ele...]
    pallas_call x0 -> x4, Pallas kernels: none -> 8.4 us  [the longest x1 4.46 us: contribute(): pl.pallas_call(functools.partial(contribute_kernel, extents, capacity), g...]
    concatenate x4 -> x0, other arithmetic: 6.89 us -> none  [move_layers(): jnp.concatenate([lower_move(lower), middle, upper_move(upper)], axis=dim)]
    reshape x4 -> x0, local copies, waits for them, and re-layouts: 6.62 us -> none  [the longest x1 2.53 us: on_device(): arrived = arrived.reshape(27 * capacity, feature)]
    slice x12 -> x0, local copies, waits for them, and re-layouts: 6.28 us -> none  [the longest x6 2.91 us: move_layers(): lower = lax.index_in_dim(buffer, 0, dim, keepdims=True)]
    unnamed x18 -> x16, local copies, waits for them, and re-layouts: 4.42 us -> 6.45 us
  transfers between devices with their start and end apart: 12 -> 22, of which waited for: 10 -> 9; matrix products, arithmetic and copies ran while one was open for 4% -> 0% of each run, Pallas kernels for 0% -> 0%
where the time goes in v1:
time: 83 us; the launch traced here: 82.8 us
  starting transfers between devices  46 us (55%)
  waiting for transfers between devices  21.1 us (25%)
  Pallas kernels  8.4 us (10%)
  local copies, waits for them, and re-layouts  6.45 us (8%)
    ppermute x22, starting transfers between devices, shift(): return lax.ppermute(array, AXES, pairs)  46 us
    ppermute x22, waiting for transfers between devices, shift(): return lax.ppermute(array, AXES, pairs)  21.1 us
    unnamed x16, local copies, waits for them, and re-layouts  6.45 us
    pallas_call x1, Pallas kernels, contribute(): pl.pallas_call(functools.partial(contribute_kernel, extents, capacity), g...  4.46 us
    pallas_call x1, Pallas kernels, collect(): pl.pallas_call(functools.partial(collect_kernel, extents, capacity), in_s...  2.25 us
  transfers between devices with their start and end apart: 22, of which 9 were waited for; matrix products, arithmetic and copies ran while one was open for 0% of the time, Pallas kernels for 0%

profile of v1, /device:TPU:1, one launch (start us, length us, event | category | flops | bytes accessed | tf_op | source)
XLA Modules:
  0.0 82.8 jit_solution(5797687496680809527)
XLA Ops:
  0.6 4.0 %copy-done = bf16[4,1152,1152]{2,1,0:T(8,128)(2,1)S(1)} copy-done((bf16[4,1152,1152]{2,1,0:T(8,128)(2,1)S(1)}, bf16[4,1152,1152]{2,1,0:T(8,128)(2,1)}, u32[]{:S(2)}) %copy-start) | copy-done | bytes 10616856
  4.7 1.1 %copy-done.2 = bf16[4,64,1152]{2,1,0:T(8,128)(2,1)S(1)} copy-done((bf16[4,64,1152]{2,1,0:T(8,128)(2,1)S(1)}, bf16[4,64,1152]{2,1,0:T(8,128)(2,1)}, u32[]{:S(2)}) %copy-start.2) | copy-done | bytes 589848
  5.7 0.7 copy-done.3
  6.4 0.7 copy-done.5
  7.1 4.5 %shard_map.68 = (f32[6,64,128]{2,1,0:T(8,128)S(1)}, f32[6,64,128]{2,1,0:T(8,128)S(1)}, f32[6,64,128]{2,1,0:T(8,128)S(1)}, f32[6,64,128]{2,1,0:T(8,128)S(1)}, f32...) custom-call(s32[4,9]{1,0:T(4,128)S(1)} %copy-done.3, ...), custom_call_target="tpu_custom_call" | custom-call | tf_op jit(solution)/shard_map/pallas_call | solution.py:63
  11.6 5.2 %collective-permute-start.2 = (f32[6,64,128]{2,1,0:T(8,128)S(1)}, f32[6,64,128]{2,1,0:T(8,128)S(1)}, u32[]{:S(2)}, u32[]{:S(2)}) collective-permute-start(f32[6,64,128]{2,1,0:T(8,128)S(1)} %get-tuple-element.23), channel_id=1, source_target_pairs={{0,31},{1,28},{2,29},{3,30},{4,3},{5,0},{6,1},{7,2},{8,7},{9,4},{1... | collective-permute-start | bytes 589832 | tf_op jit(solution)/shard_map/ppermute | solution.py:172
  16.8 2.3 %collective-permute-start.3 = (f32[6,64,128]{2,1,0:T(8,128)S(1)}, f32[6,64,128]{2,1,0:T(8,128)S(1)}, u32[]{:S(2)}, u32[]{:S(2)}) collective-permute-start(f32[6,64,128]{2,1,0:T(8,128)S(1)} %get-tuple-element.24), channel_id=1, source_target_pairs={{0,28},{1,29},{2,30},{3,31},{4,0},{5,1},{6,2},{7,3},{8,4},{9,5},{1... | collective-permute-start | bytes 589832 | tf_op jit(solution)/shard_map/ppermute | solution.py:172
  19.1 2.5 %collective-permute-start.1 = (s32[2,27]{1,0:T(2,128)S(1)}, s32[2,27]{1,0:T(2,128)S(1)}, u32[]{:S(2)}, u32[]{:S(2)}) collective-permute-start(s32[2,27]{1,0:T(2,128)S(1)} %bitcast.3), channel_id=1, source_target_pairs={{0,96},{1,97},{2,98},{3,99},{4,100},{5,101},{6,102},{7,103},{8,104... | collective-permute-start | bytes 656 | tf_op jit(solution)/shard_map/ppermute | solution.py:172
  21.5 0.7 collective-permute-done.1.refs_2_
  22.3 3.4 %collective-permute-start.5 = (f32[6,64,128]{2,1,0:T(8,128)S(1)}, f32[6,64,128]{2,1,0:T(8,128)S(1)}, u32[]{:S(2)}, u32[]{:S(2)}) collective-permute-start(f32[6,64,128]{2,1,0:T(8,128)S(1)} %get-tuple-element.26), channel_id=1, source_target_pairs={{0,3},{1,0},{2,1},{3,2},{4,7},{5,4},{6,5},{7,6},{8,11},{9,8},{10,9... | collective-permute-start | bytes 589832 | tf_op jit(solution)/shard_map/ppermute | solution.py:172
  25.7 4.8 %collective-permute-start.7 = (f32[6,64,128]{2,1,0:T(8,128)S(1)}, f32[6,64,128]{2,1,0:T(8,128)S(1)}, u32[]{:S(2)}, u32[]{:S(2)}) collective-permute-start(f32[6,64,128]{2,1,0:T(8,128)S(1)} %get-tuple-element.29), channel_id=1, source_target_pairs={{0,7},{1,4},{2,5},{3,6},{4,11},{5,8},{6,9},{7,10},{8,15},{9,12},{1... | collective-permute-start | bytes 589832 | tf_op jit(solution)/shard_map/ppermute | solution.py:172
  30.5 0.1 collective-permute-start.9
  30.6 1.4 %collective-permute-done.6.refs_8_ = f32[6,64,128]{2,1,0:T(8,128)S(1)} collective-permute-done((f32[6,64,128]{2,1,0:T(8,128)S(1)}, f32[6,64,128]{2,1,0:T(8,128)S(1)}, u32[]{:S(2)}, u32[]{:S(2)}) %collective-permute-start.6) | collective-permute-done | bytes 196640 | tf_op jit(solution)/shard_map/ppermute | solution.py:172
  32.0 1.2 %collective-permute-done.7.refs_9_ = f32[6,64,128]{2,1,0:T(8,128)S(1)} collective-permute-done((f32[6,64,128]{2,1,0:T(8,128)S(1)}, f32[6,64,128]{2,1,0:T(8,128)S(1)}, u32[]{:S(2)}, u32[]{:S(2)}) %collective-permute-start.7) | collective-permute-done | bytes 196640 | tf_op jit(solution)/shard_map/ppermute | solution.py:172
  33.1 2.1 %collective-permute-done.8.refs_10_ = f32[6,64,128]{2,1,0:T(8,128)S(1)} collective-permute-done((f32[6,64,128]{2,1,0:T(8,128)S(1)}, f32[6,64,128]{2,1,0:T(8,128)S(1)}, u32[]{:S(2)}, u32[]{:S(2)}) %collective-permute-start.8) | collective-permute-done | bytes 196640 | tf_op jit(solution)/shard_map/ppermute | solution.py:172
  35.2 2.1 %collective-permute-done.9.refs_11_ = f32[6,64,128]{2,1,0:T(8,128)S(1)} collective-permute-done((f32[6,64,128]{2,1,0:T(8,128)S(1)}, f32[6,64,128]{2,1,0:T(8,128)S(1)}, u32[]{:S(2)}, u32[]{:S(2)}) %collective-permute-start.9) | collective-permute-done | bytes 196640 | tf_op jit(solution)/shard_map/ppermute | solution.py:172
  37.3 1.0 %shard_map.69 = (f32[8,64,128]{2,1,0:T(8,128)S(1)}, f32[8,64,128]{2,1,0:T(8,128)S(1)}, f32[8,64,128]{2,1,0:T(8,128)S(1)}) custom-call(s32[2,27]{1,0:T(2,128)S(1)} %collective-permute-done.refs_0_, s32[2,27]{1,0:T(2,128)S(1)} %bitcast.5, s32[2,27]{1,0:T(2,128)S(1)} %collective-permute-done.1.refs_2_, f32[6,64,128]{2,1,0:T(8,128)S(1)} %collective-permute-done.2.refs_3_, ...), custom_call_target="tpu_custom_call" | custom-call | tf_op jit(solution)/shard_map/pallas_call | solution.py:100
  38.3 0.5 collective-permute-start.10
  38.9 4.2 %collective-permute-start.11 = (f32[8,64,128]{2,1,0:T(8,128)S(1)}, f32[8,64,128]{2,1,0:T(8,128)S(1)}, u32[]{:S(2)}, u32[]{:S(2)}) collective-permute-start(f32[8,64,128]{2,1,0:T(8,128)S(1)} %get-tuple-element.34), channel_id=1, source_target_pairs={{0,96},{1,97},{2,98},{3,99},{4,100},{5,101},{6,102},{7,103},{8,104... | collective-permute-start | bytes 786440 | tf_op jit(solution)/shard_map/ppermute | solution.py:172
  43.1 3.7 %collective-permute-done.10 = f32[8,64,128]{2,1,0:T(8,128)S(1)} collective-permute-done((f32[8,64,128]{2,1,0:T(8,128)S(1)}, f32[8,64,128]{2,1,0:T(8,128)S(1)}, u32[]{:S(2)}, u32[]{:S(2)}) %collective-permute-start.10) | collective-permute-done | bytes 262176 | tf_op jit(solution)/shard_map/ppermute | solution.py:172
  46.8 3.7 %collective-permute-start.13 = (f32[8,64,128]{2,1,0:T(8,128)S(1)}, f32[8,64,128]{2,1,0:T(8,128)S(1)}, u32[]{:S(2)}, u32[]{:S(2)}) collective-permute-start(f32[8,64,128]{2,1,0:T(8,128)S(1)} %add_add_fusion.refs_4_), channel_id=1, source_target_pairs={{0,96},{1,97},{2,98},{3,99},{4,100},{5,101},{6,102},{7,103},{8,104... | collective-permute-start | bytes 786440 | tf_op jit(solution)/shard_map/ppermute | solution.py:172
  50.5 3.8 %collective-permute-done.13.refs_5_ = f32[8,64,128]{2,1,0:T(8,128)S(1)} collective-permute-done((f32[8,64,128]{2,1,0:T(8,128)S(1)}, f32[8,64,128]{2,1,0:T(8,128)S(1)}, u32[]{:S(2)}, u32[]{:S(2)}) %collective-permute-start.13) | collective-permute-done | bytes 262176 | tf_op jit(solution)/shard_map/ppermute | solution.py:172
  54.3 2.7 %collective-permute-done.12.refs_3_ = f32[8,64,128]{2,1,0:T(8,128)S(1)} collective-permute-done((f32[8,64,128]{2,1,0:T(8,128)S(1)}, f32[8,64,128]{2,1,0:T(8,128)S(1)}, u32[]{:S(2)}, u32[]{:S(2)}) %collective-permute-start.12) | collective-permute-done | bytes 262176 | tf_op jit(solution)/shard_map/ppermute | solution.py:172
  57.0 0.7 shard_map.70
  57.7 4.8 %collective-permute-start.14 = (f32[6,64,128]{2,1,0:T(8,128)S(1)}, f32[6,64,128]{2,1,0:T(8,128)S(1)}, u32[]{:S(2)}, u32[]{:S(2)}) collective-permute-start(f32[6,64,128]{2,1,0:T(8,128)S(1)} %get-tuple-element.35), channel_id=1, source_target_pairs={{0,5},{1,6},{2,7},{3,4},{4,9},{5,10},{6,11},{7,8},{8,13},{9,14},{1... | collective-permute-start | bytes 589832 | tf_op jit(solution)/shard_map/ppermute | solution.py:172
  62.4 2.9 %collective-permute-start.16 = (f32[6,64,128]{2,1,0:T(8,128)S(1)}, f32[6,64,128]{2,1,0:T(8,128)S(1)}, u32[]{:S(2)}, u32[]{:S(2)}) collective-permute-start(f32[6,64,128]{2,1,0:T(8,128)S(1)} %get-tuple-element.37), channel_id=1, source_target_pairs={{0,7},{1,4},{2,5},{3,6},{4,11},{5,8},{6,9},{7,10},{8,15},{9,12},{1... | collective-permute-start | bytes 589832 | tf_op jit(solution)/shard_map/ppermute | solution.py:172
  65.3 2.7 %collective-permute-start.18 = (f32[6,64,128]{2,1,0:T(8,128)S(1)}, f32[6,64,128]{2,1,0:T(8,128)S(1)}, u32[]{:S(2)}, u32[]{:S(2)}) collective-permute-start(f32[6,64,128]{2,1,0:T(8,128)S(1)} %get-tuple-element.40), channel_id=1, source_target_pairs={{0,3},{1,0},{2,1},{3,2},{4,7},{5,4},{6,5},{7,6},{8,11},{9,8},{10,9... | collective-permute-start | bytes 589832 | tf_op jit(solution)/shard_map/ppermute | solution.py:172
  68.0 3.6 %collective-permute-start.19 = (f32[6,64,128]{2,1,0:T(8,128)S(1)}, f32[6,64,128]{2,1,0:T(8,128)S(1)}, u32[]{:S(2)}, u32[]{:S(2)}) collective-permute-start(f32[6,64,128]{2,1,0:T(8,128)S(1)} %get-tuple-element.41), channel_id=1, source_target_pairs={{0,29},{1,30},{2,31},{3,28},{4,1},{5,2},{6,3},{7,0},{8,5},{9,6},{1... | collective-permute-start | bytes 589832 | tf_op jit(solution)/shard_map/ppermute | solution.py:172
  71.6 0.9 %collective-permute-start.20 = (f32[6,64,128]{2,1,0:T(8,128)S(1)}, f32[6,64,128]{2,1,0:T(8,128)S(1)}, u32[]{:S(2)}, u32[]{:S(2)}) collective-permute-start(f32[6,64,128]{2,1,0:T(8,128)S(1)} %get-tuple-element.42), channel_id=1, source_target_pairs={{0,28},{1,29},{2,30},{3,31},{4,0},{5,1},{6,2},{7,3},{8,4},{9,5},{1... | collective-permute-start | bytes 589832 | tf_op jit(solution)/shard_map/ppermute | solution.py:172
  72.5 4.5 %collective-permute-start.21 = (f32[6,64,128]{2,1,0:T(8,128)S(1)}, f32[6,64,128]{2,1,0:T(8,128)S(1)}, u32[]{:S(2)}, u32[]{:S(2)}) collective-permute-start(f32[6,64,128]{2,1,0:T(8,128)S(1)} %get-tuple-element.43), channel_id=1, source_target_pairs={{0,31},{1,28},{2,29},{3,30},{4,3},{5,0},{6,1},{7,2},{8,7},{9,4},{1... | collective-permute-start | bytes 589832 | tf_op jit(solution)/shard_map/ppermute | solution.py:172
  77.0 3.5 %collective-permute-done.21.refs_8_ = f32[6,64,128]{2,1,0:T(8,128)S(1)} collective-permute-done((f32[6,64,128]{2,1,0:T(8,128)S(1)}, f32[6,64,128]{2,1,0:T(8,128)S(1)}, u32[]{:S(2)}, u32[]{:S(2)}) %collective-permute-start.21) | collective-permute-done | bytes 196640 | tf_op jit(solution)/shard_map/ppermute | solution.py:172
  80.5 2.3 %shard_map.71 = f32[4,9,64,128]{3,2,1,0:T(8,128)} custom-call(s32[4,9]{1,0:T(4,128)S(1)} %copy-done.4, s32[4,9]{1,0:T(4,128)S(1)} %copy-done.6, f32[6,64,128]{2,1,0:T(8,128)S(1)} %collective-permute-done.14.refs_0_, f32[6,64,128]{2,1,0:T(8,128)S(1)} %collective-permute-done.15.refs_1_, f32[6,64,128]{2,1,0:T(8,128)S(1)} %collective-permute-done.16.refs_2_, ...), custom_call_target="tpu_custom_call" | custom-call | tf_op jit(solution)/shard_map/pallas_call | solution.py:151
  (33 shorter events, 0.1 us)
Async XLA Ops:
  0.6 4.0 %copy-start = (bf16[4,1152,1152]{2,1,0:T(8,128)(2,1)S(1)}, bf16[4,1152,1152]{2,1,0:T(8,128)(2,1)}, u32[]{:S(2)}) copy-start(bf16[4,1152,1152]{2,1,0:T(8,128)(2,1)} %inverse_ref.1) | copy-start | bytes 31850500
  4.6 1.1 %copy-start.2 = (bf16[4,64,1152]{2,1,0:T(8,128)(2,1)S(1)}, bf16[4,64,1152]{2,1,0:T(8,128)(2,1)}, u32[]{:S(2)}) copy-start(bf16[4,64,1152]{2,1,0:T(8,128)(2,1)} %residual_ref.1) | copy-start | bytes 1769476
  5.7 0.7 copy-start.3
  6.4 0.7 copy-start.5
  7.1 12.0 %copy-start.7 = (s32[1,27,2]{1,2,0:T(2,128)S(1)}, s32[1,27,2]{1,2,0:T(2,128)}, u32[]{:S(2)}) copy-start(s32[1,27,2]{1,2,0:T(2,128)} %param.9) | copy-start | bytes 652
  7.1 73.4 %copy-start.4 = (s32[4,9]{1,0:T(4,128)S(1)}, s32[4,9]{1,0:T(4,128)}, u32[]{:S(2)}) copy-start(s32[4,9]{1,0:T(4,128)} %owner_ref.3) | copy-start | bytes 436
  7.1 73.4 %copy-start.6 = (s32[4,9]{1,0:T(4,128)S(1)}, s32[4,9]{1,0:T(4,128)}, u32[]{:S(2)}) copy-start(s32[4,9]{1,0:T(4,128)} %slot_ref.3) | copy-start | bytes 436
  11.6 14.1 %collective-permute-start.2 = (f32[6,64,128]{2,1,0:T(8,128)S(1)}, f32[6,64,128]{2,1,0:T(8,128)S(1)}, u32[]{:S(2)}, u32[]{:S(2)}) collective-permute-start(f32[6,64,128]{2,1,0:T(8,128)S(1)} %get-tuple-element.23), channel_id=1, source_target_pairs={{0,31},{1,28},{2,29},{3,30},{4,3},{5,0},{6,1},{7,2},{8,7},{9,4},{1... | collective-permute-start | bytes 589832 | tf_op jit(solution)/shard_map/ppermute | solution.py:172
  16.8 13.7 %collective-permute-start.3 = (f32[6,64,128]{2,1,0:T(8,128)S(1)}, f32[6,64,128]{2,1,0:T(8,128)S(1)}, u32[]{:S(2)}, u32[]{:S(2)}) collective-permute-start(f32[6,64,128]{2,1,0:T(8,128)S(1)} %get-tuple-element.24), channel_id=1, source_target_pairs={{0,28},{1,29},{2,30},{3,31},{4,0},{5,1},{6,2},{7,3},{8,4},{9,5},{1... | collective-permute-start | bytes 589832 | tf_op jit(solution)/shard_map/ppermute | solution.py:172
  19.1 11.4 %collective-permute-start.4 = (f32[6,64,128]{2,1,0:T(8,128)S(1)}, f32[6,64,128]{2,1,0:T(8,128)S(1)}, u32[]{:S(2)}, u32[]{:S(2)}) collective-permute-start(f32[6,64,128]{2,1,0:T(8,128)S(1)} %get-tuple-element.25), channel_id=1, source_target_pairs={{0,29},{1,30},{2,31},{3,28},{4,1},{5,2},{6,3},{7,0},{8,5},{9,6},{1... | collective-permute-start | bytes 589832 | tf_op jit(solution)/shard_map/ppermute | solution.py:172
  19.1 3.2 %collective-permute-start.1 = (s32[2,27]{1,0:T(2,128)S(1)}, s32[2,27]{1,0:T(2,128)S(1)}, u32[]{:S(2)}, u32[]{:S(2)}) collective-permute-start(s32[2,27]{1,0:T(2,128)S(1)} %bitcast.3), channel_id=1, source_target_pairs={{0,96},{1,97},{2,98},{3,99},{4,100},{5,101},{6,102},{7,103},{8,104... | collective-permute-start | bytes 656 | tf_op jit(solution)/shard_map/ppermute | solution.py:172
  21.5 4.1 %collective-permute-start = (s32[2,27]{1,0:T(2,128)S(1)}, s32[2,27]{1,0:T(2,128)S(1)}, u32[]{:S(2)}, u32[]{:S(2)}) collective-permute-start(s32[2,27]{1,0:T(2,128)S(1)} %bitcast.4), channel_id=1, source_target_pairs={{0,32},{1,33},{2,34},{3,35},{4,36},{5,37},{6,38},{7,39},{8,40},{9,... | collective-permute-start | bytes 656 | tf_op jit(solution)/shard_map/ppermute | solution.py:172
  22.3 8.3 %collective-permute-start.5 = (f32[6,64,128]{2,1,0:T(8,128)S(1)}, f32[6,64,128]{2,1,0:T(8,128)S(1)}, u32[]{:S(2)}, u32[]{:S(2)}) collective-permute-start(f32[6,64,128]{2,1,0:T(8,128)S(1)} %get-tuple-element.26), channel_id=1, source_target_pairs={{0,3},{1,0},{2,1},{3,2},{4,7},{5,4},{6,5},{7,6},{8,11},{9,8},{10,9... | collective-permute-start | bytes 589832 | tf_op jit(solution)/shard_map/ppermute | solution.py:172
  25.7 6.3 %collective-permute-start.6 = (f32[6,64,128]{2,1,0:T(8,128)S(1)}, f32[6,64,128]{2,1,0:T(8,128)S(1)}, u32[]{:S(2)}, u32[]{:S(2)}) collective-permute-start(f32[6,64,128]{2,1,0:T(8,128)S(1)} %get-tuple-element.28), channel_id=1, source_target_pairs={{0,1},{1,2},{2,3},{3,0},{4,5},{5,6},{6,7},{7,4},{8,9},{9,10},{10,1... | collective-permute-start | bytes 589832 | tf_op jit(solution)/shard_map/ppermute | solution.py:172
  25.7 7.4 %collective-permute-start.7 = (f32[6,64,128]{2,1,0:T(8,128)S(1)}, f32[6,64,128]{2,1,0:T(8,128)S(1)}, u32[]{:S(2)}, u32[]{:S(2)}) collective-permute-start(f32[6,64,128]{2,1,0:T(8,128)S(1)} %get-tuple-element.29), channel_id=1, source_target_pairs={{0,7},{1,4},{2,5},{3,6},{4,11},{5,8},{6,9},{7,10},{8,15},{9,12},{1... | collective-permute-start | bytes 589832 | tf_op jit(solution)/shard_map/ppermute | solution.py:172
  30.5 4.8 %collective-permute-start.8 = (f32[6,64,128]{2,1,0:T(8,128)S(1)}, f32[6,64,128]{2,1,0:T(8,128)S(1)}, u32[]{:S(2)}, u32[]{:S(2)}) collective-permute-start(f32[6,64,128]{2,1,0:T(8,128)S(1)} %get-tuple-element.30), channel_id=1, source_target_pairs={{0,4},{1,5},{2,6},{3,7},{4,8},{5,9},{6,10},{7,11},{8,12},{9,13},{1... | collective-permute-start | bytes 589832 | tf_op jit(solution)/shard_map/ppermute | solution.py:172
  30.5 6.9 %collective-permute-start.9 = (f32[6,64,128]{2,1,0:T(8,128)S(1)}, f32[6,64,128]{2,1,0:T(8,128)S(1)}, u32[]{:S(2)}, u32[]{:S(2)}) collective-permute-start(f32[6,64,128]{2,1,0:T(8,128)S(1)} %get-tuple-element.31), channel_id=1, source_target_pairs={{0,5},{1,6},{2,7},{3,4},{4,9},{5,10},{6,11},{7,8},{8,13},{9,14},{1... | collective-permute-start | bytes 589832 | tf_op jit(solution)/shard_map/ppermute | solution.py:172
  38.3 8.5 %collective-permute-start.10 = (f32[8,64,128]{2,1,0:T(8,128)S(1)}, f32[8,64,128]{2,1,0:T(8,128)S(1)}, u32[]{:S(2)}, u32[]{:S(2)}) collective-permute-start(f32[8,64,128]{2,1,0:T(8,128)S(1)} %get-tuple-element.33), channel_id=1, source_target_pairs={{0,32},{1,33},{2,34},{3,35},{4,36},{5,37},{6,38},{7,39},{8,40},{9,... | collective-permute-start | bytes 786440 | tf_op jit(solution)/shard_map/ppermute | solution.py:172
  38.9 7.9 %collective-permute-start.11 = (f32[8,64,128]{2,1,0:T(8,128)S(1)}, f32[8,64,128]{2,1,0:T(8,128)S(1)}, u32[]{:S(2)}, u32[]{:S(2)}) collective-permute-start(f32[8,64,128]{2,1,0:T(8,128)S(1)} %get-tuple-element.34), channel_id=1, source_target_pairs={{0,96},{1,97},{2,98},{3,99},{4,100},{5,101},{6,102},{7,103},{8,104... | collective-permute-start | bytes 786440 | tf_op jit(solution)/shard_map/ppermute | solution.py:172
  46.8 35.9 %copy-start.1 = (f32[8,64,128]{2,1,0:T(8,128)}, f32[8,64,128]{2,1,0:T(8,128)S(1)}, u32[]{:S(2)}) copy-start(f32[8,64,128]{2,1,0:T(8,128)S(1)} %add_add_fusion.refs_4_) | copy-start | bytes 786436
  46.8 7.4 %collective-permute-start.13 = (f32[8,64,128]{2,1,0:T(8,128)S(1)}, f32[8,64,128]{2,1,0:T(8,128)S(1)}, u32[]{:S(2)}, u32[]{:S(2)}) collective-permute-start(f32[8,64,128]{2,1,0:T(8,128)S(1)} %add_add_fusion.refs_4_), channel_id=1, source_target_pairs={{0,96},{1,97},{2,98},{3,99},{4,100},{5,101},{6,102},{7,103},{8,104... | collective-permute-start | bytes 786440 | tf_op jit(solution)/shard_map/ppermute | solution.py:172
  50.5 6.4 %collective-permute-start.12 = (f32[8,64,128]{2,1,0:T(8,128)S(1)}, f32[8,64,128]{2,1,0:T(8,128)S(1)}, u32[]{:S(2)}, u32[]{:S(2)}) collective-permute-start(f32[8,64,128]{2,1,0:T(8,128)S(1)} %add_add_fusion.refs_4_), channel_id=1, source_target_pairs={{0,32},{1,33},{2,34},{3,35},{4,36},{5,37},{6,38},{7,39},{8,40},{9,... | collective-permute-start | bytes 786440 | tf_op jit(solution)/shard_map/ppermute | solution.py:172
  57.7 10.4 %collective-permute-start.14 = (f32[6,64,128]{2,1,0:T(8,128)S(1)}, f32[6,64,128]{2,1,0:T(8,128)S(1)}, u32[]{:S(2)}, u32[]{:S(2)}) collective-permute-start(f32[6,64,128]{2,1,0:T(8,128)S(1)} %get-tuple-element.35), channel_id=1, source_target_pairs={{0,5},{1,6},{2,7},{3,4},{4,9},{5,10},{6,11},{7,8},{8,13},{9,14},{1... | collective-permute-start | bytes 589832 | tf_op jit(solution)/shard_map/ppermute | solution.py:172
  62.4 9.2 %collective-permute-start.15 = (f32[6,64,128]{2,1,0:T(8,128)S(1)}, f32[6,64,128]{2,1,0:T(8,128)S(1)}, u32[]{:S(2)}, u32[]{:S(2)}) collective-permute-start(f32[6,64,128]{2,1,0:T(8,128)S(1)} %get-tuple-element.36), channel_id=1, source_target_pairs={{0,4},{1,5},{2,6},{3,7},{4,8},{5,9},{6,10},{7,11},{8,12},{9,13},{1... | collective-permute-start | bytes 589832 | tf_op jit(solution)/shard_map/ppermute | solution.py:172
  62.4 10.1 %collective-permute-start.16 = (f32[6,64,128]{2,1,0:T(8,128)S(1)}, f32[6,64,128]{2,1,0:T(8,128)S(1)}, u32[]{:S(2)}, u32[]{:S(2)}) collective-permute-start(f32[6,64,128]{2,1,0:T(8,128)S(1)} %get-tuple-element.37), channel_id=1, source_target_pairs={{0,7},{1,4},{2,5},{3,6},{4,11},{5,8},{6,9},{7,10},{8,15},{9,12},{1... | collective-permute-start | bytes 589832 | tf_op jit(solution)/shard_map/ppermute | solution.py:172
  65.3 11.7 %collective-permute-start.17 = (f32[6,64,128]{2,1,0:T(8,128)S(1)}, f32[6,64,128]{2,1,0:T(8,128)S(1)}, u32[]{:S(2)}, u32[]{:S(2)}) collective-permute-start(f32[6,64,128]{2,1,0:T(8,128)S(1)} %get-tuple-element.38), channel_id=1, source_target_pairs={{0,1},{1,2},{2,3},{3,0},{4,5},{5,6},{6,7},{7,4},{8,9},{9,10},{10,1... | collective-permute-start | bytes 589832 | tf_op jit(solution)/shard_map/ppermute | solution.py:172
  65.3 11.7 %collective-permute-start.18 = (f32[6,64,128]{2,1,0:T(8,128)S(1)}, f32[6,64,128]{2,1,0:T(8,128)S(1)}, u32[]{:S(2)}, u32[]{:S(2)}) collective-permute-start(f32[6,64,128]{2,1,0:T(8,128)S(1)} %get-tuple-element.40), channel_id=1, source_target_pairs={{0,3},{1,0},{2,1},{3,2},{4,7},{5,4},{6,5},{7,6},{8,11},{9,8},{10,9... | collective-permute-start | bytes 589832 | tf_op jit(solution)/shard_map/ppermute | solution.py:172
  68.0 9.0 %collective-permute-start.19 = (f32[6,64,128]{2,1,0:T(8,128)S(1)}, f32[6,64,128]{2,1,0:T(8,128)S(1)}, u32[]{:S(2)}, u32[]{:S(2)}) collective-permute-start(f32[6,64,128]{2,1,0:T(8,128)S(1)} %get-tuple-element.41), channel_id=1, source_target_pairs={{0,29},{1,30},{2,31},{3,28},{4,1},{5,2},{6,3},{7,0},{8,5},{9,6},{1... | collective-permute-start | bytes 589832 | tf_op jit(solution)/shard_map/ppermute | solution.py:172
  71.6 5.4 %collective-permute-start.20 = (f32[6,64,128]{2,1,0:T(8,128)S(1)}, f32[6,64,128]{2,1,0:T(8,128)S(1)}, u32[]{:S(2)}, u32[]{:S(2)}) collective-permute-start(f32[6,64,128]{2,1,0:T(8,128)S(1)} %get-tuple-element.42), channel_id=1, source_target_pairs={{0,28},{1,29},{2,30},{3,31},{4,0},{5,1},{6,2},{7,3},{8,4},{9,5},{1... | collective-permute-start | bytes 589832 | tf_op jit(solution)/shard_map/ppermute | solution.py:172
  72.5 8.0 %collective-permute-start.21 = (f32[6,64,128]{2,1,0:T(8,128)S(1)}, f32[6,64,128]{2,1,0:T(8,128)S(1)}, u32[]{:S(2)}, u32[]{:S(2)}) collective-permute-start(f32[6,64,128]{2,1,0:T(8,128)S(1)} %get-tuple-element.43), channel_id=1, source_target_pairs={{0,31},{1,28},{2,29},{3,30},{4,3},{5,0},{6,1},{7,2},{8,7},{9,4},{1... | collective-permute-start | bytes 589832 | tf_op jit(solution)/shard_map/ppermute | solution.py:172

commit v2 on v1

v2 whole, which is shorter than its diff:
```python
import functools

import jax
import jax.numpy as jnp
from jax import lax
from jax.experimental import pallas as pl
from jax.experimental.pallas import tpu as pltpu
from jax.sharding import PartitionSpec as P

OWNB = 8
AXES = ("gx", "gy", "gz")
VMEM = pltpu.VMEM
SMEM = pltpu.SMEM

PLANE = [(1, 0), (-1, 0), (1, 2), (-1, 2), (0, 2), (1, 1), (-1, 1), (0, 1), (0, 0)]
HOME = len(PLANE) - 1


def toward(y, way):
    if way == 0:
        return y
    up = (y % 2 == 0) == (way == 1)
    return y + 1 if up else y - 1


def way_code(way, near_y):
    if way == 0:
        return 1
    even = lax.rem(near_y, 2) == 0
    return jnp.where(even, 2, 0) if way == 1 else jnp.where(even, 0, 2)


def axis_code(far, near, extent):
    ahead = jnp.where(near == extent - 1, 0, near + 1)
    return jnp.where(far == near, 1, jnp.where(far == ahead, 2, 0))


def place(owner, slot, near, extents, capacity):
    size_x, size_y, size_z = extents
    code_x = axis_code(lax.div(owner, size_y * size_z), near[0], size_x)
    code_y = axis_code(lax.rem(lax.div(owner, size_z), size_y), near[1], size_y)
    code_z = axis_code(lax.rem(owner, size_z), near[2], size_z)
    return ((code_x * 3 + code_y) * 3 + code_z) * capacity + slot


def contribute_kernel(extents, capacity, blocks, key_hbm, residual_hbm, inverse_hbm, *rest):
    outs = rest[:9]
    back, placed, key, residual, inverse, key_sem, res_sem, inv_sem = rest[9:]
    patches = inverse.shape[0]
    key_copy = pltpu.make_async_copy(key_hbm, key, key_sem)
    res_copy = pltpu.make_async_copy(residual_hbm, residual, res_sem)
    inv_copies = [
        pltpu.make_async_copy(inverse_hbm.at[p], inverse.at[p], inv_sem.at[p])
        for p in range(patches)
    ]
    key_copy.start()
    res_copy.start()
    for copy in inv_copies:
        copy.start()

    width = inverse.shape[1] // blocks
    near = [lax.axis_index(a) for a in AXES]
    per = 3 * capacity
    for k in range(9 * per):
        back[k] = patches * blocks
    key_copy.wait()
    at = []
    for p in range(patches):
        for b in range(blocks):
            owner, slot = lax.div(key[p, b], capacity), lax.rem(key[p, b], capacity)
            at.append(place(owner, slot, near, extents, capacity))
            back[at[-1]] = p * blocks + b
    res_copy.wait()
    for p in range(patches):
        inv_copies[p].wait()
        product = lax.dot_general(
            residual[p],
            inverse[p],
            (((1,), (1,)), ((), ())),
            preferred_element_type=jnp.float32,
        )
        for b in range(blocks):
            placed[at[p * blocks + b]] = product[:, b * width : (b + 1) * width]
    for i, (dx, way) in enumerate(PLANE):
        first = ((dx + 1) * 3 + way_code(way, near[1])) * per
        for k in range(per):
            outs[i][k] = placed[first + k]


def contribute(key, residual, inverse, extents, capacity):
    patches, rhs, order = residual.shape
    blocks = key.shape[1]
    width = order // blocks
    per = 3 * capacity
    return pl.pallas_call(
        functools.partial(contribute_kernel, extents, capacity, blocks),
        in_specs=[pl.BlockSpec(memory_space=pl.ANY)] * 3,
        out_specs=[pl.BlockSpec(memory_space=VMEM)] * 9 + [pl.BlockSpec(memory_space=SMEM)],
        out_shape=[jax.ShapeDtypeStruct((per, rhs, width), jnp.float32)] * 9
        + [jax.ShapeDtypeStruct((9 * per,), jnp.int32)],
        scratch_shapes=[
            VMEM((9 * per, rhs, width), jnp.float32),
            SMEM(key.shape, jnp.int32),
            VMEM(residual.shape, residual.dtype),
            VMEM(inverse.shape, inverse.dtype),
            pltpu.SemaphoreType.DMA,
            pltpu.SemaphoreType.DMA,
            pltpu.SemaphoreType.DMA((patches,)),
        ],
        compiler_params=pltpu.CompilerParams(vmem_limit_bytes=52 * 2**20),
    )(key, residual, inverse)


def entry(tables, plane, cz, c, near_y):
    dx, way = PLANE[plane]
    code_y = 1 if way == 0 else 2 - way_code(way, near_y)
    return tables[cz][c, 9 * (dx + 1) + 3 * code_y + cz]


def gather_kernel(capacity, *refs):
    tables, arrived = refs[0:3], refs[3:12]
    outs, total = refs[12:15], refs[15]
    near_y = lax.axis_index("gy")
    total[...] = jnp.zeros_like(total)
    for i in range(9):
        for cz in range(3):
            for c in range(capacity):
                t = entry(tables, i, cz, c, near_y)
                t = jnp.where(t < 0, OWNB, t)
                total[cz, t] += arrived[i][cz * capacity + c]
    for cz in range(3):
        outs[cz][...] = total[cz, :OWNB]


def gather(tables, arrived, capacity):
    _, rhs, width = arrived[0].shape
    return pl.pallas_call(
        functools.partial(gather_kernel, capacity),
        in_specs=[pl.BlockSpec(memory_space=SMEM)] * 3 + [pl.BlockSpec(memory_space=VMEM)] * 9,
        out_specs=[pl.BlockSpec(memory_space=VMEM)] * 3,
        out_shape=[jax.ShapeDtypeStruct((OWNB, rhs, width), jnp.float32)] * 3,
        scratch_shapes=[VMEM((3, OWNB + 1, rhs, width), jnp.float32)],
        compiler_params=pltpu.CompilerParams(vmem_limit_bytes=32 * 2**20),
    )(*tables, *arrived)


def answer_kernel(capacity, *refs):
    tables, totals, outs = refs[0:3], refs[3:6], refs[6:15]
    near_y = lax.axis_index("gy")
    for i in range(9):
        for cz in range(3):
            for c in range(capacity):
                t = entry(tables, i, cz, c, near_y)
                outs[i][cz * capacity + c] = totals[cz][jnp.maximum(t, 0)]


def answer(tables, totals, capacity):
    _, rhs, width = totals[0].shape
    per = 3 * capacity
    return pl.pallas_call(
        functools.partial(answer_kernel, capacity),
        in_specs=[pl.BlockSpec(memory_space=SMEM)] * 3 + [pl.BlockSpec(memory_space=VMEM)] * 3,
        out_specs=[pl.BlockSpec(memory_space=VMEM)] * 9,
        out_shape=[jax.ShapeDtypeStruct((per, rhs, width), jnp.float32)] * 9,
        compiler_params=pltpu.CompilerParams(vmem_limit_bytes=32 * 2**20),
    )(*tables, *totals)


def collect_kernel(capacity, patches, blocks, back, *refs):
    returned, out, wide = refs[0:9], refs[9], refs[10]
    near_y = lax.axis_index("gy")
    per = 3 * capacity
    for i, (dx, way) in enumerate(PLANE):
        first = ((dx + 1) * 3 + way_code(way, near_y)) * per
        for k in range(per):
            wide[back[first + k]] = returned[i][k]
    for p in range(patches):
        out[p] = wide[p * blocks : (p + 1) * blocks]


def collect(back, returned, patches, blocks, capacity):
    _, rhs, width = returned[0].shape
    return pl.pallas_call(
        functools.partial(collect_kernel, capacity, patches, blocks),
        in_specs=[pl.BlockSpec(memory_space=SMEM)] + [pl.BlockSpec(memory_space=VMEM)] * 9,
        out_specs=pl.BlockSpec(memory_space=VMEM),
        out_shape=jax.ShapeDtypeStruct((patches, blocks, rhs, width), jnp.float32),
        scratch_shapes=[VMEM((patches * blocks + 1, rhs, width), jnp.float32)],
        compiler_params=pltpu.CompilerParams(vmem_limit_bytes=32 * 2**20),
    )(back, *returned)


def move(array, extents, dx, way, dz):
    size_x, size_y, size_z = extents
    pairs = []
    for x in range(size_x):
        for y in range(size_y):
            for z in range(size_z):
                to_x, to_y, to_z = (x + dx) % size_x, toward(y, way) % size_y, (z + dz) % size_z
                pairs.append(
                    ((x * size_y + y) * size_z + z, (to_x * size_y + to_y) * size_z + to_z)
                )
    return lax.ppermute(array, AXES, pairs)


def on_device(star_residual, patch_inverse, block_owner, block_slot, recv_target):
    extents = tuple(lax.axis_size(a) for a in AXES)
    capacity = recv_target.shape[2]
    table = jnp.swapaxes(recv_target, 1, 2)[0]
    key = block_owner * capacity + block_slot
    *outgoing, back = contribute(key, star_residual, patch_inverse, extents, capacity)
    arrived = [
        outgoing[i] if i == HOME else move(outgoing[i], extents, dx, way, 0)
        for i, (dx, way) in enumerate(PLANE)
    ]
    table, arrived[7] = lax.optimization_barrier((table, arrived[7]))
    tables = [move(table, extents, 0, 0, 1), table, move(table, extents, 0, 0, -1)]
    below, own, above = gather(tables, arrived, capacity)
    owned = own + move(above, extents, 0, 0, 1) + move(below, extents, 0, 0, -1)
    totals = [move(owned, extents, 0, 0, 1), owned, move(owned, extents, 0, 0, -1)]
    answers = answer(tables, totals, capacity)
    returned = [
        answers[i] if i == HOME else move(answers[i], extents, -dx, way, 0)
        for i, (dx, way) in enumerate(PLANE)
    ]
    combined = collect(back, returned, *block_owner.shape, capacity)
    return owned, combined


def solution(mesh):
    return jax.shard_map(
        on_device,
        mesh=mesh,
        in_specs=(
            P(AXES, None, None),
            P(AXES, None, None),
            P(AXES, None),
            P(AXES, None),
            P(AXES, None, None),
        ),
        out_specs=(P(AXES, None, None), P(AXES, None, None, None)),
        check_vma=False,
    )
```

time: 83 us -> 74.1 us (0.89)
  starting transfers between devices: 46 us -> 38.1 us
  local copies, waits for them, and re-layouts: 6.45 us -> 0.01 us
  Pallas kernels: 8.4 us -> 11.4 us
  waiting for transfers between devices: 21.1 us -> 22.9 us
    ppermute x22, starting transfers between devices: 46 us -> 38.1 us  [move(): return lax.ppermute(array, AXES, pairs)]
    unnamed x16 -> x4, local copies, waits for them, and re-layouts: 6.45 us -> 0.01 us
    pallas_call x2, Pallas kernels: 6.71 us -> 9.71 us  [the longest x1 7.96 us: contribute(): pl.pallas_call(functools.partial(contribute_kernel, extents, capacity, bl...]
    ppermute x22, waiting for transfers between devices: 21.1 us -> 22.9 us  [move(): return lax.ppermute(array, AXES, pairs)]
  transfers between devices with their start and end apart: 22 -> 22, of which waited for: 9 -> 10; matrix products, arithmetic and copies ran while one was open for 0% -> 0% of each run, Pallas kernels for 0% -> 0%
where the time goes in v2:
time: 74.1 us; the launch traced here: 73.9 us
  starting transfers between devices  38.1 us (51%)
  waiting for transfers between devices  22.9 us (31%)
  Pallas kernels  11.4 us (15%)
  other arithmetic  0.75 us (1%)
    ppermute x22, starting transfers between devices, move(): return lax.ppermute(array, AXES, pairs)  38.1 us
    ppermute x22, waiting for transfers between devices, move(): return lax.ppermute(array, AXES, pairs)  22.9 us
    pallas_call x1, Pallas kernels, contribute(): pl.pallas_call(functools.partial(contribute_kernel, extents, capacity, bl...  7.96 us
    pallas_call x1, Pallas kernels, collect(): pl.pallas_call(functools.partial(collect_kernel, capacity, patches, block...  1.75 us
  transfers between devices with their start and end apart: 22, of which 10 were waited for; matrix products, arithmetic and copies ran while one was open for 0% of the time, Pallas kernels for 0%

profile of v2, /device:TPU:1, one launch (start us, length us, event | category | flops | bytes accessed | tf_op | source)
XLA Modules:
  0.0 73.9 jit_solution(9481388056914819138)
XLA Ops:
  0.6 0.7 multiply_add_fusion.key_hbm
  1.3 8.0 %shard_map.68 = (f32[6,64,128]{2,1,0:T(8,128)S(1)}, f32[6,64,128]{2,1,0:T(8,128)S(1)}, f32[6,64,128]{2,1,0:T(8,128)S(1)}, f32[6,64,128]{2,1,0:T(8,128)S(1)}, f32...) custom-call(s32[4,9]{1,0:T(4,128)S(1)} %multiply_add_fusion.key_hbm,, ...), custom_call_target="tpu_custom_call" | custom-call | tf_op jit(solution)/shard_map/pallas_call | solution.py:95
  9.3 1.5 %collective-permute-start = (f32[6,64,128]{2,1,0:T(8,128)S(1)}, f32[6,64,128]{2,1,0:T(8,128)S(1)}, u32[]{:S(2)}, u32[]{:S(2)}) collective-permute-start(f32[6,64,128]{2,1,0:T(8,128)S(1)} %get-tuple-element.26), channel_id=1, source_target_pairs={{0,4},{1,5},{2,6},{3,7},{4,0},{5,1},{6,2},{7,3},{8,12},{9,13},{10,... | collective-permute-start | bytes 589832 | tf_op jit(solution)/shard_map/ppermute | solution.py:203
  10.8 1.3 %collective-permute-start.3 = (f32[6,64,128]{2,1,0:T(8,128)S(1)}, f32[6,64,128]{2,1,0:T(8,128)S(1)}, u32[]{:S(2)}, u32[]{:S(2)}) collective-permute-start(f32[6,64,128]{2,1,0:T(8,128)S(1)} %get-tuple-element.28), channel_id=1, source_target_pairs={{0,32},{1,33},{2,34},{3,35},{4,36},{5,37},{6,38},{7,39},{8,40},{9,... | collective-permute-start | bytes 589832 | tf_op jit(solution)/shard_map/ppermute | solution.py:203
  12.1 1.4 %collective-permute-start.4 = (f32[6,64,128]{2,1,0:T(8,128)S(1)}, f32[6,64,128]{2,1,0:T(8,128)S(1)}, u32[]{:S(2)}, u32[]{:S(2)}) collective-permute-start(f32[6,64,128]{2,1,0:T(8,128)S(1)} %get-tuple-element.29), channel_id=1, source_target_pairs={{0,96},{1,97},{2,98},{3,99},{4,100},{5,101},{6,102},{7,103},{8,104... | collective-permute-start | bytes 589832 | tf_op jit(solution)/shard_map/ppermute | solution.py:203
  13.5 1.6 %collective-permute-start.5 = (f32[6,64,128]{2,1,0:T(8,128)S(1)}, f32[6,64,128]{2,1,0:T(8,128)S(1)}, u32[]{:S(2)}, u32[]{:S(2)}) collective-permute-start(f32[6,64,128]{2,1,0:T(8,128)S(1)} %get-tuple-element.30), channel_id=1, source_target_pairs={{0,60},{1,61},{2,62},{3,63},{4,40},{5,41},{6,42},{7,43},{8,36},{9,... | collective-permute-start | bytes 589832 | tf_op jit(solution)/shard_map/ppermute | solution.py:203
  15.1 2.2 %collective-permute-start.6 = (f32[6,64,128]{2,1,0:T(8,128)S(1)}, f32[6,64,128]{2,1,0:T(8,128)S(1)}, u32[]{:S(2)}, u32[]{:S(2)}) collective-permute-start(f32[6,64,128]{2,1,0:T(8,128)S(1)} %get-tuple-element.31), channel_id=1, source_target_pairs={{0,124},{1,125},{2,126},{3,127},{4,104},{5,105},{6,106},{7,107},{8... | collective-permute-start | bytes 589832 | tf_op jit(solution)/shard_map/ppermute | solution.py:203
  17.4 1.9 %collective-permute-start.7 = (f32[6,64,128]{2,1,0:T(8,128)S(1)}, f32[6,64,128]{2,1,0:T(8,128)S(1)}, u32[]{:S(2)}, u32[]{:S(2)}) collective-permute-start(f32[6,64,128]{2,1,0:T(8,128)S(1)} %get-tuple-element.32), channel_id=1, source_target_pairs={{0,28},{1,29},{2,30},{3,31},{4,8},{5,9},{6,10},{7,11},{8,4},{9,5},... | collective-permute-start | bytes 589832 | tf_op jit(solution)/shard_map/ppermute | solution.py:203
  19.3 1.2 %collective-permute-start.8 = (f32[6,64,128]{2,1,0:T(8,128)S(1)}, f32[6,64,128]{2,1,0:T(8,128)S(1)}, u32[]{:S(2)}, u32[]{:S(2)}) collective-permute-start(f32[6,64,128]{2,1,0:T(8,128)S(1)} %get-tuple-element.33), channel_id=1, source_target_pairs={{0,36},{1,37},{2,38},{3,39},{4,32},{5,33},{6,34},{7,35},{8,44},{9,... | collective-permute-start | bytes 589832 | tf_op jit(solution)/shard_map/ppermute | solution.py:203
  20.5 1.7 %collective-permute-start.9 = (f32[6,64,128]{2,1,0:T(8,128)S(1)}, f32[6,64,128]{2,1,0:T(8,128)S(1)}, u32[]{:S(2)}, u32[]{:S(2)}) collective-permute-start(f32[6,64,128]{2,1,0:T(8,128)S(1)} %get-tuple-element.34), channel_id=1, source_target_pairs={{0,100},{1,101},{2,102},{3,103},{4,96},{5,97},{6,98},{7,99},{8,108... | collective-permute-start | bytes 589832 | tf_op jit(solution)/shard_map/ppermute | solution.py:203
  22.2 2.0 %collective-permute-done.5.refs_5_ = f32[6,64,128]{2,1,0:T(8,128)S(1)} collective-permute-done((f32[6,64,128]{2,1,0:T(8,128)S(1)}, f32[6,64,128]{2,1,0:T(8,128)S(1)}, u32[]{:S(2)}, u32[]{:S(2)}) %collective-permute-start.5) | collective-permute-done | bytes 196640 | tf_op jit(solution)/shard_map/ppermute | solution.py:203
  24.2 3.8 %collective-permute-start.2 = (s32[2,27]{1,0:T(2,128)S(1)}, s32[2,27]{1,0:T(2,128)S(1)}, u32[]{:S(2)}, u32[]{:S(2)}) collective-permute-start(s32[2,27]{1,0:T(2,128)S(1)} %bitcast.3), channel_id=1, source_target_pairs={{0,3},{1,0},{2,1},{3,2},{4,7},{5,4},{6,5},{7,6},{8,11},{9,8},{10,9... | collective-permute-start | bytes 656 | tf_op jit(solution)/shard_map/ppermute | solution.py:203
  28.0 0.7 collective-permute-done.2.refs_2_
  28.7 2.9 %collective-permute-done.1.refs_0_ = s32[2,27]{1,0:T(2,128)S(1)} collective-permute-done((s32[2,27]{1,0:T(2,128)S(1)}, s32[2,27]{1,0:T(2,128)S(1)}, u32[]{:S(2)}, u32[]{:S(2)}) %collective-permute-start.1) | collective-permute-done | bytes 248 | tf_op jit(solution)/shard_map/ppermute | solution.py:203
  31.6 1.0 %shard_map.69 = (f32[8,64,128]{2,1,0:T(8,128)S(1)}, f32[8,64,128]{2,1,0:T(8,128)S(1)}, f32[8,64,128]{2,1,0:T(8,128)S(1)}) custom-call(s32[2,27]{1,0:T(2,128)S(1)} %collective-permute-done.1.refs_0_, s32[2,27]{1,0:T(2,128)S(1)} %bitcast.5, s32[2,27]{1,0:T(2,128)S(1)} %collective-permute-done.2.refs_2_, f32[6,64,128]{2,1,0:T(8,128)S(1)} %collective-permute-done.3.refs_3_, ...), custom_call_target="tpu_custom_call" | custom-call | tf_op jit(solution)/shard_map/pallas_call | solution.py:137
  32.6 0.1 collective-permute-start.10
  32.7 2.7 %collective-permute-start.11 = (f32[8,64,128]{2,1,0:T(8,128)S(1)}, f32[8,64,128]{2,1,0:T(8,128)S(1)}, u32[]{:S(2)}, u32[]{:S(2)}) collective-permute-start(f32[8,64,128]{2,1,0:T(8,128)S(1)} %get-tuple-element.39), channel_id=1, source_target_pairs={{0,3},{1,0},{2,1},{3,2},{4,7},{5,4},{6,5},{7,6},{8,11},{9,8},{10,9... | collective-permute-start | bytes 786440 | tf_op jit(solution)/shard_map/ppermute | solution.py:203
  35.4 3.8 %collective-permute-done.10 = f32[8,64,128]{2,1,0:T(8,128)S(1)} collective-permute-done((f32[8,64,128]{2,1,0:T(8,128)S(1)}, f32[8,64,128]{2,1,0:T(8,128)S(1)}, u32[]{:S(2)}, u32[]{:S(2)}) %collective-permute-start.10) | collective-permute-done | bytes 262176 | tf_op jit(solution)/shard_map/ppermute | solution.py:203
  39.2 2.7 %collective-permute-start.13 = (f32[8,64,128]{2,1,0:T(8,128)S(1)}, f32[8,64,128]{2,1,0:T(8,128)S(1)}, u32[]{:S(2)}, u32[]{:S(2)}) collective-permute-start(f32[8,64,128]{2,1,0:T(8,128)S(1)} %add_add_fusion.refs_4_), channel_id=1, source_target_pairs={{0,3},{1,0},{2,1},{3,2},{4,7},{5,4},{6,5},{7,6},{8,11},{9,8},{10,9... | collective-permute-start | bytes 786440 | tf_op jit(solution)/shard_map/ppermute | solution.py:203
  41.9 3.3 %collective-permute-done.13.refs_5_ = f32[8,64,128]{2,1,0:T(8,128)S(1)} collective-permute-done((f32[8,64,128]{2,1,0:T(8,128)S(1)}, f32[8,64,128]{2,1,0:T(8,128)S(1)}, u32[]{:S(2)}, u32[]{:S(2)}) %collective-permute-start.13) | collective-permute-done | bytes 262176 | tf_op jit(solution)/shard_map/ppermute | solution.py:203
  45.2 3.1 %collective-permute-done.12.refs_3_ = f32[8,64,128]{2,1,0:T(8,128)S(1)} collective-permute-done((f32[8,64,128]{2,1,0:T(8,128)S(1)}, f32[8,64,128]{2,1,0:T(8,128)S(1)}, u32[]{:S(2)}, u32[]{:S(2)}) %collective-permute-start.12) | collective-permute-done | bytes 262176 | tf_op jit(solution)/shard_map/ppermute | solution.py:203
  48.4 0.7 shard_map.70
  49.1 1.9 %collective-permute-start.14 = (f32[6,64,128]{2,1,0:T(8,128)S(1)}, f32[6,64,128]{2,1,0:T(8,128)S(1)}, u32[]{:S(2)}, u32[]{:S(2)}) collective-permute-start(f32[6,64,128]{2,1,0:T(8,128)S(1)} %get-tuple-element.41), channel_id=1, source_target_pairs={{0,96},{1,97},{2,98},{3,99},{4,100},{5,101},{6,102},{7,103},{8,104... | collective-permute-start | bytes 589832 | tf_op jit(solution)/shard_map/ppermute | solution.py:203
  50.9 9.0 %collective-permute-start.16 = (f32[6,64,128]{2,1,0:T(8,128)S(1)}, f32[6,64,128]{2,1,0:T(8,128)S(1)}, u32[]{:S(2)}, u32[]{:S(2)}) collective-permute-start(f32[6,64,128]{2,1,0:T(8,128)S(1)} %get-tuple-element.43), channel_id=1, source_target_pairs={{0,124},{1,125},{2,126},{3,127},{4,104},{5,105},{6,106},{7,107},{8... | collective-permute-start | bytes 589832 | tf_op jit(solution)/shard_map/ppermute | solution.py:203
  59.9 1.3 %collective-permute-start.18 = (f32[6,64,128]{2,1,0:T(8,128)S(1)}, f32[6,64,128]{2,1,0:T(8,128)S(1)}, u32[]{:S(2)}, u32[]{:S(2)}) collective-permute-start(f32[6,64,128]{2,1,0:T(8,128)S(1)} %get-tuple-element.45), channel_id=1, source_target_pairs={{0,28},{1,29},{2,30},{3,31},{4,8},{5,9},{6,10},{7,11},{8,4},{9,5},... | collective-permute-start | bytes 589832 | tf_op jit(solution)/shard_map/ppermute | solution.py:203
  61.2 3.2 %collective-permute-start.19 = (f32[6,64,128]{2,1,0:T(8,128)S(1)}, f32[6,64,128]{2,1,0:T(8,128)S(1)}, u32[]{:S(2)}, u32[]{:S(2)}) collective-permute-start(f32[6,64,128]{2,1,0:T(8,128)S(1)} %get-tuple-element.46), channel_id=1, source_target_pairs={{0,100},{1,101},{2,102},{3,103},{4,96},{5,97},{6,98},{7,99},{8,108... | collective-permute-start | bytes 589832 | tf_op jit(solution)/shard_map/ppermute | solution.py:203
  64.5 1.9 %collective-permute-done.16.refs_2_ = f32[6,64,128]{2,1,0:T(8,128)S(1)} collective-permute-done((f32[6,64,128]{2,1,0:T(8,128)S(1)}, f32[6,64,128]{2,1,0:T(8,128)S(1)}, u32[]{:S(2)}, u32[]{:S(2)}) %collective-permute-start.16) | collective-permute-done | bytes 196640 | tf_op jit(solution)/shard_map/ppermute | solution.py:203
  66.4 0.6 collective-permute-start.21
  67.0 0.8 %collective-permute-done.17.refs_3_ = f32[6,64,128]{2,1,0:T(8,128)S(1)} collective-permute-done((f32[6,64,128]{2,1,0:T(8,128)S(1)}, f32[6,64,128]{2,1,0:T(8,128)S(1)}, u32[]{:S(2)}, u32[]{:S(2)}) %collective-permute-start.17) | collective-permute-done | bytes 196640 | tf_op jit(solution)/shard_map/ppermute | solution.py:203
  67.8 1.2 %collective-permute-done.18.refs_4_ = f32[6,64,128]{2,1,0:T(8,128)S(1)} collective-permute-done((f32[6,64,128]{2,1,0:T(8,128)S(1)}, f32[6,64,128]{2,1,0:T(8,128)S(1)}, u32[]{:S(2)}, u32[]{:S(2)}) %collective-permute-start.18) | collective-permute-done | bytes 196640 | tf_op jit(solution)/shard_map/ppermute | solution.py:203
  69.0 3.2 %collective-permute-done.20.refs_6_ = f32[6,64,128]{2,1,0:T(8,128)S(1)} collective-permute-done((f32[6,64,128]{2,1,0:T(8,128)S(1)}, f32[6,64,128]{2,1,0:T(8,128)S(1)}, u32[]{:S(2)}, u32[]{:S(2)}) %collective-permute-start.20) | collective-permute-done | bytes 196640 | tf_op jit(solution)/shard_map/ppermute | solution.py:203
  72.2 1.8 %shard_map.71 = f32[4,9,64,128]{3,2,1,0:T(8,128)} custom-call(s32[54]{0:T(128)S(1)} %get-tuple-element.40.back, f32[6,64,128]{2,1,0:T(8,128)S(1)} %collective-permute-done.14.refs_0_, f32[6,64,128]{2,1,0:T(8,128)S(1)} %collective-permute-done.15.refs_1_, f32[6,64,128]{2,1,0:T(8,128)S(1)} %collective-permute-done.16.refs_2_, ...), custom_call_target="tpu_custom_call" | custom-call | tf_op jit(solution)/shard_map/pallas_call | solution.py:183
  (22 shorter events, 0.1 us)
Async XLA Ops:
  0.6 23.6 %copy-start.1 = (s32[1,27,2]{1,2,0:T(2,128)S(1)}, s32[1,27,2]{1,2,0:T(2,128)}, u32[]{:S(2)}) copy-start(s32[1,27,2]{1,2,0:T(2,128)} %param.9) | copy-start | bytes 652
  9.3 8.1 %collective-permute-start = (f32[6,64,128]{2,1,0:T(8,128)S(1)}, f32[6,64,128]{2,1,0:T(8,128)S(1)}, u32[]{:S(2)}, u32[]{:S(2)}) collective-permute-start(f32[6,64,128]{2,1,0:T(8,128)S(1)} %get-tuple-element.26), channel_id=1, source_target_pairs={{0,4},{1,5},{2,6},{3,7},{4,0},{5,1},{6,2},{7,3},{8,12},{9,13},{10,... | collective-permute-start | bytes 589832 | tf_op jit(solution)/shard_map/ppermute | solution.py:203
  10.8 8.4 %collective-permute-start.3 = (f32[6,64,128]{2,1,0:T(8,128)S(1)}, f32[6,64,128]{2,1,0:T(8,128)S(1)}, u32[]{:S(2)}, u32[]{:S(2)}) collective-permute-start(f32[6,64,128]{2,1,0:T(8,128)S(1)} %get-tuple-element.28), channel_id=1, source_target_pairs={{0,32},{1,33},{2,34},{3,35},{4,36},{5,37},{6,38},{7,39},{8,40},{9,... | collective-permute-start | bytes 589832 | tf_op jit(solution)/shard_map/ppermute | solution.py:203
  12.1 8.4 %collective-permute-start.4 = (f32[6,64,128]{2,1,0:T(8,128)S(1)}, f32[6,64,128]{2,1,0:T(8,128)S(1)}, u32[]{:S(2)}, u32[]{:S(2)}) collective-permute-start(f32[6,64,128]{2,1,0:T(8,128)S(1)} %get-tuple-element.29), channel_id=1, source_target_pairs={{0,96},{1,97},{2,98},{3,99},{4,100},{5,101},{6,102},{7,103},{8,104... | collective-permute-start | bytes 589832 | tf_op jit(solution)/shard_map/ppermute | solution.py:203
  13.5 10.7 %collective-permute-start.5 = (f32[6,64,128]{2,1,0:T(8,128)S(1)}, f32[6,64,128]{2,1,0:T(8,128)S(1)}, u32[]{:S(2)}, u32[]{:S(2)}) collective-permute-start(f32[6,64,128]{2,1,0:T(8,128)S(1)} %get-tuple-element.30), channel_id=1, source_target_pairs={{0,60},{1,61},{2,62},{3,63},{4,40},{5,41},{6,42},{7,43},{8,36},{9,... | collective-permute-start | bytes 589832 | tf_op jit(solution)/shard_map/ppermute | solution.py:203
  15.1 12.9 %collective-permute-start.6 = (f32[6,64,128]{2,1,0:T(8,128)S(1)}, f32[6,64,128]{2,1,0:T(8,128)S(1)}, u32[]{:S(2)}, u32[]{:S(2)}) collective-permute-start(f32[6,64,128]{2,1,0:T(8,128)S(1)} %get-tuple-element.31), channel_id=1, source_target_pairs={{0,124},{1,125},{2,126},{3,127},{4,104},{5,105},{6,106},{7,107},{8... | collective-permute-start | bytes 589832 | tf_op jit(solution)/shard_map/ppermute | solution.py:203
  17.4 10.6 %collective-permute-start.7 = (f32[6,64,128]{2,1,0:T(8,128)S(1)}, f32[6,64,128]{2,1,0:T(8,128)S(1)}, u32[]{:S(2)}, u32[]{:S(2)}) collective-permute-start(f32[6,64,128]{2,1,0:T(8,128)S(1)} %get-tuple-element.32), channel_id=1, source_target_pairs={{0,28},{1,29},{2,30},{3,31},{4,8},{5,9},{6,10},{7,11},{8,4},{9,5},... | collective-permute-start | bytes 589832 | tf_op jit(solution)/shard_map/ppermute | solution.py:203
  19.3 8.7 %collective-permute-start.8 = (f32[6,64,128]{2,1,0:T(8,128)S(1)}, f32[6,64,128]{2,1,0:T(8,128)S(1)}, u32[]{:S(2)}, u32[]{:S(2)}) collective-permute-start(f32[6,64,128]{2,1,0:T(8,128)S(1)} %get-tuple-element.33), channel_id=1, source_target_pairs={{0,36},{1,37},{2,38},{3,39},{4,32},{5,33},{6,34},{7,35},{8,44},{9,... | collective-permute-start | bytes 589832 | tf_op jit(solution)/shard_map/ppermute | solution.py:203
  20.5 7.5 %collective-permute-start.9 = (f32[6,64,128]{2,1,0:T(8,128)S(1)}, f32[6,64,128]{2,1,0:T(8,128)S(1)}, u32[]{:S(2)}, u32[]{:S(2)}) collective-permute-start(f32[6,64,128]{2,1,0:T(8,128)S(1)} %get-tuple-element.34), channel_id=1, source_target_pairs={{0,100},{1,101},{2,102},{3,103},{4,96},{5,97},{6,98},{7,99},{8,108... | collective-permute-start | bytes 589832 | tf_op jit(solution)/shard_map/ppermute | solution.py:203
  24.2 4.5 %collective-permute-start.2 = (s32[2,27]{1,0:T(2,128)S(1)}, s32[2,27]{1,0:T(2,128)S(1)}, u32[]{:S(2)}, u32[]{:S(2)}) collective-permute-start(s32[2,27]{1,0:T(2,128)S(1)} %bitcast.3), channel_id=1, source_target_pairs={{0,3},{1,0},{2,1},{3,2},{4,7},{5,4},{6,5},{7,6},{8,11},{9,8},{10,9... | collective-permute-start | bytes 656 | tf_op jit(solution)/shard_map/ppermute | solution.py:203
  28.0 3.6 %collective-permute-start.1 = (s32[2,27]{1,0:T(2,128)S(1)}, s32[2,27]{1,0:T(2,128)S(1)}, u32[]{:S(2)}, u32[]{:S(2)}) collective-permute-start(s32[2,27]{1,0:T(2,128)S(1)} %bitcast.4), channel_id=1, source_target_pairs={{0,1},{1,2},{2,3},{3,0},{4,5},{5,6},{6,7},{7,4},{8,9},{9,10},{10,1... | collective-permute-start | bytes 656 | tf_op jit(solution)/shard_map/ppermute | solution.py:203
  32.6 6.5 %collective-permute-start.10 = (f32[8,64,128]{2,1,0:T(8,128)S(1)}, f32[8,64,128]{2,1,0:T(8,128)S(1)}, u32[]{:S(2)}, u32[]{:S(2)}) collective-permute-start(f32[8,64,128]{2,1,0:T(8,128)S(1)} %get-tuple-element.38), channel_id=1, source_target_pairs={{0,1},{1,2},{2,3},{3,0},{4,5},{5,6},{6,7},{7,4},{8,9},{9,10},{10,1... | collective-permute-start | bytes 786440 | tf_op jit(solution)/shard_map/ppermute | solution.py:203
  32.7 6.4 %collective-permute-start.11 = (f32[8,64,128]{2,1,0:T(8,128)S(1)}, f32[8,64,128]{2,1,0:T(8,128)S(1)}, u32[]{:S(2)}, u32[]{:S(2)}) collective-permute-start(f32[8,64,128]{2,1,0:T(8,128)S(1)} %get-tuple-element.39), channel_id=1, source_target_pairs={{0,3},{1,0},{2,1},{3,2},{4,7},{5,4},{6,5},{7,6},{8,11},{9,8},{10,9... | collective-permute-start | bytes 786440 | tf_op jit(solution)/shard_map/ppermute | solution.py:203
  39.2 34.8 %copy-start = (f32[8,64,128]{2,1,0:T(8,128)}, f32[8,64,128]{2,1,0:T(8,128)S(1)}, u32[]{:S(2)}) copy-start(f32[8,64,128]{2,1,0:T(8,128)S(1)} %add_add_fusion.refs_4_) | copy-start | bytes 786436
  39.2 6.1 %collective-permute-start.13 = (f32[8,64,128]{2,1,0:T(8,128)S(1)}, f32[8,64,128]{2,1,0:T(8,128)S(1)}, u32[]{:S(2)}, u32[]{:S(2)}) collective-permute-start(f32[8,64,128]{2,1,0:T(8,128)S(1)} %add_add_fusion.refs_4_), channel_id=1, source_target_pairs={{0,3},{1,0},{2,1},{3,2},{4,7},{5,4},{6,5},{7,6},{8,11},{9,8},{10,9... | collective-permute-start | bytes 786440 | tf_op jit(solution)/shard_map/ppermute | solution.py:203
  41.9 6.4 %collective-permute-start.12 = (f32[8,64,128]{2,1,0:T(8,128)S(1)}, f32[8,64,128]{2,1,0:T(8,128)S(1)}, u32[]{:S(2)}, u32[]{:S(2)}) collective-permute-start(f32[8,64,128]{2,1,0:T(8,128)S(1)} %add_add_fusion.refs_4_), channel_id=1, source_target_pairs={{0,1},{1,2},{2,3},{3,0},{4,5},{5,6},{6,7},{7,4},{8,9},{9,10},{10,1... | collective-permute-start | bytes 786440 | tf_op jit(solution)/shard_map/ppermute | solution.py:203
  49.1 12.1 %collective-permute-start.14 = (f32[6,64,128]{2,1,0:T(8,128)S(1)}, f32[6,64,128]{2,1,0:T(8,128)S(1)}, u32[]{:S(2)}, u32[]{:S(2)}) collective-permute-start(f32[6,64,128]{2,1,0:T(8,128)S(1)} %get-tuple-element.41), channel_id=1, source_target_pairs={{0,96},{1,97},{2,98},{3,99},{4,100},{5,101},{6,102},{7,103},{8,104... | collective-permute-start | bytes 589832 | tf_op jit(solution)/shard_map/ppermute | solution.py:203
  50.9 13.5 %collective-permute-start.15 = (f32[6,64,128]{2,1,0:T(8,128)S(1)}, f32[6,64,128]{2,1,0:T(8,128)S(1)}, u32[]{:S(2)}, u32[]{:S(2)}) collective-permute-start(f32[6,64,128]{2,1,0:T(8,128)S(1)} %get-tuple-element.42), channel_id=1, source_target_pairs={{0,32},{1,33},{2,34},{3,35},{4,36},{5,37},{6,38},{7,39},{8,40},{9,... | collective-permute-start | bytes 589832 | tf_op jit(solution)/shard_map/ppermute | solution.py:203
  50.9 15.4 %collective-permute-start.16 = (f32[6,64,128]{2,1,0:T(8,128)S(1)}, f32[6,64,128]{2,1,0:T(8,128)S(1)}, u32[]{:S(2)}, u32[]{:S(2)}) collective-permute-start(f32[6,64,128]{2,1,0:T(8,128)S(1)} %get-tuple-element.43), channel_id=1, source_target_pairs={{0,124},{1,125},{2,126},{3,127},{4,104},{5,105},{6,106},{7,107},{8... | collective-permute-start | bytes 589832 | tf_op jit(solution)/shard_map/ppermute | solution.py:203
  59.9 7.9 %collective-permute-start.17 = (f32[6,64,128]{2,1,0:T(8,128)S(1)}, f32[6,64,128]{2,1,0:T(8,128)S(1)}, u32[]{:S(2)}, u32[]{:S(2)}) collective-permute-start(f32[6,64,128]{2,1,0:T(8,128)S(1)} %get-tuple-element.44), channel_id=1, source_target_pairs={{0,60},{1,61},{2,62},{3,63},{4,40},{5,41},{6,42},{7,43},{8,36},{9,... | collective-permute-start | bytes 589832 | tf_op jit(solution)/shard_map/ppermute | solution.py:203
  59.9 9.1 %collective-permute-start.18 = (f32[6,64,128]{2,1,0:T(8,128)S(1)}, f32[6,64,128]{2,1,0:T(8,128)S(1)}, u32[]{:S(2)}, u32[]{:S(2)}) collective-permute-start(f32[6,64,128]{2,1,0:T(8,128)S(1)} %get-tuple-element.45), channel_id=1, source_target_pairs={{0,28},{1,29},{2,30},{3,31},{4,8},{5,9},{6,10},{7,11},{8,4},{9,5},... | collective-permute-start | bytes 589832 | tf_op jit(solution)/shard_map/ppermute | solution.py:203
  61.2 7.8 %collective-permute-start.19 = (f32[6,64,128]{2,1,0:T(8,128)S(1)}, f32[6,64,128]{2,1,0:T(8,128)S(1)}, u32[]{:S(2)}, u32[]{:S(2)}) collective-permute-start(f32[6,64,128]{2,1,0:T(8,128)S(1)} %get-tuple-element.46), channel_id=1, source_target_pairs={{0,100},{1,101},{2,102},{3,103},{4,96},{5,97},{6,98},{7,99},{8,108... | collective-permute-start | bytes 589832 | tf_op jit(solution)/shard_map/ppermute | solution.py:203
  64.5 7.7 %collective-permute-start.20 = (f32[6,64,128]{2,1,0:T(8,128)S(1)}, f32[6,64,128]{2,1,0:T(8,128)S(1)}, u32[]{:S(2)}, u32[]{:S(2)}) collective-permute-start(f32[6,64,128]{2,1,0:T(8,128)S(1)} %get-tuple-element.47), channel_id=1, source_target_pairs={{0,36},{1,37},{2,38},{3,39},{4,32},{5,33},{6,34},{7,35},{8,44},{9,... | collective-permute-start | bytes 589832 | tf_op jit(solution)/shard_map/ppermute | solution.py:203
  66.4 5.8 %collective-permute-start.21 = (f32[6,64,128]{2,1,0:T(8,128)S(1)}, f32[6,64,128]{2,1,0:T(8,128)S(1)}, u32[]{:S(2)}, u32[]{:S(2)}) collective-permute-start(f32[6,64,128]{2,1,0:T(8,128)S(1)} %get-tuple-element.48), channel_id=1, source_target_pairs={{0,4},{1,5},{2,6},{3,7},{4,0},{5,1},{6,2},{7,3},{8,12},{9,13},{10,... | collective-permute-start | bytes 589832 | tf_op jit(solution)/shard_map/ppermute | solution.py:203

commit v3 on v2

--- a/solution.py
+++ b/solution.py
@@ -12,8 +12,14 @@
 VMEM = pltpu.VMEM
 SMEM = pltpu.SMEM
 
+SIDE, LAST = 0, 2
 PLANE = [(1, 0), (-1, 0), (1, 2), (-1, 2), (0, 2), (1, 1), (-1, 1), (0, 1), (0, 0)]
 HOME = len(PLANE) - 1
+OUT_ORDER = list(range(8))
+BACK_ORDER = list(range(8))
+TABLE_AFTER = 7
+AHEAD = 2
+FIRST = 2
 
 
 def toward(y, way):
@@ -37,10 +43,12 @@
 
 def place(owner, slot, near, extents, capacity):
     size_x, size_y, size_z = extents
-    code_x = axis_code(lax.div(owner, size_y * size_z), near[0], size_x)
-    code_y = axis_code(lax.rem(lax.div(owner, size_z), size_y), near[1], size_y)
-    code_z = axis_code(lax.rem(owner, size_z), near[2], size_z)
-    return ((code_x * 3 + code_y) * 3 + code_z) * capacity + slot
+    code = [
+        axis_code(lax.div(owner, size_y * size_z), near[0], size_x),
+        axis_code(lax.rem(lax.div(owner, size_z), size_y), near[1], size_y),
+        axis_code(lax.rem(owner, size_z), near[2], size_z),
+    ]
+    return ((code[SIDE] * 3 + code[1]) * 3 + code[LAST]) * capacity + slot
 
 
 def contribute_kernel(extents, capacity, blocks, key_hbm, residual_hbm, inverse_hbm, *rest):
@@ -55,7 +63,7 @@
     ]
     key_copy.start()
     res_copy.start()
-    for copy in inv_copies:
+    for copy in inv_copies[:AHEAD]:
         copy.start()
 
     width = inverse.shape[1] // blocks
@@ -73,6 +81,8 @@
     res_copy.wait()
     for p in range(patches):
         inv_copies[p].wait()
+        if p + AHEAD < patches:
+            inv_copies[p + AHEAD].start()
         product = lax.dot_general(
             residual[p],
             inverse[p],
@@ -114,54 +124,57 @@
 def entry(tables, plane, cz, c, near_y):
     dx, way = PLANE[plane]
     code_y = 1 if way == 0 else 2 - way_code(way, near_y)
-    return tables[cz][c, 9 * (dx + 1) + 3 * code_y + cz]
-
-
-def gather_kernel(capacity, *refs):
-    tables, arrived = refs[0:3], refs[3:12]
-    outs, total = refs[12:15], refs[15]
+    code = 9 * (dx + 1) + cz if SIDE == 0 else (dx + 1) + 9 * cz
+    return tables[cz][c, code + 3 * code_y]
+
+
+def gather_kernel(capacity, codes, *refs):
+    count = len(codes)
+    tables, arrived = dict(zip(codes, refs[:count])), refs[count : count + 9]
+    outs, total = refs[count + 9 : -1], refs[-1]
     near_y = lax.axis_index("gy")
     total[...] = jnp.zeros_like(total)
     for i in range(9):
+        for n, cz in enumerate(codes):
+            for c in range(capacity):
+                t = entry(tables, i, cz, c, near_y)
+                t = jnp.where(t < 0, OWNB, t)
+                total[n, t] += arrived[i][cz * capacity + c]
+    for n in range(count):
+        outs[n][...] = total[n, :OWNB]
+
+
+def gather(tables, codes, arrived, capacity):
+    _, rhs, width = arrived[0].shape
+    return pl.pallas_call(
+        functools.partial(gather_kernel, capacity, codes),
+        in_specs=[pl.BlockSpec(memory_space=SMEM)] * len(codes)
+        + [pl.BlockSpec(memory_space=VMEM)] * 9,
+        out_specs=[pl.BlockSpec(memory_space=VMEM)] * len(codes),
+        out_shape=[jax.ShapeDtypeStruct((OWNB, rhs, width), jnp.float32)] * len(codes),
+        scratch_shapes=[VMEM((len(codes), OWNB + 1, rhs, width), jnp.float32)],
+        compiler_params=pltpu.CompilerParams(vmem_limit_bytes=32 * 2**20),
+    )(*[tables[cz] for cz in codes], *arrived)
+
+
+def answer_kernel(capacity, steps, *refs):
+    tables, totals, outs = refs[0:3], refs[3:6], refs[6:]
+    near_y = lax.axis_index("gy")
+    for out, i in zip(outs, steps):
         for cz in range(3):
             for c in range(capacity):
                 t = entry(tables, i, cz, c, near_y)
-                t = jnp.where(t < 0, OWNB, t)
-                total[cz, t] += arrived[i][cz * capacity + c]
-    for cz in range(3):
-        outs[cz][...] = total[cz, :OWNB]
-
-
-def gather(tables, arrived, capacity):
-    _, rhs, width = arrived[0].shape
-    return pl.pallas_call(
-        functools.partial(gather_kernel, capacity),
-        in_specs=[pl.BlockSpec(memory_space=SMEM)] * 3 + [pl.BlockSpec(memory_space=VMEM)] * 9,
-        out_specs=[pl.BlockSpec(memory_space=VMEM)] * 3,
-        out_shape=[jax.ShapeDtypeStruct((OWNB, rhs, width), jnp.float32)] * 3,
-        scratch_shapes=[VMEM((3, OWNB + 1, rhs, width), jnp.float32)],
-        compiler_params=pltpu.CompilerParams(vmem_limit_bytes=32 * 2**20),
-    )(*tables, *arrived)
-
-
-def answer_kernel(capacity, *refs):
-    tables, totals, outs = refs[0:3], refs[3:6], refs[6:15]
-    near_y = lax.axis_index("gy")
-    for i in range(9):
-        for cz in range(3):
-            for c in range(capacity):
-                t = entry(tables, i, cz, c, near_y)
-                outs[i][cz * capacity + c] = totals[cz][jnp.maximum(t, 0)]
-
-
-def answer(tables, totals, capacity):
+                out[cz * capacity + c] = totals[cz][jnp.maximum(t, 0)]
+
+
+def answer(tables, totals, steps, capacity):
     _, rhs, width = totals[0].shape
     per = 3 * capacity
     return pl.pallas_call(
-        functools.partial(answer_kernel, capacity),
+        functools.partial(answer_kernel, capacity, steps),
         in_specs=[pl.BlockSpec(memory_space=SMEM)] * 3 + [pl.BlockSpec(memory_space=VMEM)] * 3,
-        out_specs=[pl.BlockSpec(memory_space=VMEM)] * 9,
-        out_shape=[jax.ShapeDtypeStruct((per, rhs, width), jnp.float32)] * 9,
+        out_specs=[pl.BlockSpec(memory_space=VMEM)] * len(steps),
+        out_shape=[jax.ShapeDtypeStruct((per, rhs, width), jnp.float32)] * len(steps),
         compiler_params=pltpu.CompilerParams(vmem_limit_bytes=32 * 2**20),
     )(*tables, *totals)
 
@@ -190,13 +203,15 @@
     )(back, *returned)
 
 
-def move(array, extents, dx, way, dz):
+def move(array, extents, side, way, last):
+    by = [0, 0, 0]
+    by[SIDE], by[LAST] = side, last
     size_x, size_y, size_z = extents
     pairs = []
     for x in range(size_x):
         for y in range(size_y):
             for z in range(size_z):
-                to_x, to_y, to_z = (x + dx) % size_x, toward(y, way) % size_y, (z + dz) % size_z
+                to_x, to_y, to_z = (x + by[0]) % size_x, toward(y, way) % size_y, (z + by[2]) % size_z
                 pairs.append(
                     ((x * size_y + y) * size_z + z, (to_x * size_y + to_y) * size_z + to_z)
                 )
@@ -209,20 +224,27 @@
     table = jnp.swapaxes(recv_target, 1, 2)[0]
     key = block_owner * capacity + block_slot
     *outgoing, back = contribute(key, star_residual, patch_inverse, extents, capacity)
-    arrived = [
-        outgoing[i] if i == HOME else move(outgoing[i], extents, dx, way, 0)
-        for i, (dx, way) in enumerate(PLANE)
-    ]
-    table, arrived[7] = lax.optimization_barrier((table, arrived[7]))
+    arrived = [outgoing[HOME]] * 9
+    for i in OUT_ORDER:
+        arrived[i] = move(outgoing[i], extents, *PLANE[i], 0)
+    table, arrived[TABLE_AFTER] = lax.optimization_barrier((table, arrived[TABLE_AFTER]))
     tables = [move(table, extents, 0, 0, 1), table, move(table, extents, 0, 0, -1)]
-    below, own, above = gather(tables, arrived, capacity)
-    owned = own + move(above, extents, 0, 0, 1) + move(below, extents, 0, 0, -1)
-    totals = [move(owned, extents, 0, 0, 1), owned, move(owned, extents, 0, 0, -1)]
-    answers = answer(tables, totals, capacity)
-    returned = [
-        answers[i] if i == HOME else move(answers[i], extents, -dx, way, 0)
-        for i, (dx, way) in enumerate(PLANE)
-    ]
+    below, above = gather(tables, (0, 2), arrived, capacity)
+    (own,) = gather(tables, (1,), arrived, capacity)
+    from_below = move(above, extents, 0, 0, 1)
+    from_above = move(below, extents, 0, 0, -1)
+    rising = own + from_below
+    from_above, _ = lax.optimization_barrier((from_above, rising))
+    sinking = own + from_above
+    owned = rising + from_above
+    total_below = move(rising, extents, 0, 0, 1) + below
+    total_above = move(sinking, extents, 0, 0, -1) + above
+    totals = [total_below, owned, total_above]
+    answers = list(answer(tables, totals, tuple(range(FIRST)), capacity))
+    answers += answer(tables, totals, tuple(range(FIRST, 9)), capacity)
+    returned = [answers[HOME]] * 9
+    for i in BACK_ORDER:
+        returned[i] = move(answers[i], extents, -PLANE[i][0], PLANE[i][1], 0)
     combined = collect(back, returned, *block_owner.shape, capacity)
     return owned, combined
 

time: 74.1 us -> 70.6 us (0.953)
  waiting for transfers between devices: 22.9 us -> 19.7 us
    ppermute x22, waiting for transfers between devices: 22.9 us -> 19.7 us  [move(): return lax.ppermute(array, AXES, pairs)]
    pallas_call x1, Pallas kernels: 7.96 us -> 6.34 us  [contribute(): pl.pallas_call(functools.partial(contribute_kernel, extents, capacity, bl...]
    pallas_call x2 -> x4, Pallas kernels: 1.7 us -> 2.82 us  [the longest x2 1.52 us: gather(): pl.pallas_call(functools.partial(gather_kernel, capacity, codes), in_spec...]
  transfers between devices with their start and end apart: 22 -> 22, of which waited for: 10 -> 9; matrix products, arithmetic and copies ran while one was open for 0% -> 0% of each run, Pallas kernels for 0% -> 2%
where the time goes in v3:
time: 70.6 us; the launch traced here: 70.5 us
  starting transfers between devices  38.2 us (54%)
  waiting for transfers between devices  19.7 us (28%)
  Pallas kernels  10.9 us (15%)
  other arithmetic  0.86 us (1%)
  between operations  0.77 us (1%)
    ppermute x22, starting transfers between devices, move(): return lax.ppermute(array, AXES, pairs)  38.2 us
    ppermute x22, waiting for transfers between devices, move(): return lax.ppermute(array, AXES, pairs)  19.7 us
    pallas_call x1, Pallas kernels, contribute(): pl.pallas_call(functools.partial(contribute_kernel, extents, capacity, bl...  6.34 us
    pallas_call x1, Pallas kernels, collect(): pl.pallas_call(functools.partial(collect_kernel, capacity, patches, block...  1.75 us
    pallas_call x2, Pallas kernels, gather(): pl.pallas_call(functools.partial(gather_kernel, capacity, codes), in_spec...  1.52 us
  transfers between devices with their start and end apart: 22, of which 9 were waited for; matrix products, arithmetic and copies ran while one was open for 0% of the time, Pallas kernels for 2%

profile of v3, /device:TPU:1, one launch (start us, length us, event | category | flops | bytes accessed | tf_op | source)
XLA Modules:
  0.0 70.5 jit_solution(4749625545389068481)
XLA Ops:
  0.6 0.7 %multiply_add_fusion.key_hbm = s32[4,9]{1,0:T(4,128)S(1)} fusion(s32[4,9]{1,0:T(4,128)} %param.8, s32[4,9]{1,0:T(4,128)} %param.7), kind=kLoop, calls=%fused_computation | loop fusion | flops 72 | bytes 432 | tf_op jit(solution)/shard_map/add | solution.py:225
  1.3 6.3 %shard_map.68 = (f32[6,64,128]{2,1,0:T(8,128)S(1)}, f32[6,64,128]{2,1,0:T(8,128)S(1)}, f32[6,64,128]{2,1,0:T(8,128)S(1)}, f32[6,64,128]{2,1,0:T(8,128)S(1)}, f32...) custom-call(s32[4,9]{1,0:T(4,128)S(1)} %multiply_add_fusion.key_hbm,, ...), custom_call_target="tpu_custom_call" | custom-call | tf_op jit(solution)/shard_map/pallas_call | solution.py:105
  7.7 1.5 %collective-permute-start = (f32[6,64,128]{2,1,0:T(8,128)S(1)}, f32[6,64,128]{2,1,0:T(8,128)S(1)}, u32[]{:S(2)}, u32[]{:S(2)}) collective-permute-start(f32[6,64,128]{2,1,0:T(8,128)S(1)} %get-tuple-element.26), channel_id=1, source_target_pairs={{0,4},{1,5},{2,6},{3,7},{4,0},{5,1},{6,2},{7,3},{8,12},{9,13},{10,... | collective-permute-start | bytes 589832 | tf_op jit(solution)/shard_map/ppermute | solution.py:218
  9.2 1.3 %collective-permute-start.1 = (f32[6,64,128]{2,1,0:T(8,128)S(1)}, f32[6,64,128]{2,1,0:T(8,128)S(1)}, u32[]{:S(2)}, u32[]{:S(2)}) collective-permute-start(f32[6,64,128]{2,1,0:T(8,128)S(1)} %get-tuple-element.28), channel_id=1, source_target_pairs={{0,32},{1,33},{2,34},{3,35},{4,36},{5,37},{6,38},{7,39},{8,40},{9,... | collective-permute-start | bytes 589832 | tf_op jit(solution)/shard_map/ppermute | solution.py:218
  10.5 1.4 %collective-permute-start.2 = (f32[6,64,128]{2,1,0:T(8,128)S(1)}, f32[6,64,128]{2,1,0:T(8,128)S(1)}, u32[]{:S(2)}, u32[]{:S(2)}) collective-permute-start(f32[6,64,128]{2,1,0:T(8,128)S(1)} %get-tuple-element.29), channel_id=1, source_target_pairs={{0,96},{1,97},{2,98},{3,99},{4,100},{5,101},{6,102},{7,103},{8,104... | collective-permute-start | bytes 589832 | tf_op jit(solution)/shard_map/ppermute | solution.py:218
  11.9 1.6 %collective-permute-start.3 = (f32[6,64,128]{2,1,0:T(8,128)S(1)}, f32[6,64,128]{2,1,0:T(8,128)S(1)}, u32[]{:S(2)}, u32[]{:S(2)}) collective-permute-start(f32[6,64,128]{2,1,0:T(8,128)S(1)} %get-tuple-element.30), channel_id=1, source_target_pairs={{0,60},{1,61},{2,62},{3,63},{4,40},{5,41},{6,42},{7,43},{8,36},{9,... | collective-permute-start | bytes 589832 | tf_op jit(solution)/shard_map/ppermute | solution.py:218
  13.5 2.2 %collective-permute-start.4 = (f32[6,64,128]{2,1,0:T(8,128)S(1)}, f32[6,64,128]{2,1,0:T(8,128)S(1)}, u32[]{:S(2)}, u32[]{:S(2)}) collective-permute-start(f32[6,64,128]{2,1,0:T(8,128)S(1)} %get-tuple-element.31), channel_id=1, source_target_pairs={{0,124},{1,125},{2,126},{3,127},{4,104},{5,105},{6,106},{7,107},{8... | collective-permute-start | bytes 589832 | tf_op jit(solution)/shard_map/ppermute | solution.py:218
  15.7 1.9 %collective-permute-start.5 = (f32[6,64,128]{2,1,0:T(8,128)S(1)}, f32[6,64,128]{2,1,0:T(8,128)S(1)}, u32[]{:S(2)}, u32[]{:S(2)}) collective-permute-start(f32[6,64,128]{2,1,0:T(8,128)S(1)} %get-tuple-element.32), channel_id=1, source_target_pairs={{0,28},{1,29},{2,30},{3,31},{4,8},{5,9},{6,10},{7,11},{8,4},{9,5},... | collective-permute-start | bytes 589832 | tf_op jit(solution)/shard_map/ppermute | solution.py:218
  17.6 1.2 %collective-permute-start.6 = (f32[6,64,128]{2,1,0:T(8,128)S(1)}, f32[6,64,128]{2,1,0:T(8,128)S(1)}, u32[]{:S(2)}, u32[]{:S(2)}) collective-permute-start(f32[6,64,128]{2,1,0:T(8,128)S(1)} %get-tuple-element.33), channel_id=1, source_target_pairs={{0,36},{1,37},{2,38},{3,39},{4,32},{5,33},{6,34},{7,35},{8,44},{9,... | collective-permute-start | bytes 589832 | tf_op jit(solution)/shard_map/ppermute | solution.py:218
  18.9 1.8 %collective-permute-start.7 = (f32[6,64,128]{2,1,0:T(8,128)S(1)}, f32[6,64,128]{2,1,0:T(8,128)S(1)}, u32[]{:S(2)}, u32[]{:S(2)}) collective-permute-start(f32[6,64,128]{2,1,0:T(8,128)S(1)} %get-tuple-element.34), channel_id=1, source_target_pairs={{0,100},{1,101},{2,102},{3,103},{4,96},{5,97},{6,98},{7,99},{8,108... | collective-permute-start | bytes 589832 | tf_op jit(solution)/shard_map/ppermute | solution.py:218
  20.6 2.0 %collective-permute-done.3.refs_3_.refs_4_ = f32[6,64,128]{2,1,0:T(8,128)S(1)} collective-permute-done((f32[6,64,128]{2,1,0:T(8,128)S(1)}, f32[6,64,128]{2,1,0:T(8,128)S(1)}, u32[]{:S(2)}, u32[]{:S(2)}) %collective-permute-start.3) | collective-permute-done | bytes 196640 | tf_op jit(solution)/shard_map/ppermute | solution.py:218
  22.6 3.7 %collective-permute-start.9 = (s32[2,27]{1,0:T(2,128)S(1)}, s32[2,27]{1,0:T(2,128)S(1)}, u32[]{:S(2)}, u32[]{:S(2)}) collective-permute-start(s32[2,27]{1,0:T(2,128)S(1)} %bitcast.3), channel_id=1, source_target_pairs={{0,3},{1,0},{2,1},{3,2},{4,7},{5,4},{6,5},{7,6},{8,11},{9,8},{10,9... | collective-permute-start | bytes 656 | tf_op jit(solution)/shard_map/ppermute | solution.py:218
  26.4 0.7 collective-permute-done.9.refs_1_.refs_2_
  27.1 2.9 %collective-permute-done.8.refs_0_ = s32[2,27]{1,0:T(2,128)S(1)} collective-permute-done((s32[2,27]{1,0:T(2,128)S(1)}, s32[2,27]{1,0:T(2,128)S(1)}, u32[]{:S(2)}, u32[]{:S(2)}) %collective-permute-start.8) | collective-permute-done | bytes 248 | tf_op jit(solution)/shard_map/ppermute | solution.py:218
  30.0 0.8 %shard_map.70 = (f32[8,64,128]{2,1,0:T(8,128)S(1)}, f32[8,64,128]{2,1,0:T(8,128)S(1)}) custom-call(s32[2,27]{1,0:T(2,128)S(1)} %collective-permute-done.8.refs_0_, s32[2,27]{1,0:T(2,128)S(1)} %collective-permute-done.9.refs_1_.refs_2_, f32[6,64,128]{2,1,0:T(8,128)S(1)} %collective-permute-done.1.refs_1_.refs_2_, ...), custom_call_target="tpu_custom_call" | custom-call | tf_op jit(solution)/shard_map/pallas_call | solution.py:149
  30.9 2.7 %collective-permute-start.11 = (f32[8,64,128]{2,1,0:T(8,128)S(1)}, f32[8,64,128]{2,1,0:T(8,128)S(1)}, u32[]{:S(2)}, u32[]{:S(2)}) collective-permute-start(f32[8,64,128]{2,1,0:T(8,128)S(1)} %get-tuple-element.38), channel_id=1, source_target_pairs={{0,3},{1,0},{2,1},{3,2},{4,7},{5,4},{6,5},{7,6},{8,11},{9,8},{10,9... | collective-permute-start | bytes 786440 | tf_op jit(solution)/shard_map/ppermute | solution.py:218
  33.6 0.7 shard_map.69
  34.3 3.1 %collective-permute-done.10 = f32[8,64,128]{2,1,0:T(8,128)S(1)} collective-permute-done((f32[8,64,128]{2,1,0:T(8,128)S(1)}, f32[8,64,128]{2,1,0:T(8,128)S(1)}, u32[]{:S(2)}, u32[]{:S(2)}) %collective-permute-start.10) | collective-permute-done | bytes 262176 | tf_op jit(solution)/shard_map/ppermute | solution.py:218
  37.5 2.7 %collective-permute-start.13 = (f32[8,64,128]{2,1,0:T(8,128)S(1)}, f32[8,64,128]{2,1,0:T(8,128)S(1)}, u32[]{:S(2)}, u32[]{:S(2)}) collective-permute-start(f32[8,64,128]{2,1,0:T(8,128)S(1)} %get-tuple-element.50), channel_id=1, source_target_pairs={{0,3},{1,0},{2,1},{3,2},{4,7},{5,4},{6,5},{7,6},{8,11},{9,8},{10,9... | collective-permute-start | bytes 786440 | tf_op jit(solution)/shard_map/ppermute | solution.py:218
  40.3 3.6 %collective-permute-done.12 = f32[8,64,128]{2,1,0:T(8,128)S(1)} collective-permute-done((f32[8,64,128]{2,1,0:T(8,128)S(1)}, f32[8,64,128]{2,1,0:T(8,128)S(1)}, u32[]{:S(2)}, u32[]{:S(2)}) %collective-permute-start.12) | collective-permute-done | bytes 262176 | tf_op jit(solution)/shard_map/ppermute | solution.py:218
  44.0 0.6 shard_map.71
  44.6 1.9 %collective-permute-start.14 = (f32[6,64,128]{2,1,0:T(8,128)S(1)}, f32[6,64,128]{2,1,0:T(8,128)S(1)}, u32[]{:S(2)}, u32[]{:S(2)}) collective-permute-start(f32[6,64,128]{2,1,0:T(8,128)S(1)} %get-tuple-element.41), channel_id=1, source_target_pairs={{0,96},{1,97},{2,98},{3,99},{4,100},{5,101},{6,102},{7,103},{8,104... | collective-permute-start | bytes 589832 | tf_op jit(solution)/shard_map/ppermute | solution.py:218
  46.4 0.7 shard_map.72
  47.1 9.4 %collective-permute-start.16 = (f32[6,64,128]{2,1,0:T(8,128)S(1)}, f32[6,64,128]{2,1,0:T(8,128)S(1)}, u32[]{:S(2)}, u32[]{:S(2)}) collective-permute-start(f32[6,64,128]{2,1,0:T(8,128)S(1)} %get-tuple-element.43), channel_id=1, source_target_pairs={{0,124},{1,125},{2,126},{3,127},{4,104},{5,105},{6,106},{7,107},{8... | collective-permute-start | bytes 589832 | tf_op jit(solution)/shard_map/ppermute | solution.py:218
  56.5 1.3 %collective-permute-start.18 = (f32[6,64,128]{2,1,0:T(8,128)S(1)}, f32[6,64,128]{2,1,0:T(8,128)S(1)}, u32[]{:S(2)}, u32[]{:S(2)}) collective-permute-start(f32[6,64,128]{2,1,0:T(8,128)S(1)} %get-tuple-element.45), channel_id=1, source_target_pairs={{0,28},{1,29},{2,30},{3,31},{4,8},{5,9},{6,10},{7,11},{8,4},{9,5},... | collective-permute-start | bytes 589832 | tf_op jit(solution)/shard_map/ppermute | solution.py:218
  57.8 2.4 %collective-permute-start.19 = (f32[6,64,128]{2,1,0:T(8,128)S(1)}, f32[6,64,128]{2,1,0:T(8,128)S(1)}, u32[]{:S(2)}, u32[]{:S(2)}) collective-permute-start(f32[6,64,128]{2,1,0:T(8,128)S(1)} %get-tuple-element.46), channel_id=1, source_target_pairs={{0,100},{1,101},{2,102},{3,103},{4,96},{5,97},{6,98},{7,99},{8,108... | collective-permute-start | bytes 589832 | tf_op jit(solution)/shard_map/ppermute | solution.py:218
  60.2 1.4 %collective-permute-done.16.refs_2_ = f32[6,64,128]{2,1,0:T(8,128)S(1)} collective-permute-done((f32[6,64,128]{2,1,0:T(8,128)S(1)}, f32[6,64,128]{2,1,0:T(8,128)S(1)}, u32[]{:S(2)}, u32[]{:S(2)}) %collective-permute-start.16) | collective-permute-done | bytes 196640 | tf_op jit(solution)/shard_map/ppermute | solution.py:218
  61.6 1.2 %collective-permute-start.21 = (f32[6,64,128]{2,1,0:T(8,128)S(1)}, f32[6,64,128]{2,1,0:T(8,128)S(1)}, u32[]{:S(2)}, u32[]{:S(2)}) collective-permute-start(f32[6,64,128]{2,1,0:T(8,128)S(1)} %get-tuple-element.48), channel_id=1, source_target_pairs={{0,4},{1,5},{2,6},{3,7},{4,0},{5,1},{6,2},{7,3},{8,12},{9,13},{10,... | collective-permute-start | bytes 589832 | tf_op jit(solution)/shard_map/ppermute | solution.py:218
  62.8 1.0 %collective-permute-done.17.refs_3_ = f32[6,64,128]{2,1,0:T(8,128)S(1)} collective-permute-done((f32[6,64,128]{2,1,0:T(8,128)S(1)}, f32[6,64,128]{2,1,0:T(8,128)S(1)}, u32[]{:S(2)}, u32[]{:S(2)}) %collective-permute-start.17) | collective-permute-done | bytes 196640 | tf_op jit(solution)/shard_map/ppermute | solution.py:218
  63.8 1.1 %collective-permute-done.18.refs_4_ = f32[6,64,128]{2,1,0:T(8,128)S(1)} collective-permute-done((f32[6,64,128]{2,1,0:T(8,128)S(1)}, f32[6,64,128]{2,1,0:T(8,128)S(1)}, u32[]{:S(2)}, u32[]{:S(2)}) %collective-permute-start.18) | collective-permute-done | bytes 196640 | tf_op jit(solution)/shard_map/ppermute | solution.py:218
  64.9 3.8 %collective-permute-done.20.refs_6_ = f32[6,64,128]{2,1,0:T(8,128)S(1)} collective-permute-done((f32[6,64,128]{2,1,0:T(8,128)S(1)}, f32[6,64,128]{2,1,0:T(8,128)S(1)}, u32[]{:S(2)}, u32[]{:S(2)}) %collective-permute-start.20) | collective-permute-done | bytes 196640 | tf_op jit(solution)/shard_map/ppermute | solution.py:218
  68.7 1.8 %shard_map.73 = f32[4,9,64,128]{3,2,1,0:T(8,128)} custom-call(s32[54]{0:T(128)S(1)} %get-tuple-element.40.back, f32[6,64,128]{2,1,0:T(8,128)S(1)} %collective-permute-done.14.refs_0_, f32[6,64,128]{2,1,0:T(8,128)S(1)} %collective-permute-done.15.refs_1_, f32[6,64,128]{2,1,0:T(8,128)S(1)} %collective-permute-done.16.refs_2_, ...), custom_call_target="tpu_custom_call" | custom-call | tf_op jit(solution)/shard_map/pallas_call | solution.py:196
  (27 shorter events, 0.4 us)
Async XLA Ops:
  0.6 22.0 %copy-start.1 = (s32[1,27,2]{1,2,0:T(2,128)S(1)}, s32[1,27,2]{1,2,0:T(2,128)}, u32[]{:S(2)}) copy-start(s32[1,27,2]{1,2,0:T(2,128)} %param.9) | copy-start | bytes 652
  7.7 8.1 %collective-permute-start = (f32[6,64,128]{2,1,0:T(8,128)S(1)}, f32[6,64,128]{2,1,0:T(8,128)S(1)}, u32[]{:S(2)}, u32[]{:S(2)}) collective-permute-start(f32[6,64,128]{2,1,0:T(8,128)S(1)} %get-tuple-element.26), channel_id=1, source_target_pairs={{0,4},{1,5},{2,6},{3,7},{4,0},{5,1},{6,2},{7,3},{8,12},{9,13},{10,... | collective-permute-start | bytes 589832 | tf_op jit(solution)/shard_map/ppermute | solution.py:218
  9.2 8.4 %collective-permute-start.1 = (f32[6,64,128]{2,1,0:T(8,128)S(1)}, f32[6,64,128]{2,1,0:T(8,128)S(1)}, u32[]{:S(2)}, u32[]{:S(2)}) collective-permute-start(f32[6,64,128]{2,1,0:T(8,128)S(1)} %get-tuple-element.28), channel_id=1, source_target_pairs={{0,32},{1,33},{2,34},{3,35},{4,36},{5,37},{6,38},{7,39},{8,40},{9,... | collective-permute-start | bytes 589832 | tf_op jit(solution)/shard_map/ppermute | solution.py:218
  10.5 8.3 %collective-permute-start.2 = (f32[6,64,128]{2,1,0:T(8,128)S(1)}, f32[6,64,128]{2,1,0:T(8,128)S(1)}, u32[]{:S(2)}, u32[]{:S(2)}) collective-permute-start(f32[6,64,128]{2,1,0:T(8,128)S(1)} %get-tuple-element.29), channel_id=1, source_target_pairs={{0,96},{1,97},{2,98},{3,99},{4,100},{5,101},{6,102},{7,103},{8,104... | collective-permute-start | bytes 589832 | tf_op jit(solution)/shard_map/ppermute | solution.py:218
  11.9 10.7 %collective-permute-start.3 = (f32[6,64,128]{2,1,0:T(8,128)S(1)}, f32[6,64,128]{2,1,0:T(8,128)S(1)}, u32[]{:S(2)}, u32[]{:S(2)}) collective-permute-start(f32[6,64,128]{2,1,0:T(8,128)S(1)} %get-tuple-element.30), channel_id=1, source_target_pairs={{0,60},{1,61},{2,62},{3,63},{4,40},{5,41},{6,42},{7,43},{8,36},{9,... | collective-permute-start | bytes 589832 | tf_op jit(solution)/shard_map/ppermute | solution.py:218
  13.5 12.9 %collective-permute-start.4 = (f32[6,64,128]{2,1,0:T(8,128)S(1)}, f32[6,64,128]{2,1,0:T(8,128)S(1)}, u32[]{:S(2)}, u32[]{:S(2)}) collective-permute-start(f32[6,64,128]{2,1,0:T(8,128)S(1)} %get-tuple-element.31), channel_id=1, source_target_pairs={{0,124},{1,125},{2,126},{3,127},{4,104},{5,105},{6,106},{7,107},{8... | collective-permute-start | bytes 589832 | tf_op jit(solution)/shard_map/ppermute | solution.py:218
  15.7 10.6 %collective-permute-start.5 = (f32[6,64,128]{2,1,0:T(8,128)S(1)}, f32[6,64,128]{2,1,0:T(8,128)S(1)}, u32[]{:S(2)}, u32[]{:S(2)}) collective-permute-start(f32[6,64,128]{2,1,0:T(8,128)S(1)} %get-tuple-element.32), channel_id=1, source_target_pairs={{0,28},{1,29},{2,30},{3,31},{4,8},{5,9},{6,10},{7,11},{8,4},{9,5},... | collective-permute-start | bytes 589832 | tf_op jit(solution)/shard_map/ppermute | solution.py:218
  17.6 8.7 %collective-permute-start.6 = (f32[6,64,128]{2,1,0:T(8,128)S(1)}, f32[6,64,128]{2,1,0:T(8,128)S(1)}, u32[]{:S(2)}, u32[]{:S(2)}) collective-permute-start(f32[6,64,128]{2,1,0:T(8,128)S(1)} %get-tuple-element.33), channel_id=1, source_target_pairs={{0,36},{1,37},{2,38},{3,39},{4,32},{5,33},{6,34},{7,35},{8,44},{9,... | collective-permute-start | bytes 589832 | tf_op jit(solution)/shard_map/ppermute | solution.py:218
  18.9 7.5 %collective-permute-start.7 = (f32[6,64,128]{2,1,0:T(8,128)S(1)}, f32[6,64,128]{2,1,0:T(8,128)S(1)}, u32[]{:S(2)}, u32[]{:S(2)}) collective-permute-start(f32[6,64,128]{2,1,0:T(8,128)S(1)} %get-tuple-element.34), channel_id=1, source_target_pairs={{0,100},{1,101},{2,102},{3,103},{4,96},{5,97},{6,98},{7,99},{8,108... | collective-permute-start | bytes 589832 | tf_op jit(solution)/shard_map/ppermute | solution.py:218
  22.6 4.5 %collective-permute-start.9 = (s32[2,27]{1,0:T(2,128)S(1)}, s32[2,27]{1,0:T(2,128)S(1)}, u32[]{:S(2)}, u32[]{:S(2)}) collective-permute-start(s32[2,27]{1,0:T(2,128)S(1)} %bitcast.3), channel_id=1, source_target_pairs={{0,3},{1,0},{2,1},{3,2},{4,7},{5,4},{6,5},{7,6},{8,11},{9,8},{10,9... | collective-permute-start | bytes 656 | tf_op jit(solution)/shard_map/ppermute | solution.py:218
  26.4 3.6 %collective-permute-start.8 = (s32[2,27]{1,0:T(2,128)S(1)}, s32[2,27]{1,0:T(2,128)S(1)}, u32[]{:S(2)}, u32[]{:S(2)}) collective-permute-start(s32[2,27]{1,0:T(2,128)S(1)} %bitcast.4), channel_id=1, source_target_pairs={{0,1},{1,2},{2,3},{3,0},{4,5},{5,6},{6,7},{7,4},{8,9},{9,10},{10,1... | collective-permute-start | bytes 656 | tf_op jit(solution)/shard_map/ppermute | solution.py:218
  30.8 6.5 %collective-permute-start.10 = (f32[8,64,128]{2,1,0:T(8,128)S(1)}, f32[8,64,128]{2,1,0:T(8,128)S(1)}, u32[]{:S(2)}, u32[]{:S(2)}) collective-permute-start(f32[8,64,128]{2,1,0:T(8,128)S(1)} %get-tuple-element.37), channel_id=1, source_target_pairs={{0,1},{1,2},{2,3},{3,0},{4,5},{5,6},{6,7},{7,4},{8,9},{9,10},{10,1... | collective-permute-start | bytes 786440 | tf_op jit(solution)/shard_map/ppermute | solution.py:218
  30.9 6.5 %collective-permute-start.11 = (f32[8,64,128]{2,1,0:T(8,128)S(1)}, f32[8,64,128]{2,1,0:T(8,128)S(1)}, u32[]{:S(2)}, u32[]{:S(2)}) collective-permute-start(f32[8,64,128]{2,1,0:T(8,128)S(1)} %get-tuple-element.38), channel_id=1, source_target_pairs={{0,3},{1,0},{2,1},{3,2},{4,7},{5,4},{6,5},{7,6},{8,11},{9,8},{10,9... | collective-permute-start | bytes 786440 | tf_op jit(solution)/shard_map/ppermute | solution.py:218
  37.4 6.5 %collective-permute-start.12 = (f32[8,64,128]{2,1,0:T(8,128)S(1)}, f32[8,64,128]{2,1,0:T(8,128)S(1)}, u32[]{:S(2)}, u32[]{:S(2)}) collective-permute-start(f32[8,64,128]{2,1,0:T(8,128)S(1)} %add.19), channel_id=1, source_target_pairs={{0,1},{1,2},{2,3},{3,0},{4,5},{5,6},{6,7},{7,4},{8,9},{9,10},{10,1... | collective-permute-start | bytes 786440 | tf_op jit(solution)/shard_map/ppermute | solution.py:218
  37.5 32.9 %copy-start = (f32[8,64,128]{2,1,0:T(8,128)}, f32[8,64,128]{2,1,0:T(8,128)S(1)}, u32[]{:S(2)}) copy-start(f32[8,64,128]{2,1,0:T(8,128)S(1)} %get-tuple-element.51.refs_4_) | copy-start | bytes 786436
  37.5 6.4 %collective-permute-start.13 = (f32[8,64,128]{2,1,0:T(8,128)S(1)}, f32[8,64,128]{2,1,0:T(8,128)S(1)}, u32[]{:S(2)}, u32[]{:S(2)}) collective-permute-start(f32[8,64,128]{2,1,0:T(8,128)S(1)} %get-tuple-element.50), channel_id=1, source_target_pairs={{0,3},{1,0},{2,1},{3,2},{4,7},{5,4},{6,5},{7,6},{8,11},{9,8},{10,9... | collective-permute-start | bytes 786440 | tf_op jit(solution)/shard_map/ppermute | solution.py:218
  44.6 13.2 %collective-permute-start.14 = (f32[6,64,128]{2,1,0:T(8,128)S(1)}, f32[6,64,128]{2,1,0:T(8,128)S(1)}, u32[]{:S(2)}, u32[]{:S(2)}) collective-permute-start(f32[6,64,128]{2,1,0:T(8,128)S(1)} %get-tuple-element.41), channel_id=1, source_target_pairs={{0,96},{1,97},{2,98},{3,99},{4,100},{5,101},{6,102},{7,103},{8,104... | collective-permute-start | bytes 589832 | tf_op jit(solution)/shard_map/ppermute | solution.py:218
  46.4 13.7 %collective-permute-start.15 = (f32[6,64,128]{2,1,0:T(8,128)S(1)}, f32[6,64,128]{2,1,0:T(8,128)S(1)}, u32[]{:S(2)}, u32[]{:S(2)}) collective-permute-start(f32[6,64,128]{2,1,0:T(8,128)S(1)} %get-tuple-element.42), channel_id=1, source_target_pairs={{0,32},{1,33},{2,34},{3,35},{4,36},{5,37},{6,38},{7,39},{8,40},{9,... | collective-permute-start | bytes 589832 | tf_op jit(solution)/shard_map/ppermute | solution.py:218
  47.1 14.5 %collective-permute-start.16 = (f32[6,64,128]{2,1,0:T(8,128)S(1)}, f32[6,64,128]{2,1,0:T(8,128)S(1)}, u32[]{:S(2)}, u32[]{:S(2)}) collective-permute-start(f32[6,64,128]{2,1,0:T(8,128)S(1)} %get-tuple-element.43), channel_id=1, source_target_pairs={{0,124},{1,125},{2,126},{3,127},{4,104},{5,105},{6,106},{7,107},{8... | collective-permute-start | bytes 589832 | tf_op jit(solution)/shard_map/ppermute | solution.py:218
  56.5 7.3 %collective-permute-start.17 = (f32[6,64,128]{2,1,0:T(8,128)S(1)}, f32[6,64,128]{2,1,0:T(8,128)S(1)}, u32[]{:S(2)}, u32[]{:S(2)}) collective-permute-start(f32[6,64,128]{2,1,0:T(8,128)S(1)} %get-tuple-element.44), channel_id=1, source_target_pairs={{0,60},{1,61},{2,62},{3,63},{4,40},{5,41},{6,42},{7,43},{8,36},{9,... | collective-permute-start | bytes 589832 | tf_op jit(solution)/shard_map/ppermute | solution.py:218
  56.5 8.4 %collective-permute-start.18 = (f32[6,64,128]{2,1,0:T(8,128)S(1)}, f32[6,64,128]{2,1,0:T(8,128)S(1)}, u32[]{:S(2)}, u32[]{:S(2)}) collective-permute-start(f32[6,64,128]{2,1,0:T(8,128)S(1)} %get-tuple-element.45), channel_id=1, source_target_pairs={{0,28},{1,29},{2,30},{3,31},{4,8},{5,9},{6,10},{7,11},{8,4},{9,5},... | collective-permute-start | bytes 589832 | tf_op jit(solution)/shard_map/ppermute | solution.py:218
  57.8 7.1 %collective-permute-start.19 = (f32[6,64,128]{2,1,0:T(8,128)S(1)}, f32[6,64,128]{2,1,0:T(8,128)S(1)}, u32[]{:S(2)}, u32[]{:S(2)}) collective-permute-start(f32[6,64,128]{2,1,0:T(8,128)S(1)} %get-tuple-element.46), channel_id=1, source_target_pairs={{0,100},{1,101},{2,102},{3,103},{4,96},{5,97},{6,98},{7,99},{8,108... | collective-permute-start | bytes 589832 | tf_op jit(solution)/shard_map/ppermute | solution.py:218
  60.2 8.5 %collective-permute-start.20 = (f32[6,64,128]{2,1,0:T(8,128)S(1)}, f32[6,64,128]{2,1,0:T(8,128)S(1)}, u32[]{:S(2)}, u32[]{:S(2)}) collective-permute-start(f32[6,64,128]{2,1,0:T(8,128)S(1)} %get-tuple-element.47), channel_id=1, source_target_pairs={{0,36},{1,37},{2,38},{3,39},{4,32},{5,33},{6,34},{7,35},{8,44},{9,... | collective-permute-start | bytes 589832 | tf_op jit(solution)/shard_map/ppermute | solution.py:218
  61.6 7.1 %collective-permute-start.21 = (f32[6,64,128]{2,1,0:T(8,128)S(1)}, f32[6,64,128]{2,1,0:T(8,128)S(1)}, u32[]{:S(2)}, u32[]{:S(2)}) collective-permute-start(f32[6,64,128]{2,1,0:T(8,128)S(1)} %get-tuple-element.48), channel_id=1, source_target_pairs={{0,4},{1,5},{2,6},{3,7},{4,0},{5,1},{6,2},{7,3},{8,12},{9,13},{10,... | collective-permute-start | bytes 589832 | tf_op jit(solution)/shard_map/ppermute | solution.py:218

commit v4 on v3

--- a/solution.py
+++ b/solution.py
@@ -18,6 +18,7 @@
 OUT_ORDER = list(range(8))
 BACK_ORDER = list(range(8))
 TABLE_AFTER = 7
+EARLY = (8, 0, 1, 2)
 AHEAD = 2
 FIRST = 2
 
@@ -53,7 +54,7 @@
 
 def contribute_kernel(extents, capacity, blocks, key_hbm, residual_hbm, inverse_hbm, *rest):
     outs = rest[:9]
-    back, placed, key, residual, inverse, key_sem, res_sem, inv_sem = rest[9:]
+    placed, key, residual, inverse, key_sem, res_sem, inv_sem = rest[9:]
     patches = inverse.shape[0]
     key_copy = pltpu.make_async_copy(key_hbm, key, key_sem)
     res_copy = pltpu.make_async_copy(residual_hbm, residual, res_sem)
@@ -69,15 +70,12 @@
     width = inverse.shape[1] // blocks
     near = [lax.axis_index(a) for a in AXES]
     per = 3 * capacity
-    for k in range(9 * per):
-        back[k] = patches * blocks
     key_copy.wait()
     at = []
     for p in range(patches):
         for b in range(blocks):
             owner, slot = lax.div(key[p, b], capacity), lax.rem(key[p, b], capacity)
             at.append(place(owner, slot, near, extents, capacity))
-            back[at[-1]] = p * blocks + b
     res_copy.wait()
     for p in range(patches):
         inv_copies[p].wait()
@@ -105,9 +103,8 @@
     return pl.pallas_call(
         functools.partial(contribute_kernel, extents, capacity, blocks),
         in_specs=[pl.BlockSpec(memory_space=pl.ANY)] * 3,
-        out_specs=[pl.BlockSpec(memory_space=VMEM)] * 9 + [pl.BlockSpec(memory_space=SMEM)],
-        out_shape=[jax.ShapeDtypeStruct((per, rhs, width), jnp.float32)] * 9
-        + [jax.ShapeDtypeStruct((9 * per,), jnp.int32)],
+        out_specs=[pl.BlockSpec(memory_space=VMEM)] * 9,
+        out_shape=[jax.ShapeDtypeStruct((per, rhs, width), jnp.float32)] * 9,
         scratch_shapes=[
             VMEM((9 * per, rhs, width), jnp.float32),
             SMEM(key.shape, jnp.int32),
@@ -126,6 +123,38 @@
     code_y = 1 if way == 0 else 2 - way_code(way, near_y)
     code = 9 * (dx + 1) + cz if SIDE == 0 else (dx + 1) + 9 * cz
     return tables[cz][c, code + 3 * code_y]
+
+
+def trace(back, key, extents, capacity):
+    patches, blocks = key.shape
+    near = [lax.axis_index(a) for a in AXES]
+    for k in range(27 * capacity):
+        back[k] = patches * blocks
+    for p in range(patches):
+        for b in range(blocks):
+            owner, slot = lax.div(key[p, b], capacity), lax.rem(key[p, b], capacity)
+            back[place(owner, slot, near, extents, capacity)] = p * blocks + b
+
+
+def gather_own_kernel(capacity, extents, key, table, *refs):
+    arrived, (out, back, total) = refs[:9], refs[9:]
+    gather_kernel(capacity, (1,), table, *arrived, out, total)
+    trace(back, key, extents, capacity)
+
+
+def gather_own(key, table, arrived, extents, capacity):
+    _, rhs, width = arrived[0].shape
+    return pl.pallas_call(
+        functools.partial(gather_own_kernel, capacity, extents),
+        in_specs=[pl.BlockSpec(memory_space=SMEM)] * 2 + [pl.BlockSpec(memory_space=VMEM)] * 9,
+        out_specs=[pl.BlockSpec(memory_space=VMEM), pl.BlockSpec(memory_space=SMEM)],
+        out_shape=[
+            jax.ShapeDtypeStruct((OWNB, rhs, width), jnp.float32),
+            jax.ShapeDtypeStruct((27 * capacity,), jnp.int32),
+        ],
+        scratch_shapes=[VMEM((1, OWNB + 1, rhs, width), jnp.float32)],
+        compiler_params=pltpu.CompilerParams(vmem_limit_bytes=32 * 2**20),
+    )(key, table, *arrived)
 
 
 def gather_kernel(capacity, codes, *refs):
@@ -179,28 +208,38 @@
     )(*tables, *totals)
 
 
-def collect_kernel(capacity, patches, blocks, back, *refs):
-    returned, out, wide = refs[0:9], refs[9], refs[10]
+def collect_kernel(capacity, blocks, steps, back, *refs):
+    returned, (out, sems) = refs[: len(steps)], refs[-2:]
     near_y = lax.axis_index("gy")
     per = 3 * capacity
-    for i, (dx, way) in enumerate(PLANE):
+    jobs = []
+    for i, step in enumerate(steps):
+        dx, way = PLANE[step]
         first = ((dx + 1) * 3 + way_code(way, near_y)) * per
         for k in range(per):
-            wide[back[first + k]] = returned[i][k]
-    for p in range(patches):
-        out[p] = wide[p * blocks : (p + 1) * blocks]
-
-
-def collect(back, returned, patches, blocks, capacity):
+            row = back[first + k]
+            copy = pltpu.make_async_copy(returned[i].at[k], out.at[row], sems.at[i * per + k])
+            jobs.append((row < blocks, copy))
+    for used, copy in jobs:
+        pl.when(used)(copy.start)
+    for used, copy in jobs:
+        pl.when(used)(copy.wait)
+
+
+def collect(back, returned, steps, rows, capacity, out=None):
     _, rhs, width = returned[0].shape
-    return pl.pallas_call(
-        functools.partial(collect_kernel, capacity, patches, blocks),
-        in_specs=[pl.BlockSpec(memory_space=SMEM)] + [pl.BlockSpec(memory_space=VMEM)] * 9,
-        out_specs=pl.BlockSpec(memory_space=VMEM),
-        out_shape=jax.ShapeDtypeStruct((patches, blocks, rhs, width), jnp.float32),
-        scratch_shapes=[VMEM((patches * blocks + 1, rhs, width), jnp.float32)],
+    arrays = [back, *[returned[i] for i in steps]] + ([] if out is None else [out])
+    return pl.pallas_call(
+        functools.partial(collect_kernel, capacity, rows, steps),
+        in_specs=[pl.BlockSpec(memory_space=SMEM)]
+        + [pl.BlockSpec(memory_space=VMEM)] * len(steps)
+        + [pl.BlockSpec(memory_space=pl.ANY)] * (out is not None),
+        out_specs=pl.BlockSpec(memory_space=pl.ANY),
+        out_shape=jax.ShapeDtypeStruct((rows, rhs, width), jnp.float32),
+        scratch_shapes=[pltpu.SemaphoreType.DMA((len(steps) * 3 * capacity,))],
+        input_output_aliases={} if out is None else {len(arrays) - 1: 0},
         compiler_params=pltpu.CompilerParams(vmem_limit_bytes=32 * 2**20),
-    )(back, *returned)
+    )(*arrays)
 
 
 def move(array, extents, side, way, last):
@@ -223,14 +262,14 @@
     capacity = recv_target.shape[2]
     table = jnp.swapaxes(recv_target, 1, 2)[0]
     key = block_owner * capacity + block_slot
-    *outgoing, back = contribute(key, star_residual, patch_inverse, extents, capacity)
+    outgoing = contribute(key, star_residual, patch_inverse, extents, capacity)
     arrived = [outgoing[HOME]] * 9
     for i in OUT_ORDER:
         arrived[i] = move(outgoing[i], extents, *PLANE[i], 0)
     table, arrived[TABLE_AFTER] = lax.optimization_barrier((table, arrived[TABLE_AFTER]))
     tables = [move(table, extents, 0, 0, 1), table, move(table, extents, 0, 0, -1)]
     below, above = gather(tables, (0, 2), arrived, capacity)
-    (own,) = gather(tables, (1,), arrived, capacity)
+    own, back = gather_own(key, tables[1], arrived, extents, capacity)
     from_below = move(above, extents, 0, 0, 1)
     from_above = move(below, extents, 0, 0, -1)
     rising = own + from_below
@@ -245,7 +284,12 @@
     returned = [answers[HOME]] * 9
     for i in BACK_ORDER:
         returned[i] = move(answers[i], extents, -PLANE[i][0], PLANE[i][1], 0)
-    combined = collect(back, returned, *block_owner.shape, capacity)
+    patches, blocks = block_owner.shape
+    rows = patches * blocks
+    combined = collect(back, returned, EARLY, rows, capacity)
+    late = tuple(i for i in range(9) if i not in EARLY)
+    combined = collect(back, returned, late, rows, capacity, combined)
+    combined = combined.reshape(patches, blocks, *combined.shape[1:])
     return owned, combined
 
 

time: 70.6 us -> 70.2 us (level)
  waiting for transfers between devices: 19.7 us -> 17 us
  Pallas kernels: 10.9 us -> 13.1 us
    pallas_call x1 -> x3, Pallas kernels: 1.75 us -> 4.94 us  [the longest x2 3.18 us: collect(): pl.pallas_call(functools.partial(collect_kernel, capacity, rows, steps),...]
    ppermute x22, waiting for transfers between devices: 19.7 us -> 17 us  [move(): return lax.ppermute(array, AXES, pairs)]
    pallas_call x2 -> x1, Pallas kernels: 1.52 us -> 0.83 us  [gather(): pl.pallas_call(functools.partial(gather_kernel, capacity, codes), in_spec...]
  transfers between devices with their start and end apart: 22 -> 22, of which waited for: 9 -> 8; matrix products, arithmetic and copies ran while one was open for 0% -> 0% of each run, Pallas kernels for 2% -> 6%
where the time goes in v4:
time: 70.2 us; the launch traced here: 70 us
  starting transfers between devices  38.3 us (55%)
  waiting for transfers between devices  17 us (24%)
  Pallas kernels  13.1 us (19%)
  other arithmetic  0.87 us (1%)
  between operations  0.78 us (1%)
    ppermute x22, starting transfers between devices, move(): return lax.ppermute(array, AXES, pairs)  38.3 us
    ppermute x22, waiting for transfers between devices, move(): return lax.ppermute(array, AXES, pairs)  17 us
    pallas_call x1, Pallas kernels, contribute(): pl.pallas_call(functools.partial(contribute_kernel, extents, capacity, bl...  6 us
    pallas_call x2, Pallas kernels, collect(): pl.pallas_call(functools.partial(collect_kernel, capacity, rows, steps),...  3.18 us
    pallas_call x1, Pallas kernels, gather_own(): pl.pallas_call(functools.partial(gather_own_kernel, capacity, extents), i...  1.77 us
  transfers between devices with their start and end apart: 22, of which 8 were waited for; matrix products, arithmetic and copies ran while one was open for 0% of the time, Pallas kernels for 6%

profile of v4, /device:TPU:1, one launch (start us, length us, event | category | flops | bytes accessed | tf_op | source)
XLA Modules:
  0.0 70.0 jit_solution(13787857847324258446)
XLA Ops:
  0.6 0.7 %multiply_add_fusion.key_hbm.key = s32[4,9]{1,0:T(4,128)S(1)} fusion(s32[4,9]{1,0:T(4,128)} %param.8, s32[4,9]{1,0:T(4,128)} %param.7), kind=kLoop, calls=%fused_computation | loop fusion | flops 72 | bytes 432 | tf_op jit(solution)/shard_map/add | solution.py:264
  1.3 6.0 %shard_map.68 = (f32[6,64,128]{2,1,0:T(8,128)S(1)}, f32[6,64,128]{2,1,0:T(8,128)S(1)}, f32[6,64,128]{2,1,0:T(8,128)S(1)}, f32[6,64,128]{2,1,0:T(8,128)S(1)}, f32...) custom-call(s32[4,9]{1,0:T(4,128)S(1)} %multiply_add_fusion.key_hbm., ...), custom_call_target="tpu_custom_call" | custom-call | tf_op jit(solution)/shard_map/pallas_call | solution.py:103
  7.3 1.5 %collective-permute-start = (f32[6,64,128]{2,1,0:T(8,128)S(1)}, f32[6,64,128]{2,1,0:T(8,128)S(1)}, u32[]{:S(2)}, u32[]{:S(2)}) collective-permute-start(f32[6,64,128]{2,1,0:T(8,128)S(1)} %get-tuple-element.27), channel_id=1, source_target_pairs={{0,4},{1,5},{2,6},{3,7},{4,0},{5,1},{6,2},{7,3},{8,12},{9,13},{10,... | collective-permute-start | bytes 589832 | tf_op jit(solution)/shard_map/ppermute | solution.py:257
  8.8 1.3 %collective-permute-start.1 = (f32[6,64,128]{2,1,0:T(8,128)S(1)}, f32[6,64,128]{2,1,0:T(8,128)S(1)}, u32[]{:S(2)}, u32[]{:S(2)}) collective-permute-start(f32[6,64,128]{2,1,0:T(8,128)S(1)} %get-tuple-element.29), channel_id=1, source_target_pairs={{0,32},{1,33},{2,34},{3,35},{4,36},{5,37},{6,38},{7,39},{8,40},{9,... | collective-permute-start | bytes 589832 | tf_op jit(solution)/shard_map/ppermute | solution.py:257
  10.2 1.4 %collective-permute-start.2 = (f32[6,64,128]{2,1,0:T(8,128)S(1)}, f32[6,64,128]{2,1,0:T(8,128)S(1)}, u32[]{:S(2)}, u32[]{:S(2)}) collective-permute-start(f32[6,64,128]{2,1,0:T(8,128)S(1)} %get-tuple-element.30), channel_id=1, source_target_pairs={{0,96},{1,97},{2,98},{3,99},{4,100},{5,101},{6,102},{7,103},{8,104... | collective-permute-start | bytes 589832 | tf_op jit(solution)/shard_map/ppermute | solution.py:257
  11.5 1.6 %collective-permute-start.3 = (f32[6,64,128]{2,1,0:T(8,128)S(1)}, f32[6,64,128]{2,1,0:T(8,128)S(1)}, u32[]{:S(2)}, u32[]{:S(2)}) collective-permute-start(f32[6,64,128]{2,1,0:T(8,128)S(1)} %get-tuple-element.31), channel_id=1, source_target_pairs={{0,60},{1,61},{2,62},{3,63},{4,40},{5,41},{6,42},{7,43},{8,36},{9,... | collective-permute-start | bytes 589832 | tf_op jit(solution)/shard_map/ppermute | solution.py:257
  13.1 2.2 %collective-permute-start.4 = (f32[6,64,128]{2,1,0:T(8,128)S(1)}, f32[6,64,128]{2,1,0:T(8,128)S(1)}, u32[]{:S(2)}, u32[]{:S(2)}) collective-permute-start(f32[6,64,128]{2,1,0:T(8,128)S(1)} %get-tuple-element.32), channel_id=1, source_target_pairs={{0,124},{1,125},{2,126},{3,127},{4,104},{5,105},{6,106},{7,107},{8... | collective-permute-start | bytes 589832 | tf_op jit(solution)/shard_map/ppermute | solution.py:257
  15.4 1.9 %collective-permute-start.5 = (f32[6,64,128]{2,1,0:T(8,128)S(1)}, f32[6,64,128]{2,1,0:T(8,128)S(1)}, u32[]{:S(2)}, u32[]{:S(2)}) collective-permute-start(f32[6,64,128]{2,1,0:T(8,128)S(1)} %get-tuple-element.33), channel_id=1, source_target_pairs={{0,28},{1,29},{2,30},{3,31},{4,8},{5,9},{6,10},{7,11},{8,4},{9,5},... | collective-permute-start | bytes 589832 | tf_op jit(solution)/shard_map/ppermute | solution.py:257
  17.3 1.2 %collective-permute-start.6 = (f32[6,64,128]{2,1,0:T(8,128)S(1)}, f32[6,64,128]{2,1,0:T(8,128)S(1)}, u32[]{:S(2)}, u32[]{:S(2)}) collective-permute-start(f32[6,64,128]{2,1,0:T(8,128)S(1)} %get-tuple-element.34), channel_id=1, source_target_pairs={{0,36},{1,37},{2,38},{3,39},{4,32},{5,33},{6,34},{7,35},{8,44},{9,... | collective-permute-start | bytes 589832 | tf_op jit(solution)/shard_map/ppermute | solution.py:257
  18.5 1.8 %collective-permute-start.7 = (f32[6,64,128]{2,1,0:T(8,128)S(1)}, f32[6,64,128]{2,1,0:T(8,128)S(1)}, u32[]{:S(2)}, u32[]{:S(2)}) collective-permute-start(f32[6,64,128]{2,1,0:T(8,128)S(1)} %get-tuple-element.35), channel_id=1, source_target_pairs={{0,100},{1,101},{2,102},{3,103},{4,96},{5,97},{6,98},{7,99},{8,108... | collective-permute-start | bytes 589832 | tf_op jit(solution)/shard_map/ppermute | solution.py:257
  20.3 2.0 %collective-permute-done.3.refs_2_.refs_4_ = f32[6,64,128]{2,1,0:T(8,128)S(1)} collective-permute-done((f32[6,64,128]{2,1,0:T(8,128)S(1)}, f32[6,64,128]{2,1,0:T(8,128)S(1)}, u32[]{:S(2)}, u32[]{:S(2)}) %collective-permute-start.3) | collective-permute-done | bytes 196640 | tf_op jit(solution)/shard_map/ppermute | solution.py:257
  22.3 3.7 %collective-permute-start.9 = (s32[2,27]{1,0:T(2,128)S(1)}, s32[2,27]{1,0:T(2,128)S(1)}, u32[]{:S(2)}, u32[]{:S(2)}) collective-permute-start(s32[2,27]{1,0:T(2,128)S(1)} %bitcast.4), channel_id=1, source_target_pairs={{0,3},{1,0},{2,1},{3,2},{4,7},{5,4},{6,5},{7,6},{8,11},{9,8},{10,9... | collective-permute-start | bytes 656 | tf_op jit(solution)/shard_map/ppermute | solution.py:257
  26.0 0.7 collective-permute-done.9.refs_1_.refs_2_
  26.7 2.9 %collective-permute-done.8.refs_0_ = s32[2,27]{1,0:T(2,128)S(1)} collective-permute-done((s32[2,27]{1,0:T(2,128)S(1)}, s32[2,27]{1,0:T(2,128)S(1)}, u32[]{:S(2)}, u32[]{:S(2)}) %collective-permute-start.8) | collective-permute-done | bytes 248 | tf_op jit(solution)/shard_map/ppermute | solution.py:257
  29.6 0.8 %shard_map.70 = (f32[8,64,128]{2,1,0:T(8,128)S(1)}, f32[8,64,128]{2,1,0:T(8,128)S(1)}) custom-call(s32[2,27]{1,0:T(2,128)S(1)} %collective-permute-done.8.refs_0_, s32[2,27]{1,0:T(2,128)S(1)} %collective-permute-done.9.refs_1_.refs_2_, f32[6,64,128]{2,1,0:T(8,128)S(1)} %collective-permute-done.1.refs_0_.refs_2_, ...), custom_call_target="tpu_custom_call" | custom-call | tf_op jit(solution)/shard_map/pallas_call | solution.py:178
  30.6 2.7 %collective-permute-start.11 = (f32[8,64,128]{2,1,0:T(8,128)S(1)}, f32[8,64,128]{2,1,0:T(8,128)S(1)}, u32[]{:S(2)}, u32[]{:S(2)}) collective-permute-start(f32[8,64,128]{2,1,0:T(8,128)S(1)} %get-tuple-element.40), channel_id=1, source_target_pairs={{0,3},{1,0},{2,1},{3,2},{4,7},{5,4},{6,5},{7,6},{8,11},{9,8},{10,9... | collective-permute-start | bytes 786440 | tf_op jit(solution)/shard_map/ppermute | solution.py:257
  33.2 1.8 %shard_map.69 = (f32[8,64,128]{2,1,0:T(8,128)S(1)}, s32[54]{0:T(128)S(1)}) custom-call(s32[4,9]{1,0:T(4,128)S(1)} %multiply_add_fusion.key_hbm.key, s32[2,27]{1,0:T(2,128)S(1)} %bitcast.6, f32[6,64,128]{2,1,0:T(8,128)S(1)} %collective-permute-done.1.refs_0_.refs_2_, f32[6,64,128]{2,1,0:T(8,128)S(1)} %collective-permute-done.2.refs_1_.refs_3_, ...), custom_call_target="tpu_custom_call" | custom-call | tf_op jit(solution)/shard_map/pallas_call | solution.py:147
  35.0 2.0 %collective-permute-done.10 = f32[8,64,128]{2,1,0:T(8,128)S(1)} collective-permute-done((f32[8,64,128]{2,1,0:T(8,128)S(1)}, f32[8,64,128]{2,1,0:T(8,128)S(1)}, u32[]{:S(2)}, u32[]{:S(2)}) %collective-permute-start.10) | collective-permute-done | bytes 262176 | tf_op jit(solution)/shard_map/ppermute | solution.py:257
  37.2 2.7 %collective-permute-start.13 = (f32[8,64,128]{2,1,0:T(8,128)S(1)}, f32[8,64,128]{2,1,0:T(8,128)S(1)}, u32[]{:S(2)}, u32[]{:S(2)}) collective-permute-start(f32[8,64,128]{2,1,0:T(8,128)S(1)} %get-tuple-element.52), channel_id=1, source_target_pairs={{0,3},{1,0},{2,1},{3,2},{4,7},{5,4},{6,5},{7,6},{8,11},{9,8},{10,9... | collective-permute-start | bytes 786440 | tf_op jit(solution)/shard_map/ppermute | solution.py:257
  39.9 3.6 %collective-permute-done.12 = f32[8,64,128]{2,1,0:T(8,128)S(1)} collective-permute-done((f32[8,64,128]{2,1,0:T(8,128)S(1)}, f32[8,64,128]{2,1,0:T(8,128)S(1)}, u32[]{:S(2)}, u32[]{:S(2)}) %collective-permute-start.12) | collective-permute-done | bytes 262176 | tf_op jit(solution)/shard_map/ppermute | solution.py:257
  43.6 0.6 shard_map.72
  44.2 1.9 %collective-permute-start.19 = (f32[6,64,128]{2,1,0:T(8,128)S(1)}, f32[6,64,128]{2,1,0:T(8,128)S(1)}, u32[]{:S(2)}, u32[]{:S(2)}) collective-permute-start(f32[6,64,128]{2,1,0:T(8,128)S(1)} %get-tuple-element.49), channel_id=1, source_target_pairs={{0,96},{1,97},{2,98},{3,99},{4,100},{5,101},{6,102},{7,103},{8,104... | collective-permute-start | bytes 589832 | tf_op jit(solution)/shard_map/ppermute | solution.py:257
  46.1 0.7 shard_map.71
  46.8 9.4 %collective-permute-start.21 = (f32[6,64,128]{2,1,0:T(8,128)S(1)}, f32[6,64,128]{2,1,0:T(8,128)S(1)}, u32[]{:S(2)}, u32[]{:S(2)}) collective-permute-start(f32[6,64,128]{2,1,0:T(8,128)S(1)} %get-tuple-element.51), channel_id=1, source_target_pairs={{0,124},{1,125},{2,126},{3,127},{4,104},{5,105},{6,106},{7,107},{8... | collective-permute-start | bytes 589832 | tf_op jit(solution)/shard_map/ppermute | solution.py:257
  56.2 1.3 %collective-permute-start.15 = (f32[6,64,128]{2,1,0:T(8,128)S(1)}, f32[6,64,128]{2,1,0:T(8,128)S(1)}, u32[]{:S(2)}, u32[]{:S(2)}) collective-permute-start(f32[6,64,128]{2,1,0:T(8,128)S(1)} %get-tuple-element.44), channel_id=1, source_target_pairs={{0,28},{1,29},{2,30},{3,31},{4,8},{5,9},{6,10},{7,11},{8,4},{9,5},... | collective-permute-start | bytes 589832 | tf_op jit(solution)/shard_map/ppermute | solution.py:257
  57.5 2.4 %collective-permute-start.16 = (f32[6,64,128]{2,1,0:T(8,128)S(1)}, f32[6,64,128]{2,1,0:T(8,128)S(1)}, u32[]{:S(2)}, u32[]{:S(2)}) collective-permute-start(f32[6,64,128]{2,1,0:T(8,128)S(1)} %get-tuple-element.45), channel_id=1, source_target_pairs={{0,100},{1,101},{2,102},{3,103},{4,96},{5,97},{6,98},{7,99},{8,108... | collective-permute-start | bytes 589832 | tf_op jit(solution)/shard_map/ppermute | solution.py:257
  59.8 1.4 %collective-permute-done.21.refs_3_ = f32[6,64,128]{2,1,0:T(8,128)S(1)} collective-permute-done((f32[6,64,128]{2,1,0:T(8,128)S(1)}, f32[6,64,128]{2,1,0:T(8,128)S(1)}, u32[]{:S(2)}, u32[]{:S(2)}) %collective-permute-start.21) | collective-permute-done | bytes 196640 | tf_op jit(solution)/shard_map/ppermute | solution.py:257
  61.3 1.2 %collective-permute-start.18 = (f32[6,64,128]{2,1,0:T(8,128)S(1)}, f32[6,64,128]{2,1,0:T(8,128)S(1)}, u32[]{:S(2)}, u32[]{:S(2)}) collective-permute-start(f32[6,64,128]{2,1,0:T(8,128)S(1)} %get-tuple-element.47), channel_id=1, source_target_pairs={{0,4},{1,5},{2,6},{3,7},{4,0},{5,1},{6,2},{7,3},{8,12},{9,13},{10,... | collective-permute-start | bytes 589832 | tf_op jit(solution)/shard_map/ppermute | solution.py:257
  62.4 1.5 %shard_map.73.refs_5_ = f32[36,64,128]{2,1,0:T(8,128)} custom-call(s32[54]{0:T(128)S(1)} %get-tuple-element.42.back, f32[6,64,128]{2,1,0:T(8,128)S(1)} %get-tuple-element.48.refs_0_, f32[6,64,128]{2,1,0:T(8,128)S(1)} %collective-permute-done.19.refs_1_, f32[6,64,128]{2,1,0:T(8,128)S(1)} %collective-permute-done.20.refs_2_, ...), custom_call_target="tpu_custom_call" | custom-call | tf_op jit(solution)/shard_map/pallas_call | solution.py:232
  64.0 0.6 collective-permute-done.15.refs_1_
  64.6 3.7 %collective-permute-done.17.refs_3_ = f32[6,64,128]{2,1,0:T(8,128)S(1)} collective-permute-done((f32[6,64,128]{2,1,0:T(8,128)S(1)}, f32[6,64,128]{2,1,0:T(8,128)S(1)}, u32[]{:S(2)}, u32[]{:S(2)}) %collective-permute-start.17) | collective-permute-done | bytes 196640 | tf_op jit(solution)/shard_map/ppermute | solution.py:257
  68.3 1.7 %shard_map.74 = f32[36,64,128]{2,1,0:T(8,128)} custom-call(s32[54]{0:T(128)S(1)} %get-tuple-element.42.back, f32[6,64,128]{2,1,0:T(8,128)S(1)} %collective-permute-done.14.refs_0_, f32[6,64,128]{2,1,0:T(8,128)S(1)} %collective-permute-done.15.refs_1_, f32[6,64,128]{2,1,0:T(8,128)S(1)} %collective-permute-done.16.refs_2_, ...), custom_call_target="tpu_custom_call", output_to_operand_aliasing={{}: (6, {})} | custom-call | tf_op jit(solution)/shard_map/pallas_call | solution.py:232
  (28 shorter events, 0.4 us)
Async XLA Ops:
  1.3 20.9 %copy-start.1 = (s32[1,27,2]{1,2,0:T(2,128)S(1)}, s32[1,27,2]{1,2,0:T(2,128)}, u32[]{:S(2)}) copy-start(s32[1,27,2]{1,2,0:T(2,128)} %param.9) | copy-start | bytes 652
  7.3 8.0 %collective-permute-start = (f32[6,64,128]{2,1,0:T(8,128)S(1)}, f32[6,64,128]{2,1,0:T(8,128)S(1)}, u32[]{:S(2)}, u32[]{:S(2)}) collective-permute-start(f32[6,64,128]{2,1,0:T(8,128)S(1)} %get-tuple-element.27), channel_id=1, source_target_pairs={{0,4},{1,5},{2,6},{3,7},{4,0},{5,1},{6,2},{7,3},{8,12},{9,13},{10,... | collective-permute-start | bytes 589832 | tf_op jit(solution)/shard_map/ppermute | solution.py:257
  8.8 8.5 %collective-permute-start.1 = (f32[6,64,128]{2,1,0:T(8,128)S(1)}, f32[6,64,128]{2,1,0:T(8,128)S(1)}, u32[]{:S(2)}, u32[]{:S(2)}) collective-permute-start(f32[6,64,128]{2,1,0:T(8,128)S(1)} %get-tuple-element.29), channel_id=1, source_target_pairs={{0,32},{1,33},{2,34},{3,35},{4,36},{5,37},{6,38},{7,39},{8,40},{9,... | collective-permute-start | bytes 589832 | tf_op jit(solution)/shard_map/ppermute | solution.py:257
  10.2 8.3 %collective-permute-start.2 = (f32[6,64,128]{2,1,0:T(8,128)S(1)}, f32[6,64,128]{2,1,0:T(8,128)S(1)}, u32[]{:S(2)}, u32[]{:S(2)}) collective-permute-start(f32[6,64,128]{2,1,0:T(8,128)S(1)} %get-tuple-element.30), channel_id=1, source_target_pairs={{0,96},{1,97},{2,98},{3,99},{4,100},{5,101},{6,102},{7,103},{8,104... | collective-permute-start | bytes 589832 | tf_op jit(solution)/shard_map/ppermute | solution.py:257
  11.5 10.7 %collective-permute-start.3 = (f32[6,64,128]{2,1,0:T(8,128)S(1)}, f32[6,64,128]{2,1,0:T(8,128)S(1)}, u32[]{:S(2)}, u32[]{:S(2)}) collective-permute-start(f32[6,64,128]{2,1,0:T(8,128)S(1)} %get-tuple-element.31), channel_id=1, source_target_pairs={{0,60},{1,61},{2,62},{3,63},{4,40},{5,41},{6,42},{7,43},{8,36},{9,... | collective-permute-start | bytes 589832 | tf_op jit(solution)/shard_map/ppermute | solution.py:257
  13.1 12.9 %collective-permute-start.4 = (f32[6,64,128]{2,1,0:T(8,128)S(1)}, f32[6,64,128]{2,1,0:T(8,128)S(1)}, u32[]{:S(2)}, u32[]{:S(2)}) collective-permute-start(f32[6,64,128]{2,1,0:T(8,128)S(1)} %get-tuple-element.32), channel_id=1, source_target_pairs={{0,124},{1,125},{2,126},{3,127},{4,104},{5,105},{6,106},{7,107},{8... | collective-permute-start | bytes 589832 | tf_op jit(solution)/shard_map/ppermute | solution.py:257
  15.4 10.6 %collective-permute-start.5 = (f32[6,64,128]{2,1,0:T(8,128)S(1)}, f32[6,64,128]{2,1,0:T(8,128)S(1)}, u32[]{:S(2)}, u32[]{:S(2)}) collective-permute-start(f32[6,64,128]{2,1,0:T(8,128)S(1)} %get-tuple-element.33), channel_id=1, source_target_pairs={{0,28},{1,29},{2,30},{3,31},{4,8},{5,9},{6,10},{7,11},{8,4},{9,5},... | collective-permute-start | bytes 589832 | tf_op jit(solution)/shard_map/ppermute | solution.py:257
  17.3 8.7 %collective-permute-start.6 = (f32[6,64,128]{2,1,0:T(8,128)S(1)}, f32[6,64,128]{2,1,0:T(8,128)S(1)}, u32[]{:S(2)}, u32[]{:S(2)}) collective-permute-start(f32[6,64,128]{2,1,0:T(8,128)S(1)} %get-tuple-element.34), channel_id=1, source_target_pairs={{0,36},{1,37},{2,38},{3,39},{4,32},{5,33},{6,34},{7,35},{8,44},{9,... | collective-permute-start | bytes 589832 | tf_op jit(solution)/shard_map/ppermute | solution.py:257
  18.5 7.5 %collective-permute-start.7 = (f32[6,64,128]{2,1,0:T(8,128)S(1)}, f32[6,64,128]{2,1,0:T(8,128)S(1)}, u32[]{:S(2)}, u32[]{:S(2)}) collective-permute-start(f32[6,64,128]{2,1,0:T(8,128)S(1)} %get-tuple-element.35), channel_id=1, source_target_pairs={{0,100},{1,101},{2,102},{3,103},{4,96},{5,97},{6,98},{7,99},{8,108... | collective-permute-start | bytes 589832 | tf_op jit(solution)/shard_map/ppermute | solution.py:257
  22.3 4.5 %collective-permute-start.9 = (s32[2,27]{1,0:T(2,128)S(1)}, s32[2,27]{1,0:T(2,128)S(1)}, u32[]{:S(2)}, u32[]{:S(2)}) collective-permute-start(s32[2,27]{1,0:T(2,128)S(1)} %bitcast.4), channel_id=1, source_target_pairs={{0,3},{1,0},{2,1},{3,2},{4,7},{5,4},{6,5},{7,6},{8,11},{9,8},{10,9... | collective-permute-start | bytes 656 | tf_op jit(solution)/shard_map/ppermute | solution.py:257
  26.0 3.6 %collective-permute-start.8 = (s32[2,27]{1,0:T(2,128)S(1)}, s32[2,27]{1,0:T(2,128)S(1)}, u32[]{:S(2)}, u32[]{:S(2)}) collective-permute-start(s32[2,27]{1,0:T(2,128)S(1)} %bitcast.5), channel_id=1, source_target_pairs={{0,1},{1,2},{2,3},{3,0},{4,5},{5,6},{6,7},{7,4},{8,9},{9,10},{10,1... | collective-permute-start | bytes 656 | tf_op jit(solution)/shard_map/ppermute | solution.py:257
  30.5 6.5 %collective-permute-start.10 = (f32[8,64,128]{2,1,0:T(8,128)S(1)}, f32[8,64,128]{2,1,0:T(8,128)S(1)}, u32[]{:S(2)}, u32[]{:S(2)}) collective-permute-start(f32[8,64,128]{2,1,0:T(8,128)S(1)} %get-tuple-element.39), channel_id=1, source_target_pairs={{0,1},{1,2},{2,3},{3,0},{4,5},{5,6},{6,7},{7,4},{8,9},{9,10},{10,1... | collective-permute-start | bytes 786440 | tf_op jit(solution)/shard_map/ppermute | solution.py:257
  30.6 6.5 %collective-permute-start.11 = (f32[8,64,128]{2,1,0:T(8,128)S(1)}, f32[8,64,128]{2,1,0:T(8,128)S(1)}, u32[]{:S(2)}, u32[]{:S(2)}) collective-permute-start(f32[8,64,128]{2,1,0:T(8,128)S(1)} %get-tuple-element.40), channel_id=1, source_target_pairs={{0,3},{1,0},{2,1},{3,2},{4,7},{5,4},{6,5},{7,6},{8,11},{9,8},{10,9... | collective-permute-start | bytes 786440 | tf_op jit(solution)/shard_map/ppermute | solution.py:257
  37.0 6.5 %collective-permute-start.12 = (f32[8,64,128]{2,1,0:T(8,128)S(1)}, f32[8,64,128]{2,1,0:T(8,128)S(1)}, u32[]{:S(2)}, u32[]{:S(2)}) collective-permute-start(f32[8,64,128]{2,1,0:T(8,128)S(1)} %add.19), channel_id=1, source_target_pairs={{0,1},{1,2},{2,3},{3,0},{4,5},{5,6},{6,7},{7,4},{8,9},{9,10},{10,1... | collective-permute-start | bytes 786440 | tf_op jit(solution)/shard_map/ppermute | solution.py:257
  37.2 8.9 %copy-start = (f32[8,64,128]{2,1,0:T(8,128)}, f32[8,64,128]{2,1,0:T(8,128)S(1)}, u32[]{:S(2)}) copy-start(f32[8,64,128]{2,1,0:T(8,128)S(1)} %get-tuple-element.53.refs_4_) | copy-start | bytes 786436
  37.2 6.4 %collective-permute-start.13 = (f32[8,64,128]{2,1,0:T(8,128)S(1)}, f32[8,64,128]{2,1,0:T(8,128)S(1)}, u32[]{:S(2)}, u32[]{:S(2)}) collective-permute-start(f32[8,64,128]{2,1,0:T(8,128)S(1)} %get-tuple-element.52), channel_id=1, source_target_pairs={{0,3},{1,0},{2,1},{3,2},{4,7},{5,4},{6,5},{7,6},{8,11},{9,8},{10,9... | collective-permute-start | bytes 786440 | tf_op jit(solution)/shard_map/ppermute | solution.py:257
  44.2 13.2 %collective-permute-start.19 = (f32[6,64,128]{2,1,0:T(8,128)S(1)}, f32[6,64,128]{2,1,0:T(8,128)S(1)}, u32[]{:S(2)}, u32[]{:S(2)}) collective-permute-start(f32[6,64,128]{2,1,0:T(8,128)S(1)} %get-tuple-element.49), channel_id=1, source_target_pairs={{0,96},{1,97},{2,98},{3,99},{4,100},{5,101},{6,102},{7,103},{8,104... | collective-permute-start | bytes 589832 | tf_op jit(solution)/shard_map/ppermute | solution.py:257
  46.1 13.8 %collective-permute-start.20 = (f32[6,64,128]{2,1,0:T(8,128)S(1)}, f32[6,64,128]{2,1,0:T(8,128)S(1)}, u32[]{:S(2)}, u32[]{:S(2)}) collective-permute-start(f32[6,64,128]{2,1,0:T(8,128)S(1)} %get-tuple-element.50), channel_id=1, source_target_pairs={{0,32},{1,33},{2,34},{3,35},{4,36},{5,37},{6,38},{7,39},{8,40},{9,... | collective-permute-start | bytes 589832 | tf_op jit(solution)/shard_map/ppermute | solution.py:257
  46.8 14.5 %collective-permute-start.21 = (f32[6,64,128]{2,1,0:T(8,128)S(1)}, f32[6,64,128]{2,1,0:T(8,128)S(1)}, u32[]{:S(2)}, u32[]{:S(2)}) collective-permute-start(f32[6,64,128]{2,1,0:T(8,128)S(1)} %get-tuple-element.51), channel_id=1, source_target_pairs={{0,124},{1,125},{2,126},{3,127},{4,104},{5,105},{6,106},{7,107},{8... | collective-permute-start | bytes 589832 | tf_op jit(solution)/shard_map/ppermute | solution.py:257
  56.2 7.8 %collective-permute-start.14 = (f32[6,64,128]{2,1,0:T(8,128)S(1)}, f32[6,64,128]{2,1,0:T(8,128)S(1)}, u32[]{:S(2)}, u32[]{:S(2)}) collective-permute-start(f32[6,64,128]{2,1,0:T(8,128)S(1)} %get-tuple-element.43), channel_id=1, source_target_pairs={{0,60},{1,61},{2,62},{3,63},{4,40},{5,41},{6,42},{7,43},{8,36},{9,... | collective-permute-start | bytes 589832 | tf_op jit(solution)/shard_map/ppermute | solution.py:257
  56.2 8.4 %collective-permute-start.15 = (f32[6,64,128]{2,1,0:T(8,128)S(1)}, f32[6,64,128]{2,1,0:T(8,128)S(1)}, u32[]{:S(2)}, u32[]{:S(2)}) collective-permute-start(f32[6,64,128]{2,1,0:T(8,128)S(1)} %get-tuple-element.44), channel_id=1, source_target_pairs={{0,28},{1,29},{2,30},{3,31},{4,8},{5,9},{6,10},{7,11},{8,4},{9,5},... | collective-permute-start | bytes 589832 | tf_op jit(solution)/shard_map/ppermute | solution.py:257
  57.5 7.1 %collective-permute-start.16 = (f32[6,64,128]{2,1,0:T(8,128)S(1)}, f32[6,64,128]{2,1,0:T(8,128)S(1)}, u32[]{:S(2)}, u32[]{:S(2)}) collective-permute-start(f32[6,64,128]{2,1,0:T(8,128)S(1)} %get-tuple-element.45), channel_id=1, source_target_pairs={{0,100},{1,101},{2,102},{3,103},{4,96},{5,97},{6,98},{7,99},{8,108... | collective-permute-start | bytes 589832 | tf_op jit(solution)/shard_map/ppermute | solution.py:257
  59.8 8.5 %collective-permute-start.17 = (f32[6,64,128]{2,1,0:T(8,128)S(1)}, f32[6,64,128]{2,1,0:T(8,128)S(1)}, u32[]{:S(2)}, u32[]{:S(2)}) collective-permute-start(f32[6,64,128]{2,1,0:T(8,128)S(1)} %get-tuple-element.46), channel_id=1, source_target_pairs={{0,36},{1,37},{2,38},{3,39},{4,32},{5,33},{6,34},{7,35},{8,44},{9,... | collective-permute-start | bytes 589832 | tf_op jit(solution)/shard_map/ppermute | solution.py:257
  61.3 7.1 %collective-permute-start.18 = (f32[6,64,128]{2,1,0:T(8,128)S(1)}, f32[6,64,128]{2,1,0:T(8,128)S(1)}, u32[]{:S(2)}, u32[]{:S(2)}) collective-permute-start(f32[6,64,128]{2,1,0:T(8,128)S(1)} %get-tuple-element.47), channel_id=1, source_target_pairs={{0,4},{1,5},{2,6},{3,7},{4,0},{5,1},{6,2},{7,3},{8,12},{9,13},{10,... | collective-permute-start | bytes 589832 | tf_op jit(solution)/shard_map/ppermute | solution.py:257

commit v5 on v4

--- a/solution.py
+++ b/solution.py
@@ -13,7 +13,7 @@
 SMEM = pltpu.SMEM
 
 SIDE, LAST = 0, 2
-PLANE = [(1, 0), (-1, 0), (1, 2), (-1, 2), (0, 2), (1, 1), (-1, 1), (0, 1), (0, 0)]
+PLANE = [(1, 0), (-1, 0), (1, 2), (-1, 2), (1, 1), (-1, 1), (0, 2), (0, 1), (0, 0)]
 HOME = len(PLANE) - 1
 OUT_ORDER = list(range(8))
 BACK_ORDER = list(range(8))

time: 70.2 us -> 69 us (0.983)
  waiting for transfers between devices: 17 us -> 15.4 us
    ppermute x22, waiting for transfers between devices: 17 us -> 15.4 us  [move(): return lax.ppermute(array, AXES, pairs)]
  transfers between devices with their start and end apart: 22 -> 22, of which waited for: 8 -> 9; matrix products, arithmetic and copies ran while one was open for 0% -> 0% of each run, Pallas kernels for 6% -> 6%
where the time goes in v5:
time: 69 us; the launch traced here: 68.9 us
  starting transfers between devices  38.7 us (56%)
  waiting for transfers between devices  15.4 us (22%)
  Pallas kernels  13.1 us (19%)
  other arithmetic  0.87 us (1%)
  between operations  0.77 us (1%)
    ppermute x22, starting transfers between devices, move(): return lax.ppermute(array, AXES, pairs)  38.7 us
    ppermute x22, waiting for transfers between devices, move(): return lax.ppermute(array, AXES, pairs)  15.4 us
    pallas_call x1, Pallas kernels, contribute(): pl.pallas_call(functools.partial(contribute_kernel, extents, capacity, bl...  6 us
    pallas_call x2, Pallas kernels, collect(): pl.pallas_call(functools.partial(collect_kernel, capacity, rows, steps),...  3.17 us
    pallas_call x1, Pallas kernels, gather_own(): pl.pallas_call(functools.partial(gather_own_kernel, capacity, extents), i...  1.77 us
  transfers between devices with their start and end apart: 22, of which 9 were waited for; matrix products, arithmetic and copies ran while one was open for 0% of the time, Pallas kernels for 6%

profile of v5, /device:TPU:1, one launch (start us, length us, event | category | flops | bytes accessed | tf_op | source)
XLA Modules:
  0.0 68.9 jit_solution(2490314652707341300)
XLA Ops:
  0.6 0.7 %multiply_add_fusion.key_hbm.key = s32[4,9]{1,0:T(4,128)S(1)} fusion(s32[4,9]{1,0:T(4,128)} %param.8, s32[4,9]{1,0:T(4,128)} %param.7), kind=kLoop, calls=%fused_computation | loop fusion | flops 72 | bytes 432 | tf_op jit(solution)/shard_map/add | solution.py:264
  1.3 6.0 %shard_map.68 = (f32[6,64,128]{2,1,0:T(8,128)S(1)}, f32[6,64,128]{2,1,0:T(8,128)S(1)}, f32[6,64,128]{2,1,0:T(8,128)S(1)}, f32[6,64,128]{2,1,0:T(8,128)S(1)}, f32...) custom-call(s32[4,9]{1,0:T(4,128)S(1)} %multiply_add_fusion.key_hbm., ...), custom_call_target="tpu_custom_call" | custom-call | tf_op jit(solution)/shard_map/pallas_call | solution.py:103
  7.3 1.5 %collective-permute-start = (f32[6,64,128]{2,1,0:T(8,128)S(1)}, f32[6,64,128]{2,1,0:T(8,128)S(1)}, u32[]{:S(2)}, u32[]{:S(2)}) collective-permute-start(f32[6,64,128]{2,1,0:T(8,128)S(1)} %get-tuple-element.27), channel_id=1, source_target_pairs={{0,4},{1,5},{2,6},{3,7},{4,0},{5,1},{6,2},{7,3},{8,12},{9,13},{10,... | collective-permute-start | bytes 589832 | tf_op jit(solution)/shard_map/ppermute | solution.py:257
  8.8 1.3 %collective-permute-start.1 = (f32[6,64,128]{2,1,0:T(8,128)S(1)}, f32[6,64,128]{2,1,0:T(8,128)S(1)}, u32[]{:S(2)}, u32[]{:S(2)}) collective-permute-start(f32[6,64,128]{2,1,0:T(8,128)S(1)} %get-tuple-element.29), channel_id=1, source_target_pairs={{0,32},{1,33},{2,34},{3,35},{4,36},{5,37},{6,38},{7,39},{8,40},{9,... | collective-permute-start | bytes 589832 | tf_op jit(solution)/shard_map/ppermute | solution.py:257
  10.2 1.4 %collective-permute-start.2 = (f32[6,64,128]{2,1,0:T(8,128)S(1)}, f32[6,64,128]{2,1,0:T(8,128)S(1)}, u32[]{:S(2)}, u32[]{:S(2)}) collective-permute-start(f32[6,64,128]{2,1,0:T(8,128)S(1)} %get-tuple-element.30), channel_id=1, source_target_pairs={{0,96},{1,97},{2,98},{3,99},{4,100},{5,101},{6,102},{7,103},{8,104... | collective-permute-start | bytes 589832 | tf_op jit(solution)/shard_map/ppermute | solution.py:257
  11.5 1.6 %collective-permute-start.3 = (f32[6,64,128]{2,1,0:T(8,128)S(1)}, f32[6,64,128]{2,1,0:T(8,128)S(1)}, u32[]{:S(2)}, u32[]{:S(2)}) collective-permute-start(f32[6,64,128]{2,1,0:T(8,128)S(1)} %get-tuple-element.31), channel_id=1, source_target_pairs={{0,60},{1,61},{2,62},{3,63},{4,40},{5,41},{6,42},{7,43},{8,36},{9,... | collective-permute-start | bytes 589832 | tf_op jit(solution)/shard_map/ppermute | solution.py:257
  13.1 2.2 %collective-permute-start.4 = (f32[6,64,128]{2,1,0:T(8,128)S(1)}, f32[6,64,128]{2,1,0:T(8,128)S(1)}, u32[]{:S(2)}, u32[]{:S(2)}) collective-permute-start(f32[6,64,128]{2,1,0:T(8,128)S(1)} %get-tuple-element.32), channel_id=1, source_target_pairs={{0,124},{1,125},{2,126},{3,127},{4,104},{5,105},{6,106},{7,107},{8... | collective-permute-start | bytes 589832 | tf_op jit(solution)/shard_map/ppermute | solution.py:257
  15.4 0.6 collective-permute-start.5
  16.0 0.5 collective-permute-done.1.refs_0_.refs_2_
  16.5 2.6 %collective-permute-start.6 = (f32[6,64,128]{2,1,0:T(8,128)S(1)}, f32[6,64,128]{2,1,0:T(8,128)S(1)}, u32[]{:S(2)}, u32[]{:S(2)}) collective-permute-start(f32[6,64,128]{2,1,0:T(8,128)S(1)} %get-tuple-element.34), channel_id=1, source_target_pairs={{0,100},{1,101},{2,102},{3,103},{4,96},{5,97},{6,98},{7,99},{8,108... | collective-permute-start | bytes 589832 | tf_op jit(solution)/shard_map/ppermute | solution.py:257
  19.1 1.2 %collective-permute-start.7 = (f32[6,64,128]{2,1,0:T(8,128)S(1)}, f32[6,64,128]{2,1,0:T(8,128)S(1)}, u32[]{:S(2)}, u32[]{:S(2)}) collective-permute-start(f32[6,64,128]{2,1,0:T(8,128)S(1)} %get-tuple-element.35), channel_id=1, source_target_pairs={{0,28},{1,29},{2,30},{3,31},{4,8},{5,9},{6,10},{7,11},{8,4},{9,5},... | collective-permute-start | bytes 589832 | tf_op jit(solution)/shard_map/ppermute | solution.py:257
  20.3 2.0 %collective-permute-done.3.refs_2_.refs_4_ = f32[6,64,128]{2,1,0:T(8,128)S(1)} collective-permute-done((f32[6,64,128]{2,1,0:T(8,128)S(1)}, f32[6,64,128]{2,1,0:T(8,128)S(1)}, u32[]{:S(2)}, u32[]{:S(2)}) %collective-permute-start.3) | collective-permute-done | bytes 196640 | tf_op jit(solution)/shard_map/ppermute | solution.py:257
  22.2 3.7 %collective-permute-start.9 = (s32[2,27]{1,0:T(2,128)S(1)}, s32[2,27]{1,0:T(2,128)S(1)}, u32[]{:S(2)}, u32[]{:S(2)}) collective-permute-start(s32[2,27]{1,0:T(2,128)S(1)} %bitcast.4), channel_id=1, source_target_pairs={{0,3},{1,0},{2,1},{3,2},{4,7},{5,4},{6,5},{7,6},{8,11},{9,8},{10,9... | collective-permute-start | bytes 656 | tf_op jit(solution)/shard_map/ppermute | solution.py:257
  26.0 0.7 %collective-permute-done.9.refs_1_.refs_2_ = s32[2,27]{1,0:T(2,128)S(1)} collective-permute-done((s32[2,27]{1,0:T(2,128)S(1)}, s32[2,27]{1,0:T(2,128)S(1)}, u32[]{:S(2)}, u32[]{:S(2)}) %collective-permute-start.9) | collective-permute-done | bytes 248 | tf_op jit(solution)/shard_map/ppermute | solution.py:257
  26.7 2.9 %collective-permute-done.8.refs_0_ = s32[2,27]{1,0:T(2,128)S(1)} collective-permute-done((s32[2,27]{1,0:T(2,128)S(1)}, s32[2,27]{1,0:T(2,128)S(1)}, u32[]{:S(2)}, u32[]{:S(2)}) %collective-permute-start.8) | collective-permute-done | bytes 248 | tf_op jit(solution)/shard_map/ppermute | solution.py:257
  29.6 0.8 %shard_map.70 = (f32[8,64,128]{2,1,0:T(8,128)S(1)}, f32[8,64,128]{2,1,0:T(8,128)S(1)}) custom-call(s32[2,27]{1,0:T(2,128)S(1)} %collective-permute-done.8.refs_0_, s32[2,27]{1,0:T(2,128)S(1)} %collective-permute-done.9.refs_1_.refs_2_, f32[6,64,128]{2,1,0:T(8,128)S(1)} %collective-permute-done.1.refs_0_.refs_2_, ...), custom_call_target="tpu_custom_call" | custom-call | tf_op jit(solution)/shard_map/pallas_call | solution.py:178
  30.5 2.7 %collective-permute-start.11 = (f32[8,64,128]{2,1,0:T(8,128)S(1)}, f32[8,64,128]{2,1,0:T(8,128)S(1)}, u32[]{:S(2)}, u32[]{:S(2)}) collective-permute-start(f32[8,64,128]{2,1,0:T(8,128)S(1)} %get-tuple-element.40), channel_id=1, source_target_pairs={{0,3},{1,0},{2,1},{3,2},{4,7},{5,4},{6,5},{7,6},{8,11},{9,8},{10,9... | collective-permute-start | bytes 786440 | tf_op jit(solution)/shard_map/ppermute | solution.py:257
  33.2 1.8 %shard_map.69 = (f32[8,64,128]{2,1,0:T(8,128)S(1)}, s32[54]{0:T(128)S(1)}) custom-call(s32[4,9]{1,0:T(4,128)S(1)} %multiply_add_fusion.key_hbm.key, s32[2,27]{1,0:T(2,128)S(1)} %bitcast.6, f32[6,64,128]{2,1,0:T(8,128)S(1)} %collective-permute-done.1.refs_0_.refs_2_, f32[6,64,128]{2,1,0:T(8,128)S(1)} %collective-permute-done.2.refs_1_.refs_3_, ...), custom_call_target="tpu_custom_call" | custom-call | tf_op jit(solution)/shard_map/pallas_call | solution.py:147
  35.0 2.0 %collective-permute-done.10 = f32[8,64,128]{2,1,0:T(8,128)S(1)} collective-permute-done((f32[8,64,128]{2,1,0:T(8,128)S(1)}, f32[8,64,128]{2,1,0:T(8,128)S(1)}, u32[]{:S(2)}, u32[]{:S(2)}) %collective-permute-start.10) | collective-permute-done | bytes 262176 | tf_op jit(solution)/shard_map/ppermute | solution.py:257
  37.2 2.7 %collective-permute-start.13 = (f32[8,64,128]{2,1,0:T(8,128)S(1)}, f32[8,64,128]{2,1,0:T(8,128)S(1)}, u32[]{:S(2)}, u32[]{:S(2)}) collective-permute-start(f32[8,64,128]{2,1,0:T(8,128)S(1)} %get-tuple-element.52), channel_id=1, source_target_pairs={{0,3},{1,0},{2,1},{3,2},{4,7},{5,4},{6,5},{7,6},{8,11},{9,8},{10,9... | collective-permute-start | bytes 786440 | tf_op jit(solution)/shard_map/ppermute | solution.py:257
  39.9 3.6 %collective-permute-done.12 = f32[8,64,128]{2,1,0:T(8,128)S(1)} collective-permute-done((f32[8,64,128]{2,1,0:T(8,128)S(1)}, f32[8,64,128]{2,1,0:T(8,128)S(1)}, u32[]{:S(2)}, u32[]{:S(2)}) %collective-permute-start.12) | collective-permute-done | bytes 262176 | tf_op jit(solution)/shard_map/ppermute | solution.py:257
  43.6 0.6 shard_map.72
  44.2 1.9 %collective-permute-start.19 = (f32[6,64,128]{2,1,0:T(8,128)S(1)}, f32[6,64,128]{2,1,0:T(8,128)S(1)}, u32[]{:S(2)}, u32[]{:S(2)}) collective-permute-start(f32[6,64,128]{2,1,0:T(8,128)S(1)} %get-tuple-element.49), channel_id=1, source_target_pairs={{0,96},{1,97},{2,98},{3,99},{4,100},{5,101},{6,102},{7,103},{8,104... | collective-permute-start | bytes 589832 | tf_op jit(solution)/shard_map/ppermute | solution.py:257
  46.1 0.7 %shard_map.71 = (f32[6,64,128]{2,1,0:T(8,128)S(1)}, f32[6,64,128]{2,1,0:T(8,128)S(1)}, f32[6,64,128]{2,1,0:T(8,128)S(1)}, f32[6,64,128]{2,1,0:T(8,128)S(1)}, f32...) custom-call(s32[2,27]{1,0:T(2,128)S(1)} %collective-permute-done.8.refs_0_, ...), custom_call_target="tpu_custom_call" | custom-call | tf_op jit(solution)/shard_map/pallas_call | solution.py:202
  46.8 10.1 %collective-permute-start.21 = (f32[6,64,128]{2,1,0:T(8,128)S(1)}, f32[6,64,128]{2,1,0:T(8,128)S(1)}, u32[]{:S(2)}, u32[]{:S(2)}) collective-permute-start(f32[6,64,128]{2,1,0:T(8,128)S(1)} %get-tuple-element.51), channel_id=1, source_target_pairs={{0,124},{1,125},{2,126},{3,127},{4,104},{5,105},{6,106},{7,107},{8... | collective-permute-start | bytes 589832 | tf_op jit(solution)/shard_map/ppermute | solution.py:257
  56.8 2.9 %collective-permute-start.15 = (f32[6,64,128]{2,1,0:T(8,128)S(1)}, f32[6,64,128]{2,1,0:T(8,128)S(1)}, u32[]{:S(2)}, u32[]{:S(2)}) collective-permute-start(f32[6,64,128]{2,1,0:T(8,128)S(1)} %get-tuple-element.44), channel_id=1, source_target_pairs={{0,100},{1,101},{2,102},{3,103},{4,96},{5,97},{6,98},{7,99},{8,108... | collective-permute-start | bytes 589832 | tf_op jit(solution)/shard_map/ppermute | solution.py:257
  59.8 0.8 %collective-permute-start.17 = (f32[6,64,128]{2,1,0:T(8,128)S(1)}, f32[6,64,128]{2,1,0:T(8,128)S(1)}, u32[]{:S(2)}, u32[]{:S(2)}) collective-permute-start(f32[6,64,128]{2,1,0:T(8,128)S(1)} %get-tuple-element.46), channel_id=1, source_target_pairs={{0,28},{1,29},{2,30},{3,31},{4,8},{5,9},{6,10},{7,11},{8,4},{9,5},... | collective-permute-start | bytes 589832 | tf_op jit(solution)/shard_map/ppermute | solution.py:257
  60.8 1.4 %collective-permute-start.18 = (f32[6,64,128]{2,1,0:T(8,128)S(1)}, f32[6,64,128]{2,1,0:T(8,128)S(1)}, u32[]{:S(2)}, u32[]{:S(2)}) collective-permute-start(f32[6,64,128]{2,1,0:T(8,128)S(1)} %get-tuple-element.47), channel_id=1, source_target_pairs={{0,4},{1,5},{2,6},{3,7},{4,0},{5,1},{6,2},{7,3},{8,12},{9,13},{10,... | collective-permute-start | bytes 589832 | tf_op jit(solution)/shard_map/ppermute | solution.py:257
  62.2 1.6 %shard_map.73.refs_5_ = f32[36,64,128]{2,1,0:T(8,128)} custom-call(s32[54]{0:T(128)S(1)} %get-tuple-element.42.back, f32[6,64,128]{2,1,0:T(8,128)S(1)} %get-tuple-element.48.refs_0_, f32[6,64,128]{2,1,0:T(8,128)S(1)} %collective-permute-done.19.refs_1_, f32[6,64,128]{2,1,0:T(8,128)S(1)} %collective-permute-done.20.refs_2_, ...), custom_call_target="tpu_custom_call" | custom-call | tf_op jit(solution)/shard_map/pallas_call | solution.py:232
  63.8 2.3 %collective-permute-done.14.refs_0_ = f32[6,64,128]{2,1,0:T(8,128)S(1)} collective-permute-done((f32[6,64,128]{2,1,0:T(8,128)S(1)}, f32[6,64,128]{2,1,0:T(8,128)S(1)}, u32[]{:S(2)}, u32[]{:S(2)}) %collective-permute-start.14) | collective-permute-done | bytes 196640 | tf_op jit(solution)/shard_map/ppermute | solution.py:257
  66.1 1.2 %collective-permute-done.16.refs_2_ = f32[6,64,128]{2,1,0:T(8,128)S(1)} collective-permute-done((f32[6,64,128]{2,1,0:T(8,128)S(1)}, f32[6,64,128]{2,1,0:T(8,128)S(1)}, u32[]{:S(2)}, u32[]{:S(2)}) %collective-permute-start.16) | collective-permute-done | bytes 196640 | tf_op jit(solution)/shard_map/ppermute | solution.py:257
  67.3 1.6 %shard_map.74 = f32[36,64,128]{2,1,0:T(8,128)} custom-call(s32[54]{0:T(128)S(1)} %get-tuple-element.42.back, f32[6,64,128]{2,1,0:T(8,128)S(1)} %collective-permute-done.14.refs_0_, f32[6,64,128]{2,1,0:T(8,128)S(1)} %collective-permute-done.15.refs_1_, f32[6,64,128]{2,1,0:T(8,128)S(1)} %collective-permute-done.16.refs_2_, ...), custom_call_target="tpu_custom_call", output_to_operand_aliasing={{}: (6, {})} | custom-call | tf_op jit(solution)/shard_map/pallas_call | solution.py:232
  (28 shorter events, 0.6 us)
Async XLA Ops:
  1.3 20.9 %copy-start.1 = (s32[1,27,2]{1,2,0:T(2,128)S(1)}, s32[1,27,2]{1,2,0:T(2,128)}, u32[]{:S(2)}) copy-start(s32[1,27,2]{1,2,0:T(2,128)} %param.9) | copy-start | bytes 652
  7.3 8.0 %collective-permute-start = (f32[6,64,128]{2,1,0:T(8,128)S(1)}, f32[6,64,128]{2,1,0:T(8,128)S(1)}, u32[]{:S(2)}, u32[]{:S(2)}) collective-permute-start(f32[6,64,128]{2,1,0:T(8,128)S(1)} %get-tuple-element.27), channel_id=1, source_target_pairs={{0,4},{1,5},{2,6},{3,7},{4,0},{5,1},{6,2},{7,3},{8,12},{9,13},{10,... | collective-permute-start | bytes 589832 | tf_op jit(solution)/shard_map/ppermute | solution.py:257
  8.8 7.7 %collective-permute-start.1 = (f32[6,64,128]{2,1,0:T(8,128)S(1)}, f32[6,64,128]{2,1,0:T(8,128)S(1)}, u32[]{:S(2)}, u32[]{:S(2)}) collective-permute-start(f32[6,64,128]{2,1,0:T(8,128)S(1)} %get-tuple-element.29), channel_id=1, source_target_pairs={{0,32},{1,33},{2,34},{3,35},{4,36},{5,37},{6,38},{7,39},{8,40},{9,... | collective-permute-start | bytes 589832 | tf_op jit(solution)/shard_map/ppermute | solution.py:257
  10.2 8.9 %collective-permute-start.2 = (f32[6,64,128]{2,1,0:T(8,128)S(1)}, f32[6,64,128]{2,1,0:T(8,128)S(1)}, u32[]{:S(2)}, u32[]{:S(2)}) collective-permute-start(f32[6,64,128]{2,1,0:T(8,128)S(1)} %get-tuple-element.30), channel_id=1, source_target_pairs={{0,96},{1,97},{2,98},{3,99},{4,100},{5,101},{6,102},{7,103},{8,104... | collective-permute-start | bytes 589832 | tf_op jit(solution)/shard_map/ppermute | solution.py:257
  11.5 10.7 %collective-permute-start.3 = (f32[6,64,128]{2,1,0:T(8,128)S(1)}, f32[6,64,128]{2,1,0:T(8,128)S(1)}, u32[]{:S(2)}, u32[]{:S(2)}) collective-permute-start(f32[6,64,128]{2,1,0:T(8,128)S(1)} %get-tuple-element.31), channel_id=1, source_target_pairs={{0,60},{1,61},{2,62},{3,63},{4,40},{5,41},{6,42},{7,43},{8,36},{9,... | collective-permute-start | bytes 589832 | tf_op jit(solution)/shard_map/ppermute | solution.py:257
  13.1 12.9 %collective-permute-start.4 = (f32[6,64,128]{2,1,0:T(8,128)S(1)}, f32[6,64,128]{2,1,0:T(8,128)S(1)}, u32[]{:S(2)}, u32[]{:S(2)}) collective-permute-start(f32[6,64,128]{2,1,0:T(8,128)S(1)} %get-tuple-element.32), channel_id=1, source_target_pairs={{0,124},{1,125},{2,126},{3,127},{4,104},{5,105},{6,106},{7,107},{8... | collective-permute-start | bytes 589832 | tf_op jit(solution)/shard_map/ppermute | solution.py:257
  15.4 10.6 %collective-permute-start.5 = (f32[6,64,128]{2,1,0:T(8,128)S(1)}, f32[6,64,128]{2,1,0:T(8,128)S(1)}, u32[]{:S(2)}, u32[]{:S(2)}) collective-permute-start(f32[6,64,128]{2,1,0:T(8,128)S(1)} %get-tuple-element.33), channel_id=1, source_target_pairs={{0,36},{1,37},{2,38},{3,39},{4,32},{5,33},{6,34},{7,35},{8,44},{9,... | collective-permute-start | bytes 589832 | tf_op jit(solution)/shard_map/ppermute | solution.py:257
  16.5 9.5 %collective-permute-start.6 = (f32[6,64,128]{2,1,0:T(8,128)S(1)}, f32[6,64,128]{2,1,0:T(8,128)S(1)}, u32[]{:S(2)}, u32[]{:S(2)}) collective-permute-start(f32[6,64,128]{2,1,0:T(8,128)S(1)} %get-tuple-element.34), channel_id=1, source_target_pairs={{0,100},{1,101},{2,102},{3,103},{4,96},{5,97},{6,98},{7,99},{8,108... | collective-permute-start | bytes 589832 | tf_op jit(solution)/shard_map/ppermute | solution.py:257
  19.1 6.9 %collective-permute-start.7 = (f32[6,64,128]{2,1,0:T(8,128)S(1)}, f32[6,64,128]{2,1,0:T(8,128)S(1)}, u32[]{:S(2)}, u32[]{:S(2)}) collective-permute-start(f32[6,64,128]{2,1,0:T(8,128)S(1)} %get-tuple-element.35), channel_id=1, source_target_pairs={{0,28},{1,29},{2,30},{3,31},{4,8},{5,9},{6,10},{7,11},{8,4},{9,5},... | collective-permute-start | bytes 589832 | tf_op jit(solution)/shard_map/ppermute | solution.py:257
  22.2 4.5 %collective-permute-start.9 = (s32[2,27]{1,0:T(2,128)S(1)}, s32[2,27]{1,0:T(2,128)S(1)}, u32[]{:S(2)}, u32[]{:S(2)}) collective-permute-start(s32[2,27]{1,0:T(2,128)S(1)} %bitcast.4), channel_id=1, source_target_pairs={{0,3},{1,0},{2,1},{3,2},{4,7},{5,4},{6,5},{7,6},{8,11},{9,8},{10,9... | collective-permute-start | bytes 656 | tf_op jit(solution)/shard_map/ppermute | solution.py:257
  26.0 3.6 %collective-permute-start.8 = (s32[2,27]{1,0:T(2,128)S(1)}, s32[2,27]{1,0:T(2,128)S(1)}, u32[]{:S(2)}, u32[]{:S(2)}) collective-permute-start(s32[2,27]{1,0:T(2,128)S(1)} %bitcast.5), channel_id=1, source_target_pairs={{0,1},{1,2},{2,3},{3,0},{4,5},{5,6},{6,7},{7,4},{8,9},{9,10},{10,1... | collective-permute-start | bytes 656 | tf_op jit(solution)/shard_map/ppermute | solution.py:257
  30.5 6.5 %collective-permute-start.10 = (f32[8,64,128]{2,1,0:T(8,128)S(1)}, f32[8,64,128]{2,1,0:T(8,128)S(1)}, u32[]{:S(2)}, u32[]{:S(2)}) collective-permute-start(f32[8,64,128]{2,1,0:T(8,128)S(1)} %get-tuple-element.39), channel_id=1, source_target_pairs={{0,1},{1,2},{2,3},{3,0},{4,5},{5,6},{6,7},{7,4},{8,9},{9,10},{10,1... | collective-permute-start | bytes 786440 | tf_op jit(solution)/shard_map/ppermute | solution.py:257
  30.5 6.5 %collective-permute-start.11 = (f32[8,64,128]{2,1,0:T(8,128)S(1)}, f32[8,64,128]{2,1,0:T(8,128)S(1)}, u32[]{:S(2)}, u32[]{:S(2)}) collective-permute-start(f32[8,64,128]{2,1,0:T(8,128)S(1)} %get-tuple-element.40), channel_id=1, source_target_pairs={{0,3},{1,0},{2,1},{3,2},{4,7},{5,4},{6,5},{7,6},{8,11},{9,8},{10,9... | collective-permute-start | bytes 786440 | tf_op jit(solution)/shard_map/ppermute | solution.py:257
  37.0 6.5 %collective-permute-start.12 = (f32[8,64,128]{2,1,0:T(8,128)S(1)}, f32[8,64,128]{2,1,0:T(8,128)S(1)}, u32[]{:S(2)}, u32[]{:S(2)}) collective-permute-start(f32[8,64,128]{2,1,0:T(8,128)S(1)} %add.19), channel_id=1, source_target_pairs={{0,1},{1,2},{2,3},{3,0},{4,5},{5,6},{6,7},{7,4},{8,9},{9,10},{10,1... | collective-permute-start | bytes 786440 | tf_op jit(solution)/shard_map/ppermute | solution.py:257
  37.2 8.9 %copy-start = (f32[8,64,128]{2,1,0:T(8,128)}, f32[8,64,128]{2,1,0:T(8,128)S(1)}, u32[]{:S(2)}) copy-start(f32[8,64,128]{2,1,0:T(8,128)S(1)} %get-tuple-element.53.refs_4_) | copy-start | bytes 786436
  37.2 6.4 %collective-permute-start.13 = (f32[8,64,128]{2,1,0:T(8,128)S(1)}, f32[8,64,128]{2,1,0:T(8,128)S(1)}, u32[]{:S(2)}, u32[]{:S(2)}) collective-permute-start(f32[8,64,128]{2,1,0:T(8,128)S(1)} %get-tuple-element.52), channel_id=1, source_target_pairs={{0,3},{1,0},{2,1},{3,2},{4,7},{5,4},{6,5},{7,6},{8,11},{9,8},{10,9... | collective-permute-start | bytes 786440 | tf_op jit(solution)/shard_map/ppermute | solution.py:257
  44.2 15.6 %collective-permute-start.19 = (f32[6,64,128]{2,1,0:T(8,128)S(1)}, f32[6,64,128]{2,1,0:T(8,128)S(1)}, u32[]{:S(2)}, u32[]{:S(2)}) collective-permute-start(f32[6,64,128]{2,1,0:T(8,128)S(1)} %get-tuple-element.49), channel_id=1, source_target_pairs={{0,96},{1,97},{2,98},{3,99},{4,100},{5,101},{6,102},{7,103},{8,104... | collective-permute-start | bytes 589832 | tf_op jit(solution)/shard_map/ppermute | solution.py:257
  46.1 13.7 %collective-permute-start.20 = (f32[6,64,128]{2,1,0:T(8,128)S(1)}, f32[6,64,128]{2,1,0:T(8,128)S(1)}, u32[]{:S(2)}, u32[]{:S(2)}) collective-permute-start(f32[6,64,128]{2,1,0:T(8,128)S(1)} %get-tuple-element.50), channel_id=1, source_target_pairs={{0,32},{1,33},{2,34},{3,35},{4,36},{5,37},{6,38},{7,39},{8,40},{9,... | collective-permute-start | bytes 589832 | tf_op jit(solution)/shard_map/ppermute | solution.py:257
  46.8 14.0 %collective-permute-start.21 = (f32[6,64,128]{2,1,0:T(8,128)S(1)}, f32[6,64,128]{2,1,0:T(8,128)S(1)}, u32[]{:S(2)}, u32[]{:S(2)}) collective-permute-start(f32[6,64,128]{2,1,0:T(8,128)S(1)} %get-tuple-element.51), channel_id=1, source_target_pairs={{0,124},{1,125},{2,126},{3,127},{4,104},{5,105},{6,106},{7,107},{8... | collective-permute-start | bytes 589832 | tf_op jit(solution)/shard_map/ppermute | solution.py:257
  56.8 9.2 %collective-permute-start.14 = (f32[6,64,128]{2,1,0:T(8,128)S(1)}, f32[6,64,128]{2,1,0:T(8,128)S(1)}, u32[]{:S(2)}, u32[]{:S(2)}) collective-permute-start(f32[6,64,128]{2,1,0:T(8,128)S(1)} %get-tuple-element.43), channel_id=1, source_target_pairs={{0,60},{1,61},{2,62},{3,63},{4,40},{5,41},{6,42},{7,43},{8,36},{9,... | collective-permute-start | bytes 589832 | tf_op jit(solution)/shard_map/ppermute | solution.py:257
  56.8 9.2 %collective-permute-start.15 = (f32[6,64,128]{2,1,0:T(8,128)S(1)}, f32[6,64,128]{2,1,0:T(8,128)S(1)}, u32[]{:S(2)}, u32[]{:S(2)}) collective-permute-start(f32[6,64,128]{2,1,0:T(8,128)S(1)} %get-tuple-element.44), channel_id=1, source_target_pairs={{0,100},{1,101},{2,102},{3,103},{4,96},{5,97},{6,98},{7,99},{8,108... | collective-permute-start | bytes 589832 | tf_op jit(solution)/shard_map/ppermute | solution.py:257
  59.8 7.5 %collective-permute-start.16 = (f32[6,64,128]{2,1,0:T(8,128)S(1)}, f32[6,64,128]{2,1,0:T(8,128)S(1)}, u32[]{:S(2)}, u32[]{:S(2)}) collective-permute-start(f32[6,64,128]{2,1,0:T(8,128)S(1)} %get-tuple-element.45), channel_id=1, source_target_pairs={{0,36},{1,37},{2,38},{3,39},{4,32},{5,33},{6,34},{7,35},{8,44},{9,... | collective-permute-start | bytes 589832 | tf_op jit(solution)/shard_map/ppermute | solution.py:257
  59.8 7.5 %collective-permute-start.17 = (f32[6,64,128]{2,1,0:T(8,128)S(1)}, f32[6,64,128]{2,1,0:T(8,128)S(1)}, u32[]{:S(2)}, u32[]{:S(2)}) collective-permute-start(f32[6,64,128]{2,1,0:T(8,128)S(1)} %get-tuple-element.46), channel_id=1, source_target_pairs={{0,28},{1,29},{2,30},{3,31},{4,8},{5,9},{6,10},{7,11},{8,4},{9,5},... | collective-permute-start | bytes 589832 | tf_op jit(solution)/shard_map/ppermute | solution.py:257
  60.8 6.4 %collective-permute-start.18 = (f32[6,64,128]{2,1,0:T(8,128)S(1)}, f32[6,64,128]{2,1,0:T(8,128)S(1)}, u32[]{:S(2)}, u32[]{:S(2)}) collective-permute-start(f32[6,64,128]{2,1,0:T(8,128)S(1)} %get-tuple-element.47), channel_id=1, source_target_pairs={{0,4},{1,5},{2,6},{3,7},{4,0},{5,1},{6,2},{7,3},{8,12},{9,13},{10,... | collective-permute-start | bytes 589832 | tf_op jit(solution)/shard_map/ppermute | solution.py:257

commit v6 on v5

--- a/solution.py
+++ b/solution.py
@@ -13,7 +13,7 @@
 SMEM = pltpu.SMEM
 
 SIDE, LAST = 0, 2
-PLANE = [(1, 0), (-1, 0), (1, 2), (-1, 2), (1, 1), (-1, 1), (0, 2), (0, 1), (0, 0)]
+PLANE = [(1, 0), (-1, 0), (1, 2), (-1, 2), (-1, 1), (1, 1), (0, 2), (0, 1), (0, 0)]
 HOME = len(PLANE) - 1
 OUT_ORDER = list(range(8))
 BACK_ORDER = list(range(8))

time: 69 us -> 68.4 us (level)
  transfers between devices with their start and end apart: 22 -> 22, of which waited for: 9 -> 8; matrix products, arithmetic and copies ran while one was open for 0% -> 0% of each run, Pallas kernels for 6% -> 6%
where the time goes in v6:
time: 68.4 us; the launch traced here: 68.3 us
  starting transfers between devices  38.7 us (57%)
  waiting for transfers between devices  14.9 us (22%)
  Pallas kernels  13.1 us (19%)
  other arithmetic  0.87 us (1%)
  between operations  0.77 us (1%)
    ppermute x22, starting transfers between devices, move(): return lax.ppermute(array, AXES, pairs)  38.7 us
    ppermute x22, waiting for transfers between devices, move(): return lax.ppermute(array, AXES, pairs)  14.9 us
    pallas_call x1, Pallas kernels, contribute(): pl.pallas_call(functools.partial(contribute_kernel, extents, capacity, bl...  6 us
    pallas_call x2, Pallas kernels, collect(): pl.pallas_call(functools.partial(collect_kernel, capacity, rows, steps),...  3.17 us
    pallas_call x1, Pallas kernels, gather_own(): pl.pallas_call(functools.partial(gather_own_kernel, capacity, extents), i...  1.77 us
  transfers between devices with their start and end apart: 22, of which 8 were waited for; matrix products, arithmetic and copies ran while one was open for 0% of the time, Pallas kernels for 6%

profile of v6, /device:TPU:1, one launch (start us, length us, event | category | flops | bytes accessed | tf_op | source)
XLA Modules:
  0.0 68.3 jit_solution(5099529806849137313)
XLA Ops:
  0.6 0.7 %multiply_add_fusion.key_hbm.key = s32[4,9]{1,0:T(4,128)S(1)} fusion(s32[4,9]{1,0:T(4,128)} %param.8, s32[4,9]{1,0:T(4,128)} %param.7), kind=kLoop, calls=%fused_computation | loop fusion | flops 72 | bytes 432 | tf_op jit(solution)/shard_map/add | solution.py:264
  1.3 6.0 %shard_map.68 = (f32[6,64,128]{2,1,0:T(8,128)S(1)}, f32[6,64,128]{2,1,0:T(8,128)S(1)}, f32[6,64,128]{2,1,0:T(8,128)S(1)}, f32[6,64,128]{2,1,0:T(8,128)S(1)}, f32...) custom-call(s32[4,9]{1,0:T(4,128)S(1)} %multiply_add_fusion.key_hbm., ...), custom_call_target="tpu_custom_call" | custom-call | tf_op jit(solution)/shard_map/pallas_call | solution.py:103
  7.3 1.5 %collective-permute-start = (f32[6,64,128]{2,1,0:T(8,128)S(1)}, f32[6,64,128]{2,1,0:T(8,128)S(1)}, u32[]{:S(2)}, u32[]{:S(2)}) collective-permute-start(f32[6,64,128]{2,1,0:T(8,128)S(1)} %get-tuple-element.27), channel_id=1, source_target_pairs={{0,4},{1,5},{2,6},{3,7},{4,0},{5,1},{6,2},{7,3},{8,12},{9,13},{10,... | collective-permute-start | bytes 589832 | tf_op jit(solution)/shard_map/ppermute | solution.py:257
  8.8 1.3 %collective-permute-start.1 = (f32[6,64,128]{2,1,0:T(8,128)S(1)}, f32[6,64,128]{2,1,0:T(8,128)S(1)}, u32[]{:S(2)}, u32[]{:S(2)}) collective-permute-start(f32[6,64,128]{2,1,0:T(8,128)S(1)} %get-tuple-element.29), channel_id=1, source_target_pairs={{0,32},{1,33},{2,34},{3,35},{4,36},{5,37},{6,38},{7,39},{8,40},{9,... | collective-permute-start | bytes 589832 | tf_op jit(solution)/shard_map/ppermute | solution.py:257
  10.2 1.4 %collective-permute-start.2 = (f32[6,64,128]{2,1,0:T(8,128)S(1)}, f32[6,64,128]{2,1,0:T(8,128)S(1)}, u32[]{:S(2)}, u32[]{:S(2)}) collective-permute-start(f32[6,64,128]{2,1,0:T(8,128)S(1)} %get-tuple-element.30), channel_id=1, source_target_pairs={{0,96},{1,97},{2,98},{3,99},{4,100},{5,101},{6,102},{7,103},{8,104... | collective-permute-start | bytes 589832 | tf_op jit(solution)/shard_map/ppermute | solution.py:257
  11.5 1.6 %collective-permute-start.3 = (f32[6,64,128]{2,1,0:T(8,128)S(1)}, f32[6,64,128]{2,1,0:T(8,128)S(1)}, u32[]{:S(2)}, u32[]{:S(2)}) collective-permute-start(f32[6,64,128]{2,1,0:T(8,128)S(1)} %get-tuple-element.31), channel_id=1, source_target_pairs={{0,60},{1,61},{2,62},{3,63},{4,40},{5,41},{6,42},{7,43},{8,36},{9,... | collective-permute-start | bytes 589832 | tf_op jit(solution)/shard_map/ppermute | solution.py:257
  13.1 2.2 %collective-permute-start.4 = (f32[6,64,128]{2,1,0:T(8,128)S(1)}, f32[6,64,128]{2,1,0:T(8,128)S(1)}, u32[]{:S(2)}, u32[]{:S(2)}) collective-permute-start(f32[6,64,128]{2,1,0:T(8,128)S(1)} %get-tuple-element.32), channel_id=1, source_target_pairs={{0,124},{1,125},{2,126},{3,127},{4,104},{5,105},{6,106},{7,107},{8... | collective-permute-start | bytes 589832 | tf_op jit(solution)/shard_map/ppermute | solution.py:257
  15.4 1.9 %collective-permute-start.5 = (f32[6,64,128]{2,1,0:T(8,128)S(1)}, f32[6,64,128]{2,1,0:T(8,128)S(1)}, u32[]{:S(2)}, u32[]{:S(2)}) collective-permute-start(f32[6,64,128]{2,1,0:T(8,128)S(1)} %get-tuple-element.33), channel_id=1, source_target_pairs={{0,100},{1,101},{2,102},{3,103},{4,96},{5,97},{6,98},{7,99},{8,108... | collective-permute-start | bytes 589832 | tf_op jit(solution)/shard_map/ppermute | solution.py:257
  17.3 0.5 collective-permute-start.6
  17.8 1.6 %collective-permute-start.7 = (f32[6,64,128]{2,1,0:T(8,128)S(1)}, f32[6,64,128]{2,1,0:T(8,128)S(1)}, u32[]{:S(2)}, u32[]{:S(2)}) collective-permute-start(f32[6,64,128]{2,1,0:T(8,128)S(1)} %get-tuple-element.35), channel_id=1, source_target_pairs={{0,28},{1,29},{2,30},{3,31},{4,8},{5,9},{6,10},{7,11},{8,4},{9,5},... | collective-permute-start | bytes 589832 | tf_op jit(solution)/shard_map/ppermute | solution.py:257
  19.4 2.8 %collective-permute-done.3.refs_2_.refs_4_ = f32[6,64,128]{2,1,0:T(8,128)S(1)} collective-permute-done((f32[6,64,128]{2,1,0:T(8,128)S(1)}, f32[6,64,128]{2,1,0:T(8,128)S(1)}, u32[]{:S(2)}, u32[]{:S(2)}) %collective-permute-start.3) | collective-permute-done | bytes 196640 | tf_op jit(solution)/shard_map/ppermute | solution.py:257
  22.2 3.7 %collective-permute-start.9 = (s32[2,27]{1,0:T(2,128)S(1)}, s32[2,27]{1,0:T(2,128)S(1)}, u32[]{:S(2)}, u32[]{:S(2)}) collective-permute-start(s32[2,27]{1,0:T(2,128)S(1)} %bitcast.4), channel_id=1, source_target_pairs={{0,3},{1,0},{2,1},{3,2},{4,7},{5,4},{6,5},{7,6},{8,11},{9,8},{10,9... | collective-permute-start | bytes 656 | tf_op jit(solution)/shard_map/ppermute | solution.py:257
  26.0 0.7 %collective-permute-done.9.refs_1_.refs_2_ = s32[2,27]{1,0:T(2,128)S(1)} collective-permute-done((s32[2,27]{1,0:T(2,128)S(1)}, s32[2,27]{1,0:T(2,128)S(1)}, u32[]{:S(2)}, u32[]{:S(2)}) %collective-permute-start.9) | collective-permute-done | bytes 248 | tf_op jit(solution)/shard_map/ppermute | solution.py:257
  26.7 2.9 %collective-permute-done.8.refs_0_ = s32[2,27]{1,0:T(2,128)S(1)} collective-permute-done((s32[2,27]{1,0:T(2,128)S(1)}, s32[2,27]{1,0:T(2,128)S(1)}, u32[]{:S(2)}, u32[]{:S(2)}) %collective-permute-start.8) | collective-permute-done | bytes 248 | tf_op jit(solution)/shard_map/ppermute | solution.py:257
  29.6 0.8 %shard_map.70 = (f32[8,64,128]{2,1,0:T(8,128)S(1)}, f32[8,64,128]{2,1,0:T(8,128)S(1)}) custom-call(s32[2,27]{1,0:T(2,128)S(1)} %collective-permute-done.8.refs_0_, s32[2,27]{1,0:T(2,128)S(1)} %collective-permute-done.9.refs_1_.refs_2_, f32[6,64,128]{2,1,0:T(8,128)S(1)} %collective-permute-done.1.refs_0_.refs_2_, ...), custom_call_target="tpu_custom_call" | custom-call | tf_op jit(solution)/shard_map/pallas_call | solution.py:178
  30.5 2.7 %collective-permute-start.11 = (f32[8,64,128]{2,1,0:T(8,128)S(1)}, f32[8,64,128]{2,1,0:T(8,128)S(1)}, u32[]{:S(2)}, u32[]{:S(2)}) collective-permute-start(f32[8,64,128]{2,1,0:T(8,128)S(1)} %get-tuple-element.40), channel_id=1, source_target_pairs={{0,3},{1,0},{2,1},{3,2},{4,7},{5,4},{6,5},{7,6},{8,11},{9,8},{10,9... | collective-permute-start | bytes 786440 | tf_op jit(solution)/shard_map/ppermute | solution.py:257
  33.2 1.8 %shard_map.69 = (f32[8,64,128]{2,1,0:T(8,128)S(1)}, s32[54]{0:T(128)S(1)}) custom-call(s32[4,9]{1,0:T(4,128)S(1)} %multiply_add_fusion.key_hbm.key, s32[2,27]{1,0:T(2,128)S(1)} %bitcast.6, f32[6,64,128]{2,1,0:T(8,128)S(1)} %collective-permute-done.1.refs_0_.refs_2_, f32[6,64,128]{2,1,0:T(8,128)S(1)} %collective-permute-done.2.refs_1_.refs_3_, ...), custom_call_target="tpu_custom_call" | custom-call | tf_op jit(solution)/shard_map/pallas_call | solution.py:147
  35.0 2.0 %collective-permute-done.10 = f32[8,64,128]{2,1,0:T(8,128)S(1)} collective-permute-done((f32[8,64,128]{2,1,0:T(8,128)S(1)}, f32[8,64,128]{2,1,0:T(8,128)S(1)}, u32[]{:S(2)}, u32[]{:S(2)}) %collective-permute-start.10) | collective-permute-done | bytes 262176 | tf_op jit(solution)/shard_map/ppermute | solution.py:257
  37.2 2.7 %collective-permute-start.13 = (f32[8,64,128]{2,1,0:T(8,128)S(1)}, f32[8,64,128]{2,1,0:T(8,128)S(1)}, u32[]{:S(2)}, u32[]{:S(2)}) collective-permute-start(f32[8,64,128]{2,1,0:T(8,128)S(1)} %get-tuple-element.52), channel_id=1, source_target_pairs={{0,3},{1,0},{2,1},{3,2},{4,7},{5,4},{6,5},{7,6},{8,11},{9,8},{10,9... | collective-permute-start | bytes 786440 | tf_op jit(solution)/shard_map/ppermute | solution.py:257
  39.9 3.6 %collective-permute-done.12 = f32[8,64,128]{2,1,0:T(8,128)S(1)} collective-permute-done((f32[8,64,128]{2,1,0:T(8,128)S(1)}, f32[8,64,128]{2,1,0:T(8,128)S(1)}, u32[]{:S(2)}, u32[]{:S(2)}) %collective-permute-start.12) | collective-permute-done | bytes 262176 | tf_op jit(solution)/shard_map/ppermute | solution.py:257
  43.6 0.6 shard_map.72
  44.2 1.9 %collective-permute-start.19 = (f32[6,64,128]{2,1,0:T(8,128)S(1)}, f32[6,64,128]{2,1,0:T(8,128)S(1)}, u32[]{:S(2)}, u32[]{:S(2)}) collective-permute-start(f32[6,64,128]{2,1,0:T(8,128)S(1)} %get-tuple-element.49), channel_id=1, source_target_pairs={{0,96},{1,97},{2,98},{3,99},{4,100},{5,101},{6,102},{7,103},{8,104... | collective-permute-start | bytes 589832 | tf_op jit(solution)/shard_map/ppermute | solution.py:257
  46.1 0.7 %shard_map.71 = (f32[6,64,128]{2,1,0:T(8,128)S(1)}, f32[6,64,128]{2,1,0:T(8,128)S(1)}, f32[6,64,128]{2,1,0:T(8,128)S(1)}, f32[6,64,128]{2,1,0:T(8,128)S(1)}, f32...) custom-call(s32[2,27]{1,0:T(2,128)S(1)} %collective-permute-done.8.refs_0_, ...), custom_call_target="tpu_custom_call" | custom-call | tf_op jit(solution)/shard_map/pallas_call | solution.py:202
  46.8 10.1 %collective-permute-start.21 = (f32[6,64,128]{2,1,0:T(8,128)S(1)}, f32[6,64,128]{2,1,0:T(8,128)S(1)}, u32[]{:S(2)}, u32[]{:S(2)}) collective-permute-start(f32[6,64,128]{2,1,0:T(8,128)S(1)} %get-tuple-element.51), channel_id=1, source_target_pairs={{0,124},{1,125},{2,126},{3,127},{4,104},{5,105},{6,106},{7,107},{8... | collective-permute-start | bytes 589832 | tf_op jit(solution)/shard_map/ppermute | solution.py:257
  56.9 3.0 %collective-permute-start.16 = (f32[6,64,128]{2,1,0:T(8,128)S(1)}, f32[6,64,128]{2,1,0:T(8,128)S(1)}, u32[]{:S(2)}, u32[]{:S(2)}) collective-permute-start(f32[6,64,128]{2,1,0:T(8,128)S(1)} %get-tuple-element.45), channel_id=1, source_target_pairs={{0,100},{1,101},{2,102},{3,103},{4,96},{5,97},{6,98},{7,99},{8,108... | collective-permute-start | bytes 589832 | tf_op jit(solution)/shard_map/ppermute | solution.py:257
  59.8 0.8 %collective-permute-start.17 = (f32[6,64,128]{2,1,0:T(8,128)S(1)}, f32[6,64,128]{2,1,0:T(8,128)S(1)}, u32[]{:S(2)}, u32[]{:S(2)}) collective-permute-start(f32[6,64,128]{2,1,0:T(8,128)S(1)} %get-tuple-element.46), channel_id=1, source_target_pairs={{0,28},{1,29},{2,30},{3,31},{4,8},{5,9},{6,10},{7,11},{8,4},{9,5},... | collective-permute-start | bytes 589832 | tf_op jit(solution)/shard_map/ppermute | solution.py:257
  60.6 1.7 %collective-permute-start.18 = (f32[6,64,128]{2,1,0:T(8,128)S(1)}, f32[6,64,128]{2,1,0:T(8,128)S(1)}, u32[]{:S(2)}, u32[]{:S(2)}) collective-permute-start(f32[6,64,128]{2,1,0:T(8,128)S(1)} %get-tuple-element.47), channel_id=1, source_target_pairs={{0,4},{1,5},{2,6},{3,7},{4,0},{5,1},{6,2},{7,3},{8,12},{9,13},{10,... | collective-permute-start | bytes 589832 | tf_op jit(solution)/shard_map/ppermute | solution.py:257
  62.3 1.5 %shard_map.73.refs_5_ = f32[36,64,128]{2,1,0:T(8,128)} custom-call(s32[54]{0:T(128)S(1)} %get-tuple-element.42.back, f32[6,64,128]{2,1,0:T(8,128)S(1)} %get-tuple-element.48.refs_0_, f32[6,64,128]{2,1,0:T(8,128)S(1)} %collective-permute-done.19.refs_1_, f32[6,64,128]{2,1,0:T(8,128)S(1)} %collective-permute-done.20.refs_2_, ...), custom_call_target="tpu_custom_call" | custom-call | tf_op jit(solution)/shard_map/pallas_call | solution.py:232
  63.8 2.1 %collective-permute-done.14.refs_0_ = f32[6,64,128]{2,1,0:T(8,128)S(1)} collective-permute-done((f32[6,64,128]{2,1,0:T(8,128)S(1)}, f32[6,64,128]{2,1,0:T(8,128)S(1)}, u32[]{:S(2)}, u32[]{:S(2)}) %collective-permute-start.14) | collective-permute-done | bytes 196640 | tf_op jit(solution)/shard_map/ppermute | solution.py:257
  65.9 0.5 collective-permute-done.15.refs_1_
  66.3 0.3 collective-permute-done.17.refs_3_
  66.6 1.7 %shard_map.74 = f32[36,64,128]{2,1,0:T(8,128)} custom-call(s32[54]{0:T(128)S(1)} %get-tuple-element.42.back, f32[6,64,128]{2,1,0:T(8,128)S(1)} %collective-permute-done.14.refs_0_, f32[6,64,128]{2,1,0:T(8,128)S(1)} %collective-permute-done.15.refs_1_, f32[6,64,128]{2,1,0:T(8,128)S(1)} %collective-permute-done.16.refs_2_, ...), custom_call_target="tpu_custom_call", output_to_operand_aliasing={{}: (6, {})} | custom-call | tf_op jit(solution)/shard_map/pallas_call | solution.py:232
  (28 shorter events, 0.4 us)
Async XLA Ops:
  1.3 20.9 %copy-start.1 = (s32[1,27,2]{1,2,0:T(2,128)S(1)}, s32[1,27,2]{1,2,0:T(2,128)}, u32[]{:S(2)}) copy-start(s32[1,27,2]{1,2,0:T(2,128)} %param.9) | copy-start | bytes 652
  7.3 8.0 %collective-permute-start = (f32[6,64,128]{2,1,0:T(8,128)S(1)}, f32[6,64,128]{2,1,0:T(8,128)S(1)}, u32[]{:S(2)}, u32[]{:S(2)}) collective-permute-start(f32[6,64,128]{2,1,0:T(8,128)S(1)} %get-tuple-element.27), channel_id=1, source_target_pairs={{0,4},{1,5},{2,6},{3,7},{4,0},{5,1},{6,2},{7,3},{8,12},{9,13},{10,... | collective-permute-start | bytes 589832 | tf_op jit(solution)/shard_map/ppermute | solution.py:257
  8.8 8.4 %collective-permute-start.1 = (f32[6,64,128]{2,1,0:T(8,128)S(1)}, f32[6,64,128]{2,1,0:T(8,128)S(1)}, u32[]{:S(2)}, u32[]{:S(2)}) collective-permute-start(f32[6,64,128]{2,1,0:T(8,128)S(1)} %get-tuple-element.29), channel_id=1, source_target_pairs={{0,32},{1,33},{2,34},{3,35},{4,36},{5,37},{6,38},{7,39},{8,40},{9,... | collective-permute-start | bytes 589832 | tf_op jit(solution)/shard_map/ppermute | solution.py:257
  10.2 7.7 %collective-permute-start.2 = (f32[6,64,128]{2,1,0:T(8,128)S(1)}, f32[6,64,128]{2,1,0:T(8,128)S(1)}, u32[]{:S(2)}, u32[]{:S(2)}) collective-permute-start(f32[6,64,128]{2,1,0:T(8,128)S(1)} %get-tuple-element.30), channel_id=1, source_target_pairs={{0,96},{1,97},{2,98},{3,99},{4,100},{5,101},{6,102},{7,103},{8,104... | collective-permute-start | bytes 589832 | tf_op jit(solution)/shard_map/ppermute | solution.py:257
  11.5 10.7 %collective-permute-start.3 = (f32[6,64,128]{2,1,0:T(8,128)S(1)}, f32[6,64,128]{2,1,0:T(8,128)S(1)}, u32[]{:S(2)}, u32[]{:S(2)}) collective-permute-start(f32[6,64,128]{2,1,0:T(8,128)S(1)} %get-tuple-element.31), channel_id=1, source_target_pairs={{0,60},{1,61},{2,62},{3,63},{4,40},{5,41},{6,42},{7,43},{8,36},{9,... | collective-permute-start | bytes 589832 | tf_op jit(solution)/shard_map/ppermute | solution.py:257
  13.1 12.9 %collective-permute-start.4 = (f32[6,64,128]{2,1,0:T(8,128)S(1)}, f32[6,64,128]{2,1,0:T(8,128)S(1)}, u32[]{:S(2)}, u32[]{:S(2)}) collective-permute-start(f32[6,64,128]{2,1,0:T(8,128)S(1)} %get-tuple-element.32), channel_id=1, source_target_pairs={{0,124},{1,125},{2,126},{3,127},{4,104},{5,105},{6,106},{7,107},{8... | collective-permute-start | bytes 589832 | tf_op jit(solution)/shard_map/ppermute | solution.py:257
  15.4 10.6 %collective-permute-start.5 = (f32[6,64,128]{2,1,0:T(8,128)S(1)}, f32[6,64,128]{2,1,0:T(8,128)S(1)}, u32[]{:S(2)}, u32[]{:S(2)}) collective-permute-start(f32[6,64,128]{2,1,0:T(8,128)S(1)} %get-tuple-element.33), channel_id=1, source_target_pairs={{0,100},{1,101},{2,102},{3,103},{4,96},{5,97},{6,98},{7,99},{8,108... | collective-permute-start | bytes 589832 | tf_op jit(solution)/shard_map/ppermute | solution.py:257
  17.3 8.7 %collective-permute-start.6 = (f32[6,64,128]{2,1,0:T(8,128)S(1)}, f32[6,64,128]{2,1,0:T(8,128)S(1)}, u32[]{:S(2)}, u32[]{:S(2)}) collective-permute-start(f32[6,64,128]{2,1,0:T(8,128)S(1)} %get-tuple-element.34), channel_id=1, source_target_pairs={{0,36},{1,37},{2,38},{3,39},{4,32},{5,33},{6,34},{7,35},{8,44},{9,... | collective-permute-start | bytes 589832 | tf_op jit(solution)/shard_map/ppermute | solution.py:257
  17.8 8.2 %collective-permute-start.7 = (f32[6,64,128]{2,1,0:T(8,128)S(1)}, f32[6,64,128]{2,1,0:T(8,128)S(1)}, u32[]{:S(2)}, u32[]{:S(2)}) collective-permute-start(f32[6,64,128]{2,1,0:T(8,128)S(1)} %get-tuple-element.35), channel_id=1, source_target_pairs={{0,28},{1,29},{2,30},{3,31},{4,8},{5,9},{6,10},{7,11},{8,4},{9,5},... | collective-permute-start | bytes 589832 | tf_op jit(solution)/shard_map/ppermute | solution.py:257
  22.2 4.5 %collective-permute-start.9 = (s32[2,27]{1,0:T(2,128)S(1)}, s32[2,27]{1,0:T(2,128)S(1)}, u32[]{:S(2)}, u32[]{:S(2)}) collective-permute-start(s32[2,27]{1,0:T(2,128)S(1)} %bitcast.4), channel_id=1, source_target_pairs={{0,3},{1,0},{2,1},{3,2},{4,7},{5,4},{6,5},{7,6},{8,11},{9,8},{10,9... | collective-permute-start | bytes 656 | tf_op jit(solution)/shard_map/ppermute | solution.py:257
  26.0 3.6 %collective-permute-start.8 = (s32[2,27]{1,0:T(2,128)S(1)}, s32[2,27]{1,0:T(2,128)S(1)}, u32[]{:S(2)}, u32[]{:S(2)}) collective-permute-start(s32[2,27]{1,0:T(2,128)S(1)} %bitcast.5), channel_id=1, source_target_pairs={{0,1},{1,2},{2,3},{3,0},{4,5},{5,6},{6,7},{7,4},{8,9},{9,10},{10,1... | collective-permute-start | bytes 656 | tf_op jit(solution)/shard_map/ppermute | solution.py:257
  30.5 6.5 %collective-permute-start.10 = (f32[8,64,128]{2,1,0:T(8,128)S(1)}, f32[8,64,128]{2,1,0:T(8,128)S(1)}, u32[]{:S(2)}, u32[]{:S(2)}) collective-permute-start(f32[8,64,128]{2,1,0:T(8,128)S(1)} %get-tuple-element.39), channel_id=1, source_target_pairs={{0,1},{1,2},{2,3},{3,0},{4,5},{5,6},{6,7},{7,4},{8,9},{9,10},{10,1... | collective-permute-start | bytes 786440 | tf_op jit(solution)/shard_map/ppermute | solution.py:257
  30.5 6.5 %collective-permute-start.11 = (f32[8,64,128]{2,1,0:T(8,128)S(1)}, f32[8,64,128]{2,1,0:T(8,128)S(1)}, u32[]{:S(2)}, u32[]{:S(2)}) collective-permute-start(f32[8,64,128]{2,1,0:T(8,128)S(1)} %get-tuple-element.40), channel_id=1, source_target_pairs={{0,3},{1,0},{2,1},{3,2},{4,7},{5,4},{6,5},{7,6},{8,11},{9,8},{10,9... | collective-permute-start | bytes 786440 | tf_op jit(solution)/shard_map/ppermute | solution.py:257
  37.0 6.5 %collective-permute-start.12 = (f32[8,64,128]{2,1,0:T(8,128)S(1)}, f32[8,64,128]{2,1,0:T(8,128)S(1)}, u32[]{:S(2)}, u32[]{:S(2)}) collective-permute-start(f32[8,64,128]{2,1,0:T(8,128)S(1)} %add.19), channel_id=1, source_target_pairs={{0,1},{1,2},{2,3},{3,0},{4,5},{5,6},{6,7},{7,4},{8,9},{9,10},{10,1... | collective-permute-start | bytes 786440 | tf_op jit(solution)/shard_map/ppermute | solution.py:257
  37.2 8.9 %copy-start = (f32[8,64,128]{2,1,0:T(8,128)}, f32[8,64,128]{2,1,0:T(8,128)S(1)}, u32[]{:S(2)}) copy-start(f32[8,64,128]{2,1,0:T(8,128)S(1)} %get-tuple-element.53.refs_4_) | copy-start | bytes 786436
  37.2 6.4 %collective-permute-start.13 = (f32[8,64,128]{2,1,0:T(8,128)S(1)}, f32[8,64,128]{2,1,0:T(8,128)S(1)}, u32[]{:S(2)}, u32[]{:S(2)}) collective-permute-start(f32[8,64,128]{2,1,0:T(8,128)S(1)} %get-tuple-element.52), channel_id=1, source_target_pairs={{0,3},{1,0},{2,1},{3,2},{4,7},{5,4},{6,5},{7,6},{8,11},{9,8},{10,9... | collective-permute-start | bytes 786440 | tf_op jit(solution)/shard_map/ppermute | solution.py:257
  44.2 12.6 %collective-permute-start.19 = (f32[6,64,128]{2,1,0:T(8,128)S(1)}, f32[6,64,128]{2,1,0:T(8,128)S(1)}, u32[]{:S(2)}, u32[]{:S(2)}) collective-permute-start(f32[6,64,128]{2,1,0:T(8,128)S(1)} %get-tuple-element.49), channel_id=1, source_target_pairs={{0,96},{1,97},{2,98},{3,99},{4,100},{5,101},{6,102},{7,103},{8,104... | collective-permute-start | bytes 589832 | tf_op jit(solution)/shard_map/ppermute | solution.py:257
  46.1 13.7 %collective-permute-start.20 = (f32[6,64,128]{2,1,0:T(8,128)S(1)}, f32[6,64,128]{2,1,0:T(8,128)S(1)}, u32[]{:S(2)}, u32[]{:S(2)}) collective-permute-start(f32[6,64,128]{2,1,0:T(8,128)S(1)} %get-tuple-element.50), channel_id=1, source_target_pairs={{0,32},{1,33},{2,34},{3,35},{4,36},{5,37},{6,38},{7,39},{8,40},{9,... | collective-permute-start | bytes 589832 | tf_op jit(solution)/shard_map/ppermute | solution.py:257
  46.8 13.8 %collective-permute-start.21 = (f32[6,64,128]{2,1,0:T(8,128)S(1)}, f32[6,64,128]{2,1,0:T(8,128)S(1)}, u32[]{:S(2)}, u32[]{:S(2)}) collective-permute-start(f32[6,64,128]{2,1,0:T(8,128)S(1)} %get-tuple-element.51), channel_id=1, source_target_pairs={{0,124},{1,125},{2,126},{3,127},{4,104},{5,105},{6,106},{7,107},{8... | collective-permute-start | bytes 589832 | tf_op jit(solution)/shard_map/ppermute | solution.py:257
  56.8 9.0 %collective-permute-start.14 = (f32[6,64,128]{2,1,0:T(8,128)S(1)}, f32[6,64,128]{2,1,0:T(8,128)S(1)}, u32[]{:S(2)}, u32[]{:S(2)}) collective-permute-start(f32[6,64,128]{2,1,0:T(8,128)S(1)} %get-tuple-element.43), channel_id=1, source_target_pairs={{0,60},{1,61},{2,62},{3,63},{4,40},{5,41},{6,42},{7,43},{8,36},{9,... | collective-permute-start | bytes 589832 | tf_op jit(solution)/shard_map/ppermute | solution.py:257
  56.8 9.5 %collective-permute-start.15 = (f32[6,64,128]{2,1,0:T(8,128)S(1)}, f32[6,64,128]{2,1,0:T(8,128)S(1)}, u32[]{:S(2)}, u32[]{:S(2)}) collective-permute-start(f32[6,64,128]{2,1,0:T(8,128)S(1)} %get-tuple-element.44), channel_id=1, source_target_pairs={{0,36},{1,37},{2,38},{3,39},{4,32},{5,33},{6,34},{7,35},{8,44},{9,... | collective-permute-start | bytes 589832 | tf_op jit(solution)/shard_map/ppermute | solution.py:257
  56.9 9.5 %collective-permute-start.16 = (f32[6,64,128]{2,1,0:T(8,128)S(1)}, f32[6,64,128]{2,1,0:T(8,128)S(1)}, u32[]{:S(2)}, u32[]{:S(2)}) collective-permute-start(f32[6,64,128]{2,1,0:T(8,128)S(1)} %get-tuple-element.45), channel_id=1, source_target_pairs={{0,100},{1,101},{2,102},{3,103},{4,96},{5,97},{6,98},{7,99},{8,108... | collective-permute-start | bytes 589832 | tf_op jit(solution)/shard_map/ppermute | solution.py:257
  59.8 6.8 %collective-permute-start.17 = (f32[6,64,128]{2,1,0:T(8,128)S(1)}, f32[6,64,128]{2,1,0:T(8,128)S(1)}, u32[]{:S(2)}, u32[]{:S(2)}) collective-permute-start(f32[6,64,128]{2,1,0:T(8,128)S(1)} %get-tuple-element.46), channel_id=1, source_target_pairs={{0,28},{1,29},{2,30},{3,31},{4,8},{5,9},{6,10},{7,11},{8,4},{9,5},... | collective-permute-start | bytes 589832 | tf_op jit(solution)/shard_map/ppermute | solution.py:257
  60.6 6.0 %collective-permute-start.18 = (f32[6,64,128]{2,1,0:T(8,128)S(1)}, f32[6,64,128]{2,1,0:T(8,128)S(1)}, u32[]{:S(2)}, u32[]{:S(2)}) collective-permute-start(f32[6,64,128]{2,1,0:T(8,128)S(1)} %get-tuple-element.47), channel_id=1, source_target_pairs={{0,4},{1,5},{2,6},{3,7},{4,0},{5,1},{6,2},{7,3},{8,12},{9,13},{10,... | collective-permute-start | bytes 589832 | tf_op jit(solution)/shard_map/ppermute | solution.py:257
